TPU v7x, 512 devices: a whole 4x8x8 slice. The times are simulated.
512 devices in a mesh: tok: 256 (over z, y, x), head: 2 (over core).
Axes of the slice: x: 4, y: 8, z: 8, core: 2. Of those that a mesh axis runs over, the one named last changes fastest.
Arguments:
- queries: bfloat16 [32768, 1536], P('tok', 'head'), may hold values from -32 to 32
- keys: bfloat16 [32768, 1536], P('tok', 'head'), may hold values from -32 to 32
- values: bfloat16 [32768, 1536], P('tok', 'head'), may hold values from -6 to 6
- window: int32 [256, 27], P('tok'), may hold values from -1 to 255, as said below
- out_weight: bfloat16 [1536, 3072], P('head', 'tok'), may hold values from -0.15625 to 0.15625
Outputs:
- projected: bfloat16 [32768, 3072], P('tok', 'head')
Inputs may be any that keep to these rules, and one draw needn't show every extreme that they name: `window`: row i lists distinct tiles: first i itself, then tiles whose frame, row and column each differ from those of i by at most one; -1 marks unused entries, which come last.
All inputs are finite; a program needn't handle non-finite values.
Results may differ from a plain program's by a relative error of at most 0.015.
Values may be sent and summed in bfloat16 or wider, within the bound.
No kernel may reach another device: no remote copies, remote signals or barrier semaphores. Data moves between devices by JAX's collectives and lax.ppermute only.
A program may use at most 128 MiB of HBM per device.

v0:
```python
import jax
import jax.numpy as jnp
from jax import lax
from jax.sharding import PartitionSpec as P

HD = 128


def passed_along(value, axis, by):
    count = lax.axis_size(axis)
    pairs = [(i, i + by) for i in range(count) if 0 <= i + by < count]
    return lax.ppermute(value, axis, pairs)


def attend_tile(running, query_heads, kv_piece, is_listed):
    peak_now, total_now, summed_now = running
    tok_rows, head_count, head_size = query_heads.shape
    key_heads = kv_piece[0].reshape(tok_rows, head_count, head_size)
    value_heads = kv_piece[1].reshape(tok_rows, head_count, head_size)
    scores = jnp.einsum("qhd,khd->hqk", query_heads, key_heads, preferred_element_type=jnp.float32)
    scores = jnp.where(is_listed, scores * HD ** (-0.5), -1e30)
    new_peak = jnp.maximum(peak_now, jnp.max(scores, axis=-1))
    rescale = jnp.exp(peak_now - new_peak)
    unrounded = jnp.exp(scores - new_peak[..., None])
    total_next = total_now * rescale + jnp.sum(unrounded, axis=-1)
    weights = unrounded.astype(jnp.bfloat16)
    summed_next = summed_now * rescale[..., None] + jnp.einsum(
        "hqk,khd->hqd", weights, value_heads, preferred_element_type=jnp.float32
    )
    return (new_peak, total_next, summed_next)


def body(queries, keys, values, window, out_weight):
    tok_rows, feat_width = queries.shape
    head_count = feat_width // HD
    tile_count = lax.axis_size("tok")
    grid_w = min(8, tile_count // 4)
    grid_h = min(4, tile_count // (2 * grid_w))
    frame_size = grid_w * grid_h
    frame_count = tile_count // frame_size
    my_tile = lax.axis_index("tok")
    my_frame = my_tile // frame_size
    my_row = my_tile // grid_w % grid_h
    my_col = my_tile % grid_w
    query_heads = queries.reshape(tok_rows, head_count, HD)
    listed_tiles = window[0]
    initial = (
        jnp.full((head_count, tok_rows), -1e30, jnp.float32),
        jnp.zeros((head_count, tok_rows), jnp.float32),
        jnp.zeros((head_count, tok_rows, HD), jnp.float32),
    )
    own_pair = jnp.stack([keys, values])
    slot_blocks = []
    for step_f in (-1, 0, 1):
        for step_h in (-1, 0, 1):
            for step_w in (-1, 0, 1):
                distance = step_f * frame_size + step_h * grid_w + step_w
                if distance == 0:
                    slot_blocks.append(own_pair)
                else:
                    slot_blocks.append(passed_along(own_pair, "tok", -distance))
    near_box = jnp.stack(slot_blocks)
    slot_range = jnp.arange(27, dtype=jnp.int32)
    slot_f = slot_range // 9 - 1
    slot_h = slot_range // 3 % 3 - 1
    slot_w = slot_range % 3 - 1
    slot_distance = slot_f * frame_size + slot_h * grid_w + slot_w
    inside = (
        (my_frame + slot_f >= 0)
        & (my_frame + slot_f < frame_count)
        & (my_row + slot_h >= 0)
        & (my_row + slot_h < grid_h)
        & (my_col + slot_w >= 0)
        & (my_col + slot_w < grid_w)
    )

    def visit_band(running, slot_index):
        key_tile = my_tile + slot_distance[slot_index]
        is_listed = inside[slot_index] & jnp.any(listed_tiles == key_tile)
        kv_piece = lax.dynamic_index_in_dim(near_box, slot_index, 0, keepdims=False)
        return (attend_tile(running, query_heads, kv_piece, is_listed), None)

    running, _ = lax.scan(visit_band, initial, slot_range)
    attended = (running[2] / running[1][..., None]).transpose(1, 0, 2).reshape(tok_rows, feat_width)
    attended = attended.astype(jnp.bfloat16)
    projection = jnp.dot(
        attended,
        lax.all_gather(out_weight, "tok", axis=1, tiled=True),
        preferred_element_type=jnp.float32,
    )
    return lax.psum_scatter(
        projection.astype(jnp.bfloat16), "head", scatter_dimension=1, tiled=True
    )


def solution(mesh):
    in_specs = (
        P("tok", "head"),
        P("tok", "head"),
        P("tok", "head"),
        P("tok", None),
        P("head", "tok"),
    )
    out_specs = P("tok", "head")
    return jax.shard_map(body, mesh=mesh, in_specs=in_specs, out_specs=out_specs, check_vma=False)
```

profile of v0, /device:TPU:1, one launch (start us, length us, event | category | flops | bytes accessed | tf_op | source)
XLA Modules:
  0.0 640.3 jit_solution(16688416256508616315)
XLA Ops:
  8.8 7.8 %collective-permute-start = (bf16[2,128,768]{1,2,0:T(8,128)(2,1)S(1)}, bf16[2,128,768]{1,2,0:T(8,128)(2,1)S(1)}, u32[]{:S(2)}, u32[]{:S(2)}) collective-permute-start(bf16[2,128,768]{1,2,0:T(8,128)(2,1)S(1)} %pad_maximum_fusion), channel_id=1, source_target_pairs={{0,82},{2,84},{4,86},{6,88},{8,90},{10,92},{12,94},{14,96},{16,98}... | collective-permute-start | bytes 1179656 | tf_op jit(solution)/shard_map/ppermute | solution.py:12
  16.6 7.3 %collective-permute-start.1 = (bf16[2,128,768]{1,2,0:T(8,128)(2,1)S(1)}, bf16[2,128,768]{1,2,0:T(8,128)(2,1)S(1)}, u32[]{:S(2)}, u32[]{:S(2)}) collective-permute-start(bf16[2,128,768]{1,2,0:T(8,128)(2,1)S(1)} %pad_maximum_fusion), channel_id=1, source_target_pairs={{0,80},{2,82},{4,84},{6,86},{8,88},{10,90},{12,92},{14,94},{16,96}... | collective-permute-start | bytes 1179656 | tf_op jit(solution)/shard_map/ppermute | solution.py:12
  23.8 5.4 collective-permute-start.2
  29.3 4.9 collective-permute-start.3
  34.2 3.1 collective-permute-start.4
  39.3 7.6 %collective-permute-start.5 = (bf16[2,128,768]{1,2,0:T(8,128)(2,1)S(1)}, bf16[2,128,768]{1,2,0:T(8,128)(2,1)S(1)}, u32[]{:S(2)}, u32[]{:S(2)}) collective-permute-start(bf16[2,128,768]{1,2,0:T(8,128)(2,1)S(1)} %pad_maximum_fusion), channel_id=1, source_target_pairs={{0,62},{2,64},{4,66},{6,68},{8,70},{10,72},{12,74},{14,76},{16,78}... | collective-permute-start | bytes 1179656 | tf_op jit(solution)/shard_map/ppermute | solution.py:12
  47.0 5.1 collective-permute-start.6
  52.1 15.5 %collective-permute-done.2 = bf16[2,128,768]{1,2,0:T(8,128)(2,1)S(1)} collective-permute-done((bf16[2,128,768]{1,2,0:T(8,128)(2,1)S(1)}, bf16[2,128,768]{1,2,0:T(8,128)(2,1)S(1)}, u32[]{:S(2)}, u32[]{:S(2)}) %collective-permute-start.2) | collective-permute-done | bytes 393248 | tf_op jit(solution)/shard_map/ppermute | solution.py:12
  67.6 1.4 collective-permute-start.7
  69.1 22.6 %collective-permute-start.8 = (bf16[2,128,768]{1,2,0:T(8,128)(2,1)S(1)}, bf16[2,128,768]{1,2,0:T(8,128)(2,1)S(1)}, u32[]{:S(2)}, u32[]{:S(2)}) collective-permute-start(bf16[2,128,768]{1,2,0:T(8,128)(2,1)S(1)} %pad_maximum_fusion), channel_id=1, source_target_pairs={{0,46},{2,48},{4,50},{6,52},{8,54},{10,56},{12,58},{14,60},{16,62}... | collective-permute-start | bytes 1179656 | tf_op jit(solution)/shard_map/ppermute | solution.py:12
  91.8 1.7 collective-permute-done.4
  93.5 16.1 %collective-permute-start.9 = (bf16[2,128,768]{1,2,0:T(8,128)(2,1)S(1)}, bf16[2,128,768]{1,2,0:T(8,128)(2,1)S(1)}, u32[]{:S(2)}, u32[]{:S(2)}) collective-permute-start(bf16[2,128,768]{1,2,0:T(8,128)(2,1)S(1)} %pad_maximum_fusion), channel_id=1, source_target_pairs={{0,18},{2,20},{4,22},{6,24},{8,26},{10,28},{12,30},{14,32},{16,34}... | collective-permute-start | bytes 1179656 | tf_op jit(solution)/shard_map/ppermute | solution.py:12
  109.8 2.0 collective-permute-start.10
  111.9 3.9 collective-permute-start.11
  115.8 1.6 collective-permute-start.12
  117.5 1.3 collective-permute-start.13
  118.9 1.3 collective-permute-start.14
  120.2 19.9 %collective-permute-done.10 = bf16[2,128,768]{1,2,0:T(8,128)(2,1)S(1)} collective-permute-done((bf16[2,128,768]{1,2,0:T(8,128)(2,1)S(1)}, bf16[2,128,768]{1,2,0:T(8,128)(2,1)S(1)}, u32[]{:S(2)}, u32[]{:S(2)}) %collective-permute-start.10) | collective-permute-done | bytes 393248 | tf_op jit(solution)/shard_map/ppermute | solution.py:12
  141.5 9.8 %collective-permute-done.11 = bf16[2,128,768]{1,2,0:T(8,128)(2,1)S(1)} collective-permute-done((bf16[2,128,768]{1,2,0:T(8,128)(2,1)S(1)}, bf16[2,128,768]{1,2,0:T(8,128)(2,1)S(1)}, u32[]{:S(2)}, u32[]{:S(2)}) %collective-permute-start.11) | collective-permute-done | bytes 393248 | tf_op jit(solution)/shard_map/ppermute | solution.py:12
  152.7 1.3 collective-permute-start.17
  154.1 1.3 collective-permute-start.18
  155.5 1.3 collective-permute-start.19
  156.8 3.3 collective-permute-done.15
  161.5 27.5 %collective-permute-done.16 = bf16[2,128,768]{1,2,0:T(8,128)(2,1)S(1)} collective-permute-done((bf16[2,128,768]{1,2,0:T(8,128)(2,1)S(1)}, bf16[2,128,768]{1,2,0:T(8,128)(2,1)S(1)}, u32[]{:S(2)}, u32[]{:S(2)}) %collective-permute-start.16) | collective-permute-done | bytes 393248 | tf_op jit(solution)/shard_map/ppermute | solution.py:12
  190.4 1.3 collective-permute-start.22
  191.8 7.6 %collective-permute-done.18 = bf16[2,128,768]{1,2,0:T(8,128)(2,1)S(1)} collective-permute-done((bf16[2,128,768]{1,2,0:T(8,128)(2,1)S(1)}, bf16[2,128,768]{1,2,0:T(8,128)(2,1)S(1)}, u32[]{:S(2)}, u32[]{:S(2)}) %collective-permute-start.18) | collective-permute-done | bytes 393248 | tf_op jit(solution)/shard_map/ppermute | solution.py:12
  199.3 1.3 collective-permute-start.23
  200.7 1.3 collective-permute-start.24
  202.0 60.9 %collective-permute-done.20 = bf16[2,128,768]{1,2,0:T(8,128)(2,1)S(1)} collective-permute-done((bf16[2,128,768]{1,2,0:T(8,128)(2,1)S(1)}, bf16[2,128,768]{1,2,0:T(8,128)(2,1)S(1)}, u32[]{:S(2)}, u32[]{:S(2)}) %collective-permute-start.20) | collective-permute-done | bytes 393248 | tf_op jit(solution)/shard_map/ppermute | solution.py:12
  264.4 2.3 collective-permute-done.23
  266.8 1.5 collective-permute-done.24
  268.3 18.9 %collective-permute-done.25 = bf16[2,128,768]{1,2,0:T(8,128)(2,1)S(1)} collective-permute-done((bf16[2,128,768]{1,2,0:T(8,128)(2,1)S(1)}, bf16[2,128,768]{1,2,0:T(8,128)(2,1)S(1)}, u32[]{:S(2)}, u32[]{:S(2)}) %collective-permute-start.25) | collective-permute-done | bytes 393248 | tf_op jit(solution)/shard_map/ppermute | solution.py:12
  287.3 4.0 copy-done
  291.3 260.9 %while.15 = (s32[]{:T(128)}, f32[6,128]{1,0:T(8,128)S(1)}, f32[6,128]{1,0:T(8,128)S(1)}, f32[6,128,128]{2,1,0:T(8,128)S(1)}, s32[27]{0:T(128)S(1)}, /*index=5*/p...) while((s32[]{:T(128)}, f32[6,128]{1,0:T(8,128)S(1)}, ...), condition=%wide.region_4.5_spmd.clone, body=%wide.region_0.4_spmd.clone.sunk | while | flops 51318588 | bytes 3391854 | solution.py:83
  294.0 1.3 dynamic_slice.23
  303.6 1.3 dynamic_slice.23
  313.3 1.3 dynamic_slice.23
  323.0 1.3 dynamic_slice.23
  332.6 1.3 dynamic_slice.23
  342.3 1.3 dynamic_slice.23
  352.0 1.3 dynamic_slice.23
  361.7 1.3 dynamic_slice.23
  371.3 1.3 dynamic_slice.23
  381.0 1.3 dynamic_slice.23
  390.6 1.3 dynamic_slice.23
  400.3 1.3 dynamic_slice.23
  410.0 1.3 dynamic_slice.23
  419.6 1.3 dynamic_slice.23
  429.3 1.3 dynamic_slice.23
  438.9 1.3 dynamic_slice.23
  448.6 1.3 dynamic_slice.23
  458.3 1.3 dynamic_slice.23
  467.9 1.3 dynamic_slice.23
  477.6 1.3 dynamic_slice.23
  487.3 1.3 dynamic_slice.23
  496.9 1.3 dynamic_slice.23
  506.6 1.3 dynamic_slice.23
  516.2 1.3 dynamic_slice.23
  525.9 1.3 dynamic_slice.23
  535.6 1.3 dynamic_slice.23
  545.2 1.3 dynamic_slice.23
  552.5 8.4 %reshape.14 = bf16[3072,768]{1,0:T(8,128)(2,1)} reshape(bf16[256,12,768]{2,1,0:T(8,128)(2,1)} %all-gather.3.cloned.1.call-done) | data formatting | bytes 9437184
  560.8 4.9 convolution_convert_fusion
  565.8 67.7 %reduce-scatter.2.cloned.1.call-done = bf16[128,1536]{1,0:T(8,128)(2,1)} async-done(((bf16[128,3072]{1,0:T(8,128)(2,1)}), bf16[128,1536]{1,0:T(8,128)(2,1)}) %reduce-scatter.2.cloned.1.call-update) | async-done | bytes 393232 | tf_op jit(solution)/shard_map/reduce_scatter | solution.py:91
  (336 shorter events, 129.0 us)
Async XLA Ops:
  6.5 545.9 %all-gather.3.cloned.1.call-start = ((), (), s32[]{:S(2)}) async-start(), calls=%async_computation.2 | async-start | bytes 6316032 | tf_op jit(solution)/shard_map/all_gather | solution.py:88
  8.8 30.5 %collective-permute-start = (bf16[2,128,768]{1,2,0:T(8,128)(2,1)S(1)}, bf16[2,128,768]{1,2,0:T(8,128)(2,1)S(1)}, u32[]{:S(2)}, u32[]{:S(2)}) collective-permute-start(bf16[2,128,768]{1,2,0:T(8,128)(2,1)S(1)} %pad_maximum_fusion), channel_id=1, source_target_pairs={{0,82},{2,84},{4,86},{6,88},{8,90},{10,92},{12,94},{14,96},{16,98}... | collective-permute-start | bytes 1179656 | tf_op jit(solution)/shard_map/ppermute | solution.py:12
  16.6 30.4 %collective-permute-start.1 = (bf16[2,128,768]{1,2,0:T(8,128)(2,1)S(1)}, bf16[2,128,768]{1,2,0:T(8,128)(2,1)S(1)}, u32[]{:S(2)}, u32[]{:S(2)}) collective-permute-start(bf16[2,128,768]{1,2,0:T(8,128)(2,1)S(1)} %pad_maximum_fusion), channel_id=1, source_target_pairs={{0,80},{2,82},{4,84},{6,86},{8,88},{10,90},{12,92},{14,94},{16,96}... | collective-permute-start | bytes 1179656 | tf_op jit(solution)/shard_map/ppermute | solution.py:12
  23.8 43.7 %collective-permute-start.2 = (bf16[2,128,768]{1,2,0:T(8,128)(2,1)S(1)}, bf16[2,128,768]{1,2,0:T(8,128)(2,1)S(1)}, u32[]{:S(2)}, u32[]{:S(2)}) collective-permute-start(bf16[2,128,768]{1,2,0:T(8,128)(2,1)S(1)} %pad_maximum_fusion), channel_id=1, source_target_pairs={{0,78},{2,80},{4,82},{6,84},{8,86},{10,88},{12,90},{14,92},{16,94}... | collective-permute-start | bytes 1179656 | tf_op jit(solution)/shard_map/ppermute | solution.py:12
  29.3 39.8 %collective-permute-start.3 = (bf16[2,128,768]{1,2,0:T(8,128)(2,1)S(1)}, bf16[2,128,768]{1,2,0:T(8,128)(2,1)S(1)}, u32[]{:S(2)}, u32[]{:S(2)}) collective-permute-start(bf16[2,128,768]{1,2,0:T(8,128)(2,1)S(1)} %pad_maximum_fusion), channel_id=1, source_target_pairs={{0,66},{2,68},{4,70},{6,72},{8,74},{10,76},{12,78},{14,80},{16,82}... | collective-permute-start | bytes 1179656 | tf_op jit(solution)/shard_map/ppermute | solution.py:12
  34.2 59.3 %collective-permute-start.4 = (bf16[2,128,768]{1,2,0:T(8,128)(2,1)S(1)}, bf16[2,128,768]{1,2,0:T(8,128)(2,1)S(1)}, u32[]{:S(2)}, u32[]{:S(2)}) collective-permute-start(bf16[2,128,768]{1,2,0:T(8,128)(2,1)S(1)} %pad_maximum_fusion), channel_id=1, source_target_pairs={{0,64},{2,66},{4,68},{6,70},{8,72},{10,74},{12,76},{14,78},{16,80}... | collective-permute-start | bytes 1179656 | tf_op jit(solution)/shard_map/ppermute | solution.py:12
  37.3 596.1 %reduce-scatter.2.cloned.1.call-start = ((), (), s32[]{:S(2)}) async-start(), calls=%async_computation.1 | async-start | bytes 1179648 | tf_op jit(solution)/shard_map/reduce_scatter | solution.py:91
  39.3 70.4 %collective-permute-start.5 = (bf16[2,128,768]{1,2,0:T(8,128)(2,1)S(1)}, bf16[2,128,768]{1,2,0:T(8,128)(2,1)S(1)}, u32[]{:S(2)}, u32[]{:S(2)}) collective-permute-start(bf16[2,128,768]{1,2,0:T(8,128)(2,1)S(1)} %pad_maximum_fusion), channel_id=1, source_target_pairs={{0,62},{2,64},{4,66},{6,68},{8,70},{10,72},{12,74},{14,76},{16,78}... | collective-permute-start | bytes 1179656 | tf_op jit(solution)/shard_map/ppermute | solution.py:12
  47.0 64.9 %collective-permute-start.6 = (bf16[2,128,768]{1,2,0:T(8,128)(2,1)S(1)}, bf16[2,128,768]{1,2,0:T(8,128)(2,1)S(1)}, u32[]{:S(2)}, u32[]{:S(2)}) collective-permute-start(bf16[2,128,768]{1,2,0:T(8,128)(2,1)S(1)} %pad_maximum_fusion), channel_id=1, source_target_pairs={{0,50},{2,52},{4,54},{6,56},{8,58},{10,60},{12,62},{14,64},{16,66}... | collective-permute-start | bytes 1179656 | tf_op jit(solution)/shard_map/ppermute | solution.py:12
  67.6 48.3 %collective-permute-start.7 = (bf16[2,128,768]{1,2,0:T(8,128)(2,1)S(1)}, bf16[2,128,768]{1,2,0:T(8,128)(2,1)S(1)}, u32[]{:S(2)}, u32[]{:S(2)}) collective-permute-start(bf16[2,128,768]{1,2,0:T(8,128)(2,1)S(1)} %pad_maximum_fusion), channel_id=1, source_target_pairs={{0,48},{2,50},{4,52},{6,54},{8,56},{10,58},{12,60},{14,62},{16,64}... | collective-permute-start | bytes 1179656 | tf_op jit(solution)/shard_map/ppermute | solution.py:12
  69.1 48.4 %collective-permute-start.8 = (bf16[2,128,768]{1,2,0:T(8,128)(2,1)S(1)}, bf16[2,128,768]{1,2,0:T(8,128)(2,1)S(1)}, u32[]{:S(2)}, u32[]{:S(2)}) collective-permute-start(bf16[2,128,768]{1,2,0:T(8,128)(2,1)S(1)} %pad_maximum_fusion), channel_id=1, source_target_pairs={{0,46},{2,48},{4,50},{6,52},{8,54},{10,56},{12,58},{14,60},{16,62}... | collective-permute-start | bytes 1179656 | tf_op jit(solution)/shard_map/ppermute | solution.py:12
  93.5 25.3 %collective-permute-start.9 = (bf16[2,128,768]{1,2,0:T(8,128)(2,1)S(1)}, bf16[2,128,768]{1,2,0:T(8,128)(2,1)S(1)}, u32[]{:S(2)}, u32[]{:S(2)}) collective-permute-start(bf16[2,128,768]{1,2,0:T(8,128)(2,1)S(1)} %pad_maximum_fusion), channel_id=1, source_target_pairs={{0,18},{2,20},{4,22},{6,24},{8,26},{10,28},{12,30},{14,32},{16,34}... | collective-permute-start | bytes 1179656 | tf_op jit(solution)/shard_map/ppermute | solution.py:12
  109.8 30.4 %collective-permute-start.10 = (bf16[2,128,768]{1,2,0:T(8,128)(2,1)S(1)}, bf16[2,128,768]{1,2,0:T(8,128)(2,1)S(1)}, u32[]{:S(2)}, u32[]{:S(2)}) collective-permute-start(bf16[2,128,768]{1,2,0:T(8,128)(2,1)S(1)} %pad_maximum_fusion), channel_id=1, source_target_pairs={{0,16},{2,18},{4,20},{6,22},{8,24},{10,26},{12,28},{14,30},{16,32}... | collective-permute-start | bytes 1179656 | tf_op jit(solution)/shard_map/ppermute | solution.py:12
  111.9 39.4 %collective-permute-start.11 = (bf16[2,128,768]{1,2,0:T(8,128)(2,1)S(1)}, bf16[2,128,768]{1,2,0:T(8,128)(2,1)S(1)}, u32[]{:S(2)}, u32[]{:S(2)}) collective-permute-start(bf16[2,128,768]{1,2,0:T(8,128)(2,1)S(1)} %pad_maximum_fusion), channel_id=1, source_target_pairs={{0,14},{2,16},{4,18},{6,20},{8,22},{10,24},{12,26},{14,28},{16,30}... | collective-permute-start | bytes 1179656 | tf_op jit(solution)/shard_map/ppermute | solution.py:12
  115.8 36.8 %collective-permute-start.12 = (bf16[2,128,768]{1,2,0:T(8,128)(2,1)S(1)}, bf16[2,128,768]{1,2,0:T(8,128)(2,1)S(1)}, u32[]{:S(2)}, u32[]{:S(2)}) collective-permute-start(bf16[2,128,768]{1,2,0:T(8,128)(2,1)S(1)} %pad_maximum_fusion), channel_id=1, source_target_pairs={{0,2},{2,4},{4,6},{6,8},{8,10},{10,12},{12,14},{14,16},{16,18},{18... | collective-permute-start | bytes 1179656 | tf_op jit(solution)/shard_map/ppermute | solution.py:12
  117.5 36.6 %collective-permute-start.13 = (bf16[2,128,768]{1,2,0:T(8,128)(2,1)S(1)}, bf16[2,128,768]{1,2,0:T(8,128)(2,1)S(1)}, u32[]{:S(2)}, u32[]{:S(2)}) collective-permute-start(bf16[2,128,768]{1,2,0:T(8,128)(2,1)S(1)} %pad_maximum_fusion), channel_id=1, source_target_pairs={{2,0},{4,2},{6,4},{8,6},{10,8},{12,10},{14,12},{16,14},{18,16},{20... | collective-permute-start | bytes 1179656 | tf_op jit(solution)/shard_map/ppermute | solution.py:12
  118.9 36.6 %collective-permute-start.14 = (bf16[2,128,768]{1,2,0:T(8,128)(2,1)S(1)}, bf16[2,128,768]{1,2,0:T(8,128)(2,1)S(1)}, u32[]{:S(2)}, u32[]{:S(2)}) collective-permute-start(bf16[2,128,768]{1,2,0:T(8,128)(2,1)S(1)} %pad_maximum_fusion), channel_id=1, source_target_pairs={{14,0},{16,2},{18,4},{20,6},{22,8},{24,10},{26,12},{28,14},{30,16}... | collective-permute-start | bytes 1179656 | tf_op jit(solution)/shard_map/ppermute | solution.py:12
  140.2 20.0 %collective-permute-start.15 = (bf16[2,128,768]{1,2,0:T(8,128)(2,1)S(1)}, bf16[2,128,768]{1,2,0:T(8,128)(2,1)S(1)}, u32[]{:S(2)}, u32[]{:S(2)}) collective-permute-start(bf16[2,128,768]{1,2,0:T(8,128)(2,1)S(1)} %pad_maximum_fusion), channel_id=1, source_target_pairs={{16,0},{18,2},{20,4},{22,6},{24,8},{26,10},{28,12},{30,14},{32,16}... | collective-permute-start | bytes 1179656 | tf_op jit(solution)/shard_map/ppermute | solution.py:12
  151.3 37.7 %collective-permute-start.16 = (bf16[2,128,768]{1,2,0:T(8,128)(2,1)S(1)}, bf16[2,128,768]{1,2,0:T(8,128)(2,1)S(1)}, u32[]{:S(2)}, u32[]{:S(2)}) collective-permute-start(bf16[2,128,768]{1,2,0:T(8,128)(2,1)S(1)} %pad_maximum_fusion), channel_id=1, source_target_pairs={{18,0},{20,2},{22,4},{24,6},{26,8},{28,10},{30,12},{32,14},{34,16}... | collective-permute-start | bytes 1179656 | tf_op jit(solution)/shard_map/ppermute | solution.py:12
  152.7 37.7 %collective-permute-start.17 = (bf16[2,128,768]{1,2,0:T(8,128)(2,1)S(1)}, bf16[2,128,768]{1,2,0:T(8,128)(2,1)S(1)}, u32[]{:S(2)}, u32[]{:S(2)}) collective-permute-start(bf16[2,128,768]{1,2,0:T(8,128)(2,1)S(1)} %pad_maximum_fusion), channel_id=1, source_target_pairs={{46,0},{48,2},{50,4},{52,6},{54,8},{56,10},{58,12},{60,14},{62,16}... | collective-permute-start | bytes 1179656 | tf_op jit(solution)/shard_map/ppermute | solution.py:12
  154.1 45.2 %collective-permute-start.18 = (bf16[2,128,768]{1,2,0:T(8,128)(2,1)S(1)}, bf16[2,128,768]{1,2,0:T(8,128)(2,1)S(1)}, u32[]{:S(2)}, u32[]{:S(2)}) collective-permute-start(bf16[2,128,768]{1,2,0:T(8,128)(2,1)S(1)} %pad_maximum_fusion), channel_id=1, source_target_pairs={{48,0},{50,2},{52,4},{54,6},{56,8},{58,10},{60,12},{62,14},{64,16}... | collective-permute-start | bytes 1179656 | tf_op jit(solution)/shard_map/ppermute | solution.py:12
  155.5 45.2 %collective-permute-start.19 = (bf16[2,128,768]{1,2,0:T(8,128)(2,1)S(1)}, bf16[2,128,768]{1,2,0:T(8,128)(2,1)S(1)}, u32[]{:S(2)}, u32[]{:S(2)}) collective-permute-start(bf16[2,128,768]{1,2,0:T(8,128)(2,1)S(1)} %pad_maximum_fusion), channel_id=1, source_target_pairs={{50,0},{52,2},{54,4},{56,6},{58,8},{60,10},{62,12},{64,14},{66,16}... | collective-permute-start | bytes 1179656 | tf_op jit(solution)/shard_map/ppermute | solution.py:12
  160.1 102.8 %collective-permute-start.20 = (bf16[2,128,768]{1,2,0:T(8,128)(2,1)S(1)}, bf16[2,128,768]{1,2,0:T(8,128)(2,1)S(1)}, u32[]{:S(2)}, u32[]{:S(2)}) collective-permute-start(bf16[2,128,768]{1,2,0:T(8,128)(2,1)S(1)} %pad_maximum_fusion), channel_id=1, source_target_pairs={{62,0},{64,2},{66,4},{68,6},{70,8},{72,10},{74,12},{76,14},{78,16}... | collective-permute-start | bytes 1179656 | tf_op jit(solution)/shard_map/ppermute | solution.py:12
  189.0 75.3 %collective-permute-start.21 = (bf16[2,128,768]{1,2,0:T(8,128)(2,1)S(1)}, bf16[2,128,768]{1,2,0:T(8,128)(2,1)S(1)}, u32[]{:S(2)}, u32[]{:S(2)}) collective-permute-start(bf16[2,128,768]{1,2,0:T(8,128)(2,1)S(1)} %pad_maximum_fusion), channel_id=1, source_target_pairs={{64,0},{66,2},{68,4},{70,6},{72,8},{74,10},{76,12},{78,14},{80,16}... | collective-permute-start | bytes 1179656 | tf_op jit(solution)/shard_map/ppermute | solution.py:12
  190.4 74.0 %collective-permute-start.22 = (bf16[2,128,768]{1,2,0:T(8,128)(2,1)S(1)}, bf16[2,128,768]{1,2,0:T(8,128)(2,1)S(1)}, u32[]{:S(2)}, u32[]{:S(2)}) collective-permute-start(bf16[2,128,768]{1,2,0:T(8,128)(2,1)S(1)} %pad_maximum_fusion), channel_id=1, source_target_pairs={{66,0},{68,2},{70,4},{72,6},{74,8},{76,10},{78,12},{80,14},{82,16}... | collective-permute-start | bytes 1179656 | tf_op jit(solution)/shard_map/ppermute | solution.py:12
  199.3 67.4 %collective-permute-start.23 = (bf16[2,128,768]{1,2,0:T(8,128)(2,1)S(1)}, bf16[2,128,768]{1,2,0:T(8,128)(2,1)S(1)}, u32[]{:S(2)}, u32[]{:S(2)}) collective-permute-start(bf16[2,128,768]{1,2,0:T(8,128)(2,1)S(1)} %pad_maximum_fusion), channel_id=1, source_target_pairs={{78,0},{80,2},{82,4},{84,6},{86,8},{88,10},{90,12},{92,14},{94,16}... | collective-permute-start | bytes 1179656 | tf_op jit(solution)/shard_map/ppermute | solution.py:12
  200.7 67.6 %collective-permute-start.24 = (bf16[2,128,768]{1,2,0:T(8,128)(2,1)S(1)}, bf16[2,128,768]{1,2,0:T(8,128)(2,1)S(1)}, u32[]{:S(2)}, u32[]{:S(2)}) collective-permute-start(bf16[2,128,768]{1,2,0:T(8,128)(2,1)S(1)} %pad_maximum_fusion), channel_id=1, source_target_pairs={{80,0},{82,2},{84,4},{86,6},{88,8},{90,10},{92,12},{94,14},{96,16}... | collective-permute-start | bytes 1179656 | tf_op jit(solution)/shard_map/ppermute | solution.py:12
  262.9 24.3 %collective-permute-start.25 = (bf16[2,128,768]{1,2,0:T(8,128)(2,1)S(1)}, bf16[2,128,768]{1,2,0:T(8,128)(2,1)S(1)}, u32[]{:S(2)}, u32[]{:S(2)}) collective-permute-start(bf16[2,128,768]{1,2,0:T(8,128)(2,1)S(1)} %pad_maximum_fusion), channel_id=1, source_target_pairs={{82,0},{84,2},{86,4},{88,6},{90,8},{92,10},{94,12},{96,14},{98,16}... | collective-permute-start | bytes 1179656 | tf_op jit(solution)/shard_map/ppermute | solution.py:12
  287.3 4.0 copy-start
Sparse Core Ops, SparseCore 0:
  37.5 324.2 all-gather.2
  565.9 67.5 reduce-scatter.1
where the time goes:
time: 644 us; the launch traced here: 640 us
  waiting for transfers between devices  237 us (37%)
  local copies, waits for them, and re-layouts  117 us (18%)
  loops' own time  109 us (17%)
  starting transfers between devices  106 us (16%)
  other arithmetic  37.4 us (6%)
  matrix products  21.2 us (3%)
  between operations  14 us (2%)
    ppermute x26, waiting for transfers between devices, passed_along(): return lax.ppermute(value, axis, pairs)  169 us
    another operation x1, loops' own time, body(): running, _ = lax.scan(visit_band, initial, slot_range)  109 us
    ppermute x26, starting transfers between devices, passed_along(): return lax.ppermute(value, axis, pairs)  106 us
    reduce_scatter x1, waiting for transfers between devices, body(): lax.psum_scatter(projection.astype(jnp.bfloat16), 'head', scatter_dimensi...  67.7 us
    dynamic_slice x27, local copies, waits for them, and re-layouts, visit_band(): key_tile = my_tile + slot_distance[slot_index]  35.6 us
    reduce_or x27, other arithmetic, visit_band(): is_listed = inside[slot_index] & jnp.any(listed_tiles == key_tile)  34.3 us
    slice x27, local copies, waits for them, and re-layouts, attend_tile(): value_heads = kv_piece[1].reshape(tok_rows, head_count, head_size)  28.6 us
    dynamic_slice x27, local copies, waits for them, and re-layouts, body(): running, _ = lax.scan(visit_band, initial, slot_range)  17.6 us
  transfers between devices with their start and end apart: 28, of which 12 were waited for; matrix products, arithmetic and copies ran while one was open for 24% of the time, Pallas kernels for 0%

commit v1 on v0

v1 whole, which is shorter than its diff:
```python
import functools

import jax
import jax.numpy as jnp
import numpy as np
from jax import lax
from jax.experimental import pallas as pl
from jax.experimental.pallas import tpu as pltpu
from jax.sharding import Mesh, PartitionSpec as P

HD = 128
TILE = 128
HEADS = 6
FEAT = HEADS * HD
TF, TH, TW = 8, 4, 8
TILES = TF * TH * TW
ALL = ("z", "y", "x", "head")
TOK = ("z", "y", "x")
FACTOR = float(HD**-0.5 * np.log2(np.e))
OFFSETS = (0, 1, -1)
FLAG_ROWS = 16


def place(tile):
    return tile // (TH * TW), tile // TW % TH, tile % TW


def from_neighbour(offset_of_core):
    pairs = []
    for tile in range(TILES):
        for core in range(2):
            f, r, c = (a + b for a, b in zip(place(tile), offset_of_core(core)))
            if 0 <= f < TF and 0 <= r < TH and 0 <= c < TW:
                source = (f * TH + r) * TW + c
                pairs.append((2 * source + core, 2 * tile + core))
    return pairs


def first_axis(step):
    return from_neighbour(lambda core: (step, 0, 0) if core == 0 else (0, 0, step))


def second_axis(step):
    return from_neighbour(lambda core: (0, 0, step) if core == 0 else (step, 0, 0))


def row_axis(step):
    return from_neighbour(lambda core: (0, step, 0))


def biases(window, my_tile, core):
    slot = jnp.arange(27, dtype=jnp.int32)

    def step(digit):
        return jnp.where(digit == 2, -1, digit)

    dr, da, db = step(slot // 9), step(slot // 3 % 3), step(slot % 3)
    df = jnp.where(core == 0, da, db)
    dc = jnp.where(core == 0, db, da)
    f, r, c = place(my_tile)
    inside = (
        (f + df >= 0) & (f + df < TF) & (r + dr >= 0) & (r + dr < TH) & (c + dc >= 0) & (c + dc < TW)
    )
    tile = my_tile + (df * TH + dr) * TW + dc
    listed = inside & jnp.any(window[0][None, :] == tile[:, None], axis=1)
    return jnp.where(listed, 0.0, -1e30).astype(jnp.bfloat16).reshape(3, 9)


def with_biases(queries, bias):
    rows = jnp.zeros((FLAG_ROWS,), jnp.bfloat16).at[:9].set(bias)
    return jnp.concatenate([queries, jnp.broadcast_to(rows[:, None], (FLAG_ROWS, queries.shape[1]))])


def attention_kernel(q0, qp, qm, kv, ap, am, bp, bm, o0, s0, op, om):
    q_refs = (q0, qp, qm)
    bias = []
    for ref in q_refs:
        rows = ref[TILE : TILE + FLAG_ROWS, :HD].astype(jnp.float32)
        bias.append([rows[j : j + 1, :] for j in range(9)])
    tiles = []
    for a, ref in enumerate((kv, ap, am)):
        tiles.append((ref, 0))
        tiles.append((bp, 2 * TILE * a))
        tiles.append((bm, 2 * TILE * a))
    lane = lax.broadcasted_iota(jnp.int32, (TILE, HD), 1)

    def head(h, stats):
        cols = pl.ds(pl.multiple_of(h * HD, HD), HD)
        k = jnp.concatenate([ref[pl.ds(lo, TILE), cols] for ref, lo in tiles], axis=0)
        v = jnp.concatenate([ref[pl.ds(lo + TILE, TILE), cols] for ref, lo in tiles], axis=0)
        new_stats = []
        for i, ref in enumerate(q_refs):
            scores = lax.dot_general(
                ref[pl.ds(0, TILE), cols], k, (((1,), (1,)), ((), ())), preferred_element_type=jnp.float32
            )
            shifted = jnp.concatenate(
                [scores[:, j * TILE : (j + 1) * TILE] * FACTOR + bias[i][j] for j in range(9)], axis=1
            )
            peak = jnp.max(shifted, axis=1, keepdims=True).astype(jnp.bfloat16).astype(jnp.float32)
            unrounded = jnp.exp2(shifted - peak)
            total = jnp.sum(unrounded, axis=1, keepdims=True)
            summed = jnp.dot(unrounded.astype(jnp.bfloat16), v, preferred_element_type=jnp.float32)
            if i == 0:
                o0[:, cols] = summed
                high = total
                low = jnp.zeros_like(total)
            else:
                (op, om)[i - 1][:, cols] = summed.astype(jnp.bfloat16)
                high = total.astype(jnp.bfloat16).astype(jnp.float32)
                low = total - high
            s = jnp.where(lane == h, peak, stats[i])
            s = jnp.where(lane == h + 8, high, s)
            s = jnp.where(lane == h + 16, low, s)
            new_stats.append(s)
        return tuple(new_stats)

    zero = jnp.zeros((TILE, HD), jnp.float32)
    stats = lax.fori_loop(0, HEADS, head, (zero, zero, zero))
    s0[...] = stats[0]
    op[:, FEAT:] = stats[1].astype(jnp.bfloat16)
    om[:, FEAT:] = stats[2].astype(jnp.bfloat16)


def attention(*operands):
    vmem = pl.BlockSpec(memory_space=pltpu.VMEM)
    back = jax.ShapeDtypeStruct((TILE, FEAT + HD), jnp.bfloat16)
    return pl.pallas_call(
        attention_kernel,
        out_shape=(
            jax.ShapeDtypeStruct((TILE, FEAT), jnp.float32),
            jax.ShapeDtypeStruct((TILE, HD), jnp.float32),
            back,
            back,
        ),
        in_specs=[vmem] * len(operands),
        out_specs=(vmem,) * 4,
        compiler_params=pltpu.CompilerParams(vmem_limit_bytes=40 * 1024 * 1024),
        cost_estimate=pl.CostEstimate(
            flops=4 * 27 * TILE * TILE * FEAT, bytes_accessed=6 * 2**20, transcendentals=27 * TILE * TILE * HEADS
        ),
    )(*operands)


def merge_kernel(o0, s0, op, om, out):
    for h in range(HEADS):
        cols = slice(h * HD, (h + 1) * HD)
        peaks, totals, sums = [s0[:, h : h + 1]], [s0[:, h + 8 : h + 9]], [o0[:, cols]]
        for ref in (op, om):
            stats = ref[:, FEAT:].astype(jnp.float32)
            total = stats[:, h + 8 : h + 9] + stats[:, h + 16 : h + 17]
            peaks.append(jnp.where(total > 0, stats[:, h : h + 1], -1e30))
            totals.append(total)
            sums.append(ref[:, cols].astype(jnp.float32))
        peak = jnp.maximum(jnp.maximum(peaks[0], peaks[1]), peaks[2])
        factors = [jnp.exp2(p - peak) for p in peaks]
        total = sum(f * t for f, t in zip(factors, totals))
        summed = sum(f * s for f, s in zip(factors, sums))
        out[:, cols] = (summed / total).astype(jnp.bfloat16)


def merge(*operands):
    vmem = pl.BlockSpec(memory_space=pltpu.VMEM)
    return pl.pallas_call(
        merge_kernel,
        out_shape=jax.ShapeDtypeStruct((TILE, FEAT), jnp.bfloat16),
        in_specs=[vmem] * len(operands),
        out_specs=vmem,
        cost_estimate=pl.CostEstimate(flops=10 * TILE * FEAT, bytes_accessed=2**20, transcendentals=0),
    )(*operands)


def body(queries, keys, values, window, out_weight):
    my_tile = lax.axis_index(TOK)
    core = lax.axis_index("head")
    kv = jnp.concatenate([keys, values])
    ap = lax.ppermute(kv, ALL, first_axis(1))
    am = lax.ppermute(kv, ALL, first_axis(-1))
    weight = lax.all_gather(out_weight.T, TOK)
    bias = biases(window, my_tile, core)
    q0 = with_biases(queries, bias[0])
    qp = lax.ppermute(with_biases(queries, bias[2]), ALL, row_axis(1))
    qm = lax.ppermute(with_biases(queries, bias[1]), ALL, row_axis(-1))
    line = jnp.concatenate([kv, ap, am])
    bp = lax.ppermute(line, ALL, second_axis(1))
    bm = lax.ppermute(line, ALL, second_axis(-1))
    o0, s0, op, om = attention(q0, qp, qm, kv, ap, am, bp, bm)
    back_p = lax.ppermute(om, ALL, row_axis(1))
    back_m = lax.ppermute(op, ALL, row_axis(-1))
    attended = merge(o0, s0, back_p, back_m)
    partial = lax.dot_general(
        attended, weight.reshape(-1, FEAT), (((1,), (1,)), ((), ())), preferred_element_type=jnp.float32
    )
    half = partial.shape[1] // 2
    mine = lax.dynamic_slice_in_dim(partial, core * half, half, 1)
    other = lax.dynamic_slice_in_dim(partial, (1 - core) * half, half, 1).astype(jnp.bfloat16)
    received = lax.ppermute(other, "head", [(0, 1), (1, 0)])
    return (mine + received.astype(jnp.float32)).astype(jnp.bfloat16)


def solution(mesh):
    fine = Mesh(mesh.devices.reshape(8, 8, 4, 2), ALL)
    in_specs = (P(TOK, "head"), P(TOK, "head"), P(TOK, "head"), P(TOK, None), P("head", TOK))
    return jax.shard_map(body, mesh=fine, in_specs=in_specs, out_specs=P(TOK, "head"), check_vma=False)
```

time: 644 us -> 176 us (0.27)
  waiting for transfers between devices: 237 us -> 102 us
  loops' own time: 109 us -> 0 us
  local copies, waits for them, and re-layouts: 117 us -> 12.6 us
  starting transfers between devices: 106 us -> 29.4 us
  other arithmetic: 37.4 us -> 1.21 us
  matrix products: 21.2 us -> 3.95 us
  Pallas kernels: 0 us -> 12.2 us
    ppermute x26 -> x9, waiting for transfers between devices: 169 us -> 19.5 us  [the longest x1 6.37 us: body(): qp = lax.ppermute(with_biases(queries, bias[2]), ALL, row_axis(1))]
    another operation x1 -> x0, loops' own time: 109 us -> none  [body(): running, _ = lax.scan(visit_band, initial, slot_range)]
    all_gather x1, waiting for transfers between devices: 0.02 us -> 81.9 us  [body(): weight = lax.all_gather(out_weight.T, TOK)]
    ppermute x26 -> x9, starting transfers between devices: 106 us -> 29.4 us  [the longest x1 6.17 us: body(): received = lax.ppermute(other, 'head', [(0, 1), (1, 0)])]
    dynamic_slice x81 -> x0, local copies, waits for them, and re-layouts: 70.7 us -> none  [the longest x27 35.6 us: visit_band(): key_tile = my_tile + slot_distance[slot_index]]
    reduce_scatter x1 -> x0, waiting for transfers between devices: 67.7 us -> none  [body(): lax.psum_scatter(projection.astype(jnp.bfloat16), 'head', scatter_dimensi...]
    reduce_or x27 -> x1, other arithmetic: 34.3 us -> 0.18 us  [biases(): listed = inside & jnp.any(window[0][None, :] == tile[:, None], axis=1)]
    slice x27 -> x1, local copies, waits for them, and re-layouts: 28.6 us -> 0.08 us  [body(): qm = lax.ppermute(with_biases(queries, bias[1]), ALL, row_axis(-1))]
  transfers between devices with their start and end apart: 28 -> 10, of which waited for: 12 -> 10; matrix products, arithmetic and copies ran while one was open for 24% -> 1% of each run, Pallas kernels for 0% -> 7%
where the time goes in v1:
time: 176 us; the launch traced here: 175 us
  waiting for transfers between devices  102 us (58%)
  starting transfers between devices  29.4 us (17%)
  between operations  13.6 us (8%)
  local copies, waits for them, and re-layouts  12.6 us (7%)
  Pallas kernels  12.2 us (7%)
  matrix products  3.95 us (2%)
    all_gather x1, waiting for transfers between devices, body(): weight = lax.all_gather(out_weight.T, TOK)  81.9 us
    unnamed x20, local copies, waits for them, and re-layouts  12.4 us
    pallas_call x1, Pallas kernels, attention(): pl.pallas_call(attention_kernel, out_shape=(jax.ShapeDtypeStruct((TILE, F...  8.24 us
    ppermute x1, waiting for transfers between devices, body(): qp = lax.ppermute(with_biases(queries, bias[2]), ALL, row_axis(1))  6.37 us
    ppermute x1, starting transfers between devices, body(): received = lax.ppermute(other, 'head', [(0, 1), (1, 0)])  6.17 us
    ppermute x1, starting transfers between devices, body(): back_m = lax.ppermute(op, ALL, row_axis(-1))  4.95 us
    ppermute x1, starting transfers between devices, body(): am = lax.ppermute(kv, ALL, first_axis(-1))  4.6 us
    ppermute x1, starting transfers between devices, body(): bm = lax.ppermute(line, ALL, second_axis(-1))  4.31 us
  transfers between devices with their start and end apart: 10, of which 10 were waited for; matrix products, arithmetic and copies ran while one was open for 1% of the time, Pallas kernels for 7%

profile of v1, /device:TPU:1, one launch (start us, length us, event | category | flops | bytes accessed | tf_op | source)
XLA Modules:
  0.0 175.1 jit_solution(17733557054054098064)
XLA Ops:
  6.5 0.0 copy-start.6
  6.5 0.0 all-gather.4.cloned.1.call-start
  6.5 0.7 all-gather.4.cloned.1.call-update
  7.3 1.0 constant_dynamic-update-slice_fusion.5
  8.2 0.0 copy-start.7
  8.2 0.0 copy-start.5
  8.2 1.0 constant_dynamic-update-slice_fusion.4
  9.2 1.3 collective-permute-start.2
  10.5 4.6 %collective-permute-start.3 = (bf16[256,768]{1,0:T(8,128)(2,1)S(1)}, bf16[256,768]{1,0:T(8,128)(2,1)S(1)}, u32[]{:S(2)}, u32[]{:S(2)}) collective-permute-start(bf16[256,768]{1,0:T(8,128)(2,1)S(1)} %get-tuple-element.50.kv), channel_id=1, source_target_pairs={{1,3},{3,5},{5,7},{7,9},{9,11},{11,13},{13,15},{17,19},{19,21},{21... | collective-permute-start | bytes 1179656 | tf_op jit(solution)/shard_map/ppermute | solution.py:177
  15.2 0.0 copy-done.6
  15.2 0.2 compare_reduce_fusion
  15.4 2.9 %collective-permute-done.2.ap = bf16[256,768]{1,0:T(8,128)(2,1)S(1)} collective-permute-done((bf16[256,768]{1,0:T(8,128)(2,1)S(1)}, bf16[256,768]{1,0:T(8,128)(2,1)S(1)}, u32[]{:S(2)}, u32[]{:S(2)}) %collective-permute-start.2) | collective-permute-done | bytes 393248 | tf_op jit(solution)/shard_map/ppermute | solution.py:176
  18.4 1.4 collective-permute-done.3.am
  19.9 4.3 %collective-permute-start.5 = (bf16[768,768]{1,0:T(8,128)(2,1)S(1)}, bf16[768,768]{1,0:T(8,128)(2,1)S(1)}, u32[]{:S(2)}, u32[]{:S(2)}) collective-permute-start(bf16[768,768]{1,0:T(8,128)(2,1)S(1)} %constant_dynamic-update-slice_fusion.2), channel_id=1, source_target_pairs={{0,2},{2,4},{4,6},{6,8},{8,10},{10,12},{12,14},{16,18},{18,20},{20... | collective-permute-start | bytes 3538952 | tf_op jit(solution)/shard_map/ppermute | solution.py:185
  24.2 1.3 collective-permute-start.4
  25.5 0.0 copy-done.7
  25.5 0.1 fusion.4
  25.6 0.0 copy-done.5
  25.6 0.1 pad_maximum_fusion
  25.8 4.2 %collective-permute-start.1 = (bf16[144,768]{1,0:T(8,128)(2,1)S(1)}, bf16[144,768]{1,0:T(8,128)(2,1)S(1)}, u32[]{:S(2)}, u32[]{:S(2)}) collective-permute-start(bf16[144,768]{1,0:T(8,128)(2,1)S(1)} %get-tuple-element.53), channel_id=1, source_target_pairs={{0,16},{1,17},{2,18},{3,19},{4,20},{5,21},{6,22},{7,23},{8,24},{9,... | collective-permute-start | bytes 663560 | tf_op jit(solution)/shard_map/ppermute | solution.py:182
  30.0 1.3 collective-permute-start
  31.3 1.5 collective-permute-done.1.qm
  32.9 6.4 %collective-permute-done.qp = bf16[144,768]{1,0:T(8,128)(2,1)S(1)} collective-permute-done((bf16[144,768]{1,0:T(8,128)(2,1)S(1)}, bf16[144,768]{1,0:T(8,128)(2,1)S(1)}, u32[]{:S(2)}, u32[]{:S(2)}) %collective-permute-start) | collective-permute-done | bytes 221216 | tf_op jit(solution)/shard_map/ppermute | solution.py:181
  39.2 0.4 collective-permute-done.5.bm
  39.6 2.6 %collective-permute-done.4.bp = bf16[768,768]{1,0:T(8,128)(2,1)S(1)} collective-permute-done((bf16[768,768]{1,0:T(8,128)(2,1)S(1)}, bf16[768,768]{1,0:T(8,128)(2,1)S(1)}, u32[]{:S(2)}, u32[]{:S(2)}) %collective-permute-start.4) | collective-permute-done | bytes 1179680 | tf_op jit(solution)/shard_map/ppermute | solution.py:184
  42.2 8.2 %shard_map.55 = (f32[128,768]{1,0:T(8,128)S(1)}, f32[128,128]{1,0:T(8,128)S(1)}, bf16[128,896]{1,0:T(8,128)(2,1)S(1)}, bf16[128,896]{1,0:T(8,128)(2,1)S(1)}) custom-call(bf16[144,768]{1,0:T(8,128)(2,1)S(1)} %get-tuple-element.55.q0, bf16[144,768]{1,0:T(8,128)(2,1)S(1)} %collective-permute-done.qp, bf16[144,768]{1,0:T(8,128)(2,1)S(1)} %collective-permute-done.1.qm, ...), custom_call_target="tpu_custom_call" | custom-call | flops 1358954496 | bytes 6291456 | tf_op jit(solution)/shard_map/pallas_call | solution.py:127
  50.4 0.0 copy-start
  50.4 0.7 copy-done
  51.2 0.0 copy-start.1
  51.2 0.6 copy-done.1
  51.8 1.3 collective-permute-start.6
  53.1 5.0 %collective-permute-start.7 = (bf16[128,896]{1,0:T(8,128)(2,1)S(1)}, bf16[128,896]{1,0:T(8,128)(2,1)S(1)}, u32[]{:S(2)}, u32[]{:S(2)}) collective-permute-start(bf16[128,896]{1,0:T(8,128)(2,1)S(1)} %get-tuple-element.48), channel_id=1, source_target_pairs={{0,16},{1,17},{2,18},{3,19},{4,20},{5,21},{6,22},{7,23},{8,24},{9,... | collective-permute-start | bytes 688136 | tf_op jit(solution)/shard_map/ppermute | solution.py:188
  58.0 1.7 collective-permute-done.6.op
  59.8 0.0 copy-start.3
  59.8 1.2 collective-permute-done.7.om
  61.0 0.0 copy-start.4
  61.0 0.0 copy-done.3
  61.0 0.7 copy-done.4
  61.7 3.9 %shard_map.56 = bf16[128,768]{1,0:T(8,128)(2,1)} custom-call(f32[128,768]{1,0:T(8,128)} %copy-done, f32[128,128]{1,0:T(8,128)} %copy-done.1, bf16[128,896]{1,0:T(8,128)(2,1)} %copy-done.3, bf16[128,896]{1,0:T(8,128)(2,1)} %copy-done.4), custom_call_target="tpu_custom_call" | custom-call | flops 983040 | bytes 1048576 | tf_op jit(solution)/shard_map/pallas_call | solution.py:163
  65.6 0.0 copy-start.2
  65.6 81.9 %all-gather.4.cloned.1.call-done = bf16[256,12,768]{2,1,0:T(8,128)(2,1)} async-done(((bf16[1,12,768]{2,1,0:T(8,128)(2,1)}), bf16[256,12,768]{2,1,0:T(8,128)(2,1)}) %all-gather.4.cloned.1.call-update) | async-done | bytes 4718608 | tf_op jit(solution)/shard_map/all_gather | solution.py:178
  147.5 8.4 %reshape.137 = bf16[3072,768]{1,0:T(8,128)(2,1)} reshape(bf16[256,12,768]{2,1,0:T(8,128)(2,1)} %all-gather.4.cloned.1.call-done) | data formatting | bytes 9437184
  155.9 0.0 copy-done.2
  155.9 3.9 %fusion.5 = f32[128,3072]{1,0:T(8,128)S(1)} fusion(bf16[128,768]{1,0:T(8,128)(2,1)S(1)} %copy-done.2, bf16[3072,768]{1,0:T(8,128)(2,1)} %reshape.137), kind=kOutput, calls=%fused_computation.35 | convolution fusion | flops 603979776 | bytes 6488064 | tf_op jit(solution)/shard_map/dot_general | solution.py:190
  159.8 0.1 dynamic-slice_convert_fusion
  159.9 6.2 %collective-permute-start.8 = (bf16[128,1536]{1,0:T(8,128)(2,1)S(1)}, bf16[128,1536]{1,0:T(8,128)(2,1)S(1)}, u32[]{:S(2)}, u32[]{:S(2)}) collective-permute-start(bf16[128,1536]{1,0:T(8,128)(2,1)S(1)} %dynamic-slice_convert_fusion), channel_id=1, source_target_pairs={{0,1},{1,0},{2,3},{3,2},{4,5},{5,4},{6,7},{7,6},{8,9},{9,8},{10,11... | collective-permute-start | bytes 1179656 | tf_op jit(solution)/shard_map/ppermute | solution.py:196
  166.1 1.3 collective-permute-done.8
  167.4 0.8 add_convert_fusion
  (7 shorter events, 0.1 us)
Async XLA Ops:
  6.5 8.7 %copy-start.6 = (s32[1,27]{1,0:T(1,128)S(1)}, s32[1,27]{1,0:T(1,128)}, u32[]{:S(2)}) copy-start(s32[1,27]{1,0:T(1,128)} %param.14) | copy-start | bytes 328
  6.5 141.0 %all-gather.4.cloned.1.call-start = ((), (), s32[]{:S(2)}) async-start(), calls=%async_computation | async-start | bytes 6316032 | tf_op jit(solution)/shard_map/all_gather | solution.py:178
  8.2 17.3 %copy-start.7 = (pred[16]{0:T(512)(128)(4,1)S(1)}, pred[16]{0:T(512)(128)(4,1)}, u32[]{:S(2)}) copy-start(pred[16]{0:T(512)(128)(4,1)} %constant.150.clone.1) | copy-start | bytes 52
  8.2 17.4 %copy-start.5 = (bf16[128,768]{1,0:T(8,128)(2,1)S(1)}, bf16[128,768]{1,0:T(8,128)(2,1)}, u32[]{:S(2)}) copy-start(bf16[128,768]{1,0:T(8,128)(2,1)} %param.11) | copy-start | bytes 589828
  9.2 9.1 %collective-permute-start.2 = (bf16[256,768]{1,0:T(8,128)(2,1)S(1)}, bf16[256,768]{1,0:T(8,128)(2,1)S(1)}, u32[]{:S(2)}, u32[]{:S(2)}) collective-permute-start(bf16[256,768]{1,0:T(8,128)(2,1)S(1)} %get-tuple-element.50.kv), channel_id=1, source_target_pairs={{64,0},{3,1},{66,2},{5,3},{68,4},{7,5},{70,6},{9,7},{72,8},{11,9},... | collective-permute-start | bytes 1179656 | tf_op jit(solution)/shard_map/ppermute | solution.py:176
  10.5 9.3 %collective-permute-start.3 = (bf16[256,768]{1,0:T(8,128)(2,1)S(1)}, bf16[256,768]{1,0:T(8,128)(2,1)S(1)}, u32[]{:S(2)}, u32[]{:S(2)}) collective-permute-start(bf16[256,768]{1,0:T(8,128)(2,1)S(1)} %get-tuple-element.50.kv), channel_id=1, source_target_pairs={{1,3},{3,5},{5,7},{7,9},{9,11},{11,13},{13,15},{17,19},{19,21},{21... | collective-permute-start | bytes 1179656 | tf_op jit(solution)/shard_map/ppermute | solution.py:177
  19.9 19.8 %collective-permute-start.5 = (bf16[768,768]{1,0:T(8,128)(2,1)S(1)}, bf16[768,768]{1,0:T(8,128)(2,1)S(1)}, u32[]{:S(2)}, u32[]{:S(2)}) collective-permute-start(bf16[768,768]{1,0:T(8,128)(2,1)S(1)} %constant_dynamic-update-slice_fusion.2), channel_id=1, source_target_pairs={{0,2},{2,4},{4,6},{6,8},{8,10},{10,12},{12,14},{16,18},{18,20},{20... | collective-permute-start | bytes 3538952 | tf_op jit(solution)/shard_map/ppermute | solution.py:185
  24.2 18.0 %collective-permute-start.4 = (bf16[768,768]{1,0:T(8,128)(2,1)S(1)}, bf16[768,768]{1,0:T(8,128)(2,1)S(1)}, u32[]{:S(2)}, u32[]{:S(2)}) collective-permute-start(bf16[768,768]{1,0:T(8,128)(2,1)S(1)} %constant_dynamic-update-slice_fusion.2), channel_id=1, source_target_pairs={{2,0},{65,1},{4,2},{67,3},{6,4},{69,5},{8,6},{71,7},{10,8},{73,9},... | collective-permute-start | bytes 3538952 | tf_op jit(solution)/shard_map/ppermute | solution.py:184
  25.8 7.1 %collective-permute-start.1 = (bf16[144,768]{1,0:T(8,128)(2,1)S(1)}, bf16[144,768]{1,0:T(8,128)(2,1)S(1)}, u32[]{:S(2)}, u32[]{:S(2)}) collective-permute-start(bf16[144,768]{1,0:T(8,128)(2,1)S(1)} %get-tuple-element.53), channel_id=1, source_target_pairs={{0,16},{1,17},{2,18},{3,19},{4,20},{5,21},{6,22},{7,23},{8,24},{9,... | collective-permute-start | bytes 663560 | tf_op jit(solution)/shard_map/ppermute | solution.py:182
  30.0 9.2 %collective-permute-start = (bf16[144,768]{1,0:T(8,128)(2,1)S(1)}, bf16[144,768]{1,0:T(8,128)(2,1)S(1)}, u32[]{:S(2)}, u32[]{:S(2)}) collective-permute-start(bf16[144,768]{1,0:T(8,128)(2,1)S(1)} %get-tuple-element.54), channel_id=1, source_target_pairs={{16,0},{17,1},{18,2},{19,3},{20,4},{21,5},{22,6},{23,7},{24,8},{25... | collective-permute-start | bytes 663560 | tf_op jit(solution)/shard_map/ppermute | solution.py:181
  50.4 0.7 copy-start
  51.2 0.6 copy-start.1
  51.8 8.0 %collective-permute-start.6 = (bf16[128,896]{1,0:T(8,128)(2,1)S(1)}, bf16[128,896]{1,0:T(8,128)(2,1)S(1)}, u32[]{:S(2)}, u32[]{:S(2)}) collective-permute-start(bf16[128,896]{1,0:T(8,128)(2,1)S(1)} %get-tuple-element.47), channel_id=1, source_target_pairs={{16,0},{17,1},{18,2},{19,3},{20,4},{21,5},{22,6},{23,7},{24,8},{25... | collective-permute-start | bytes 688136 | tf_op jit(solution)/shard_map/ppermute | solution.py:187
  53.1 7.9 %collective-permute-start.7 = (bf16[128,896]{1,0:T(8,128)(2,1)S(1)}, bf16[128,896]{1,0:T(8,128)(2,1)S(1)}, u32[]{:S(2)}, u32[]{:S(2)}) collective-permute-start(bf16[128,896]{1,0:T(8,128)(2,1)S(1)} %get-tuple-element.48), channel_id=1, source_target_pairs={{0,16},{1,17},{2,18},{3,19},{4,20},{5,21},{6,22},{7,23},{8,24},{9,... | collective-permute-start | bytes 688136 | tf_op jit(solution)/shard_map/ppermute | solution.py:188
  59.8 1.2 copy-start.3
  61.0 0.7 copy-start.4
  65.6 90.3 %copy-start.2 = (bf16[128,768]{1,0:T(8,128)(2,1)S(1)}, bf16[128,768]{1,0:T(8,128)(2,1)}, u32[]{:S(2)}) copy-start(bf16[128,768]{1,0:T(8,128)(2,1)} %shard_map.56) | copy-start | bytes 589828
  159.9 7.5 %collective-permute-start.8 = (bf16[128,1536]{1,0:T(8,128)(2,1)S(1)}, bf16[128,1536]{1,0:T(8,128)(2,1)S(1)}, u32[]{:S(2)}, u32[]{:S(2)}) collective-permute-start(bf16[128,1536]{1,0:T(8,128)(2,1)S(1)} %dynamic-slice_convert_fusion), channel_id=1, source_target_pairs={{0,1},{1,0},{2,3},{3,2},{4,5},{5,4},{6,7},{7,6},{8,9},{9,8},{10,11... | collective-permute-start | bytes 1179656 | tf_op jit(solution)/shard_map/ppermute | solution.py:196
Sparse Core Ops, SparseCore 0:
  11.7 135.7 all-gather.3

commit v2 on v1

v2 whole, which is shorter than its diff:
```python
import functools

import jax
import jax.numpy as jnp
import numpy as np
from jax import lax
from jax.experimental import pallas as pl
from jax.experimental.pallas import tpu as pltpu
from jax.sharding import Mesh, PartitionSpec as P

HD = 128
TILE = 128
HEADS = 6
FEAT = HEADS * HD
TF, TH, TW = 8, 4, 8
TILES = TF * TH * TW
ALL = ("z", "y", "x", "head")
TOK = ("z", "y", "x")
FACTOR = float(HD**-0.5 * np.log2(np.e))
OFFSETS = (0, 1, -1)
FLAG_ROWS = 16


def place(tile):
    return tile // (TH * TW), tile // TW % TH, tile % TW


def from_neighbour(offset_of_core):
    pairs = []
    for tile in range(TILES):
        for core in range(2):
            f, r, c = (a + b for a, b in zip(place(tile), offset_of_core(core)))
            if 0 <= f < TF and 0 <= r < TH and 0 <= c < TW:
                source = (f * TH + r) * TW + c
                pairs.append((2 * source + core, 2 * tile + core))
    return pairs


def first_axis(step):
    return from_neighbour(lambda core: (step, 0, 0) if core == 0 else (0, 0, step))


def second_axis(step):
    return from_neighbour(lambda core: (0, 0, step) if core == 0 else (step, 0, 0))


def row_axis(step):
    return from_neighbour(lambda core: (0, step, 0))


def biases(window, my_tile, core):
    slot = jnp.arange(27, dtype=jnp.int32)

    def step(digit):
        return jnp.where(digit == 2, -1, digit)

    dr, da, db = step(slot // 9), step(slot // 3 % 3), step(slot % 3)
    df = jnp.where(core == 0, da, db)
    dc = jnp.where(core == 0, db, da)
    f, r, c = place(my_tile)
    inside = (
        (f + df >= 0) & (f + df < TF) & (r + dr >= 0) & (r + dr < TH) & (c + dc >= 0) & (c + dc < TW)
    )
    tile = my_tile + (df * TH + dr) * TW + dc
    listed = inside & jnp.any(window[0][None, :] == tile[:, None], axis=1)
    return jnp.where(listed, 0.0, -1e30).astype(jnp.bfloat16).reshape(3, 9)


def with_biases(queries, bias):
    rows = jnp.zeros((FLAG_ROWS,), jnp.bfloat16).at[:9].set(bias)
    return jnp.concatenate([queries, jnp.broadcast_to(rows[:, None], (FLAG_ROWS, queries.shape[1]))])


def attention_kernel(groups, query_count, with_state, message, *refs):
    refs = list(refs)
    q_refs = [refs.pop(0) for _ in range(query_count)]
    kv_refs = [refs.pop(0) for _ in range(max(g[0] for g in groups) + 1)]
    old_sum, old_stats = (refs.pop(0), refs.pop(0)) if with_state else (None, None)
    rows = query_count * TILE
    bias = []
    for ref in q_refs:
        block = ref[TILE : TILE + FLAG_ROWS, :HD].astype(jnp.float32)
        bias.append([block[j : j + 1, :] for _, _, j in groups])
    lane = lax.broadcasted_iota(jnp.int32, (rows, HD), 1)
    stats = jnp.zeros((rows, HD), jnp.float32)
    for h in range(HEADS):
        cols = slice(h * HD, (h + 1) * HD)
        q = jnp.concatenate([ref[:TILE, cols] for ref in q_refs], axis=0)
        k = jnp.concatenate([kv_refs[n][lo : lo + TILE, cols] for n, lo, _ in groups], axis=0)
        v = jnp.concatenate([kv_refs[n][lo + TILE : lo + 2 * TILE, cols] for n, lo, _ in groups], axis=0)
        scores = lax.dot_general(q, k, (((1,), (1,)), ((), ())), preferred_element_type=jnp.float32)
        shifted = jnp.concatenate(
            [
                jnp.concatenate(
                    [
                        scores[i * TILE : (i + 1) * TILE, j * TILE : (j + 1) * TILE] * FACTOR + bias[i][j]
                        for j in range(len(groups))
                    ],
                    axis=1,
                )
                for i in range(query_count)
            ],
            axis=0,
        )
        peak = jnp.max(shifted, axis=1, keepdims=True)
        if with_state:
            old_peak = old_stats[:, h : h + 1]
            peak = jnp.maximum(peak, old_peak)
        peak = peak.astype(jnp.bfloat16).astype(jnp.float32)
        unrounded = jnp.exp2(shifted - peak)
        total = jnp.sum(unrounded, axis=1, keepdims=True)
        summed = jnp.dot(unrounded.astype(jnp.bfloat16), v, preferred_element_type=jnp.float32)
        if with_state:
            factor = jnp.exp2(old_peak - peak)
            total = total + factor * old_stats[:, h + 8 : h + 9]
            summed = summed + factor * old_sum[:, cols]
        stats = jnp.where(lane == h, peak, stats)
        if message:
            high = total.astype(jnp.bfloat16).astype(jnp.float32)
            stats = jnp.where(lane == h + 8, high, stats)
            stats = jnp.where(lane == h + 16, total - high, stats)
            for i in range(query_count):
                refs[i][:, cols] = summed[i * TILE : (i + 1) * TILE].astype(jnp.bfloat16)
        else:
            stats = jnp.where(lane == h + 8, total, stats)
            refs[0][:, cols] = summed
    if message:
        for i in range(query_count):
            refs[i][:, FEAT:] = stats[i * TILE : (i + 1) * TILE].astype(jnp.bfloat16)
    else:
        refs[1][...] = stats


VMEM = pl.BlockSpec(memory_space=pltpu.VMEM)


def attention(queries, pieces, groups, state=None, message=False):
    count = len(queries)
    rows = count * TILE
    if message:
        out_shape = (jax.ShapeDtypeStruct((TILE, FEAT + HD), jnp.bfloat16),) * count
    else:
        out_shape = (
            jax.ShapeDtypeStruct((rows, FEAT), jnp.float32),
            jax.ShapeDtypeStruct((rows, HD), jnp.float32),
        )
    in_specs = [VMEM] * (count + len(pieces))
    operands = [*queries, *pieces]
    if state is not None:
        (total_rows, which), arrays = state
        for array in arrays:
            in_specs.append(pl.BlockSpec((rows, array.shape[1]), lambda i: (which, 0)))
            operands.append(array)
    pairs = count * len(groups)
    return pl.pallas_call(
        functools.partial(attention_kernel, groups, count, state is not None, message),
        grid=(1,),
        out_shape=out_shape,
        in_specs=in_specs,
        out_specs=(VMEM,) * len(out_shape),
        compiler_params=pltpu.CompilerParams(vmem_limit_bytes=40 * 1024 * 1024),
        cost_estimate=pl.CostEstimate(
            flops=4 * pairs * TILE * TILE * FEAT,
            bytes_accessed=len(groups) * 4 * TILE * FEAT,
            transcendentals=pairs * TILE * TILE * HEADS,
        ),
    )(*operands)


def merge_kernel(o0, s0, op, om, out):
    own = s0[...]
    peaks, totals, sums = [own], [pltpu.roll(own, HD - 8, 1)], [o0]
    for ref in (op, om):
        stats = ref[:, FEAT:].astype(jnp.float32)
        total = pltpu.roll(stats, HD - 8, 1) + pltpu.roll(stats, HD - 16, 1)
        peaks.append(jnp.where(total > 0, stats, -1e30))
        totals.append(total)
        sums.append(ref)
    peak = jnp.maximum(jnp.maximum(peaks[0], peaks[1]), peaks[2])
    factors = [jnp.exp2(p - peak) for p in peaks]
    total = sum(f * t for f, t in zip(factors, totals))
    shares = [f / total for f in factors]
    for h in range(HEADS):
        cols = slice(h * HD, (h + 1) * HD)
        parts = [w[:, h : h + 1] * ref[:, cols].astype(jnp.float32) for w, ref in zip(shares, sums)]
        out[:, cols] = (parts[0] + parts[1] + parts[2]).astype(jnp.bfloat16)


def merge(*operands):
    return pl.pallas_call(
        merge_kernel,
        out_shape=jax.ShapeDtypeStruct((TILE, FEAT), jnp.bfloat16),
        in_specs=[VMEM] * len(operands),
        out_specs=VMEM,
        cost_estimate=pl.CostEstimate(flops=10 * TILE * FEAT, bytes_accessed=2**20, transcendentals=0),
    )(*operands)


def project_kernel(_, rows, weight, out):
    product = lax.dot_general(
        rows[...], weight[...], (((1,), (1,)), ((), ())), preferred_element_type=jnp.float32
    )
    out[...] = product.astype(out.dtype)


def project(rows, weight, which, dtype):
    half = weight.shape[0] // 2
    return pl.pallas_call(
        project_kernel,
        grid_spec=pltpu.PrefetchScalarGridSpec(
            num_scalar_prefetch=1,
            grid=(1,),
            in_specs=[
                pl.BlockSpec(rows.shape, lambda i, c: (0, 0)),
                pl.BlockSpec((half, FEAT), lambda i, c: (c[0], 0)),
            ],
            out_specs=pl.BlockSpec((rows.shape[0], half), lambda i, c: (0, 0)),
        ),
        out_shape=jax.ShapeDtypeStruct((rows.shape[0], half), dtype),
        compiler_params=pltpu.CompilerParams(vmem_limit_bytes=40 * 1024 * 1024),
        cost_estimate=pl.CostEstimate(
            flops=2 * rows.shape[0] * half * FEAT, bytes_accessed=3 * 2**20, transcendentals=0
        ),
    )(which[None], rows, weight)


PAD = 16
SHARE = 12
WIDE = 8 * 4 * SHARE


def column_order():
    order = np.zeros((4, 8, PAD, WIDE), np.float32)
    for x in range(4):
        for p in range(8):
            y = (p & 1) * 4 + (p & 2) + (p >> 2)
            for j in range(SHARE):
                order[x, p, j, (y * 4 + x) * SHARE + j] = 1
    return order.reshape(4 * HD, WIDE)


def arrange_kernel(pieces, order, out):
    for z in range(4):
        block = jnp.concatenate([pieces[x, :, z * HD : (z + 1) * HD] for x in range(4)], axis=1)
        product = jnp.dot(block, order[...], preferred_element_type=jnp.float32)
        out[:, z * WIDE : (z + 1) * WIDE] = product.astype(jnp.bfloat16)


def arrange(pieces):
    return pl.pallas_call(
        arrange_kernel,
        out_shape=jax.ShapeDtypeStruct((TILE, 4 * WIDE), jnp.bfloat16),
        in_specs=[VMEM, VMEM],
        out_specs=VMEM,
        cost_estimate=pl.CostEstimate(flops=2 * TILE * 4 * HD * 4 * WIDE, bytes_accessed=2**20, transcendentals=0),
    )(pieces, jnp.asarray(column_order(), jnp.bfloat16))


def gathered_weight(out_weight):
    part = jnp.pad(out_weight.T, ((0, PAD - SHARE), (0, 0)))
    y = lax.axis_index("y")
    for bit in (4, 2, 1):
        other = lax.ppermute(part, "y", [(i, i ^ bit) for i in range(8)])
        upper = (y & bit) != 0
        part = jnp.concatenate([jnp.where(upper, other, part), jnp.where(upper, part, other)])
    return part


def body(queries, keys, values, window, out_weight):
    my_tile = lax.axis_index(TOK)
    core = lax.axis_index("head")
    kv = jnp.concatenate([keys, values])
    ap = lax.ppermute(kv, ALL, first_axis(1))
    am = lax.ppermute(kv, ALL, first_axis(-1))
    weight = lax.all_gather(gathered_weight(out_weight), "z", tiled=True)
    bias = biases(window, my_tile, core)
    q0 = with_biases(queries, bias[0])
    qp = lax.ppermute(with_biases(queries, bias[2]), ALL, row_axis(1))
    qm = lax.ppermute(with_biases(queries, bias[1]), ALL, row_axis(-1))
    line = jnp.concatenate([kv, ap, am])
    bp = lax.ppermute(line, ALL, second_axis(1))
    bm = lax.ppermute(line, ALL, second_axis(-1))
    near = [(n, 0, 3 * n) for n in range(3)]
    far = [(n, 2 * TILE * a, 3 * a + n + 1) for n in range(2) for a in range(3)]
    state = attention((qp, qm, q0), (kv, ap, am), near)
    op, om = attention((qp, qm), (bp, bm), far, ((3, 0), state), message=True)
    back_p = lax.ppermute(om, ALL, row_axis(1))
    back_m = lax.ppermute(op, ALL, row_axis(-1))
    o0, s0 = attention((q0,), (bp, bm), far, ((3, 2), state))
    attended = merge(o0, s0, back_p, back_m)
    rows = lax.all_gather(attended, "x", tiled=True)
    other = project(rows, weight, 1 - core, jnp.bfloat16)
    received = lax.ppermute(other, "head", [(0, 1), (1, 0)])
    mine = project(rows, weight, core, jnp.float32)
    columns = (mine + received.astype(jnp.float32)).astype(jnp.bfloat16)
    pieces = lax.all_to_all(columns.reshape(4, TILE, -1), "x", 0, 0)
    return arrange(pieces)


def solution(mesh):
    fine = Mesh(mesh.devices.reshape(8, 8, 4, 2), ALL)
    in_specs = (P(TOK, "head"), P(TOK, "head"), P(TOK, "head"), P(TOK, None), P("head", TOK))
    return jax.shard_map(body, mesh=fine, in_specs=in_specs, out_specs=P(TOK, "head"), check_vma=False)
```

time: 176 us -> 148 us (0.84)
  the two profiles are of different devices: /device:TPU:1 before, /device:TPU:240 now
where the time goes in v2:
time: 148 us
  starting transfers between devices  36.2 us (24%)
  waiting for transfers between devices  35.7 us (24%)
  blocking collectives  32.8 us (22%)
  Pallas kernels  14.7 us (10%)
  between operations  13.7 us (9%)
  local copies, waits for them, and re-layouts  12.3 us (8%)
  other arithmetic  2.1 us (1%)
    all_gather x1, blocking collectives, body(): rows = lax.all_gather(attended, 'x', tiled=True)  19.6 us
    all_to_all x1, blocking collectives, body(): pieces = lax.all_to_all(columns.reshape(4, TILE, -1), 'x', 0, 0)  13.3 us
    ppermute x3, waiting for transfers between devices, gathered_weight(): other = lax.ppermute(part, 'y', [(i, i ^ bit) for i in range(8)])  12.4 us
    ppermute x3, starting transfers between devices, gathered_weight(): other = lax.ppermute(part, 'y', [(i, i ^ bit) for i in range(8)])  10.5 us
    unnamed x40, local copies, waits for them, and re-layouts  9.96 us
    pallas_call x3, Pallas kernels, attention(): pl.pallas_call(functools.partial(attention_kernel, groups, count, state i...  8.77 us
    ppermute x1, waiting for transfers between devices, body(): qm = lax.ppermute(with_biases(queries, bias[1]), ALL, row_axis(-1))  7.49 us
    ppermute x1, starting transfers between devices, body(): am = lax.ppermute(kv, ALL, first_axis(-1))  5.49 us
  transfers between devices with their start and end apart: 13, of which 10 were waited for; matrix products, arithmetic and copies ran while one was open for 2% of the time, Pallas kernels for 8%

profile of v2, /device:TPU:240, one launch (start us, length us, event | category | flops | bytes accessed | tf_op | source)
XLA Modules:
  0.0 147.6 jit_solution(9415074084278735198)
XLA Ops:
  6.5 0.0 all-gather.2.cloned.1.call-start
  6.5 0.8 pad.13
  7.3 3.8 %collective-permute-start.8 = (bf16[16,768]{1,0:T(8,128)(2,1)S(1)}, bf16[16,768]{1,0:T(8,128)(2,1)S(1)}, u32[]{:S(2)}, u32[]{:S(2)}) collective-permute-start(bf16[16,768]{1,0:T(8,128)(2,1)S(1)} %pad.13), channel_id=1, source_target_pairs={{0,32},{8,40},{16,48},{24,56},{32,0},{40,8},{48,16},{56,24},{1,33}... | collective-permute-start | bytes 73736 | tf_op jit(solution)/shard_map/ppermute | solution.py:263
  11.2 5.8 %collective-permute-done.8 = bf16[16,768]{1,0:T(8,128)(2,1)S(1)} collective-permute-done((bf16[16,768]{1,0:T(8,128)(2,1)S(1)}, bf16[16,768]{1,0:T(8,128)(2,1)S(1)}, u32[]{:S(2)}, u32[]{:S(2)}) %collective-permute-start.8) | collective-permute-done | bytes 24608 | tf_op jit(solution)/shard_map/ppermute | solution.py:263
  17.0 0.8 broadcast_select_fusion.5
  17.7 4.1 %collective-permute-start.9 = (bf16[32,768]{1,0:T(8,128)(2,1)S(1)}, bf16[32,768]{1,0:T(8,128)(2,1)S(1)}, u32[]{:S(2)}, u32[]{:S(2)}) collective-permute-start(bf16[32,768]{1,0:T(8,128)(2,1)S(1)} %pad_maximum_fusion.5), channel_id=1, source_target_pairs={{0,16},{8,24},{16,0},{24,8},{32,48},{40,56},{48,32},{56,40},{1,17}... | collective-permute-start | bytes 147464 | tf_op jit(solution)/shard_map/ppermute | solution.py:263
  21.8 2.8 %collective-permute-done.9 = bf16[32,768]{1,0:T(8,128)(2,1)S(1)} collective-permute-done((bf16[32,768]{1,0:T(8,128)(2,1)S(1)}, bf16[32,768]{1,0:T(8,128)(2,1)S(1)}, u32[]{:S(2)}, u32[]{:S(2)}) %collective-permute-start.9) | collective-permute-done | bytes 49184 | tf_op jit(solution)/shard_map/ppermute | solution.py:263
  24.6 0.0 copy-start.17
  24.7 2.6 %collective-permute-start.10 = (bf16[64,768]{1,0:T(8,128)(2,1)S(1)}, bf16[64,768]{1,0:T(8,128)(2,1)S(1)}, u32[]{:S(2)}, u32[]{:S(2)}) collective-permute-start(bf16[64,768]{1,0:T(8,128)(2,1)S(1)} %pad_maximum_fusion.4), channel_id=1, source_target_pairs={{0,8},{8,0},{16,24},{24,16},{32,40},{40,32},{48,56},{56,48},{1,9},... | collective-permute-start | bytes 294920 | tf_op jit(solution)/shard_map/ppermute | solution.py:263
  27.3 3.9 %collective-permute-done.10 = bf16[64,768]{1,0:T(8,128)(2,1)S(1)} collective-permute-done((bf16[64,768]{1,0:T(8,128)(2,1)S(1)}, bf16[64,768]{1,0:T(8,128)(2,1)S(1)}, u32[]{:S(2)}, u32[]{:S(2)}) %collective-permute-start.10) | collective-permute-done | bytes 98336 | tf_op jit(solution)/shard_map/ppermute | solution.py:263
  31.2 0.7 pad_maximum_fusion
  31.9 0.0 all-gather.2.cloned.1.call-update
  31.9 0.0 copy-done.14
  31.9 0.7 constant_dynamic-update-slice_fusion.1
  32.6 0.0 copy-done.15
  32.6 0.7 constant_dynamic-update-slice_fusion
  33.3 1.9 %collective-permute-start = (bf16[256,768]{1,0:T(8,128)(2,1)S(1)}, bf16[256,768]{1,0:T(8,128)(2,1)S(1)}, u32[]{:S(2)}, u32[]{:S(2)}) collective-permute-start(bf16[256,768]{1,0:T(8,128)(2,1)S(1)} %get-tuple-element.58.refs_3_), channel_id=1, source_target_pairs={{64,0},{3,1},{66,2},{5,3},{68,4},{7,5},{70,6},{9,7},{72,8},{11,9},... | collective-permute-start | bytes 1179656 | tf_op jit(solution)/shard_map/ppermute | solution.py:273
  35.3 5.5 %collective-permute-start.1 = (bf16[256,768]{1,0:T(8,128)(2,1)S(1)}, bf16[256,768]{1,0:T(8,128)(2,1)S(1)}, u32[]{:S(2)}, u32[]{:S(2)}) collective-permute-start(bf16[256,768]{1,0:T(8,128)(2,1)S(1)} %get-tuple-element.58.refs_3_), channel_id=1, source_target_pairs={{1,3},{3,5},{5,7},{7,9},{9,11},{11,13},{13,15},{17,19},{19,21},{21... | collective-permute-start | bytes 1179656 | tf_op jit(solution)/shard_map/ppermute | solution.py:274
  40.8 0.0 copy-done.17
  40.9 0.2 compare_reduce_fusion
  41.0 3.5 %collective-permute-done.refs_4_ = bf16[256,768]{1,0:T(8,128)(2,1)S(1)} collective-permute-done((bf16[256,768]{1,0:T(8,128)(2,1)S(1)}, bf16[256,768]{1,0:T(8,128)(2,1)S(1)}, u32[]{:S(2)}, u32[]{:S(2)}) %collective-permute-start) | collective-permute-done | bytes 393248 | tf_op jit(solution)/shard_map/ppermute | solution.py:273
  44.6 0.8 constant_dynamic-update-slice_fusion.3
  45.4 0.6 collective-permute-done.1.refs_5_
  46.0 0.0 copy-done.8
  46.0 0.0 copy-done.4
  46.0 0.8 constant_dynamic-update-slice_fusion.2
  46.8 0.7 copy-done.6
  47.6 1.3 collective-permute-start.2
  48.9 4.6 %collective-permute-start.3 = (bf16[768,768]{1,0:T(8,128)(2,1)}, bf16[768,768]{1,0:T(8,128)(2,1)S(1)}, u32[]{:S(2)}, u32[]{:S(2)}) collective-permute-start(bf16[768,768]{1,0:T(8,128)(2,1)} %constant_dynamic-update-slice_fusion.2), channel_id=1, source_target_pairs={{0,2},{2,4},{4,6},{6,8},{8,10},{10,12},{12,14},{16,18},{18,20},{20... | collective-permute-start | bytes 3538952 | tf_op jit(solution)/shard_map/ppermute | solution.py:282
  53.6 0.1 fusion.4
  53.7 0.1 pad_maximum_fusion.1
  53.8 0.0 copy-start.2
  53.8 4.6 %collective-permute-start.4 = (bf16[144,768]{1,0:T(8,128)(2,1)S(1)}, bf16[144,768]{1,0:T(8,128)(2,1)S(1)}, u32[]{:S(2)}, u32[]{:S(2)}) collective-permute-start(bf16[144,768]{1,0:T(8,128)(2,1)S(1)} %get-tuple-element.56), channel_id=1, source_target_pairs={{16,0},{17,1},{18,2},{19,3},{20,4},{21,5},{22,6},{23,7},{24,8},{25... | collective-permute-start | bytes 663560 | tf_op jit(solution)/shard_map/ppermute | solution.py:278
  58.5 1.3 collective-permute-start.5
  59.8 4.3 %collective-permute-done.4.refs_0_ = bf16[144,768]{1,0:T(8,128)(2,1)S(1)} collective-permute-done((bf16[144,768]{1,0:T(8,128)(2,1)S(1)}, bf16[144,768]{1,0:T(8,128)(2,1)S(1)}, u32[]{:S(2)}, u32[]{:S(2)}) %collective-permute-start.4) | collective-permute-done | bytes 221216 | tf_op jit(solution)/shard_map/ppermute | solution.py:278
  64.1 7.5 %collective-permute-done.5.refs_1_ = bf16[144,768]{1,0:T(8,128)(2,1)S(1)} collective-permute-done((bf16[144,768]{1,0:T(8,128)(2,1)S(1)}, bf16[144,768]{1,0:T(8,128)(2,1)S(1)}, u32[]{:S(2)}, u32[]{:S(2)}) %collective-permute-start.5) | collective-permute-done | bytes 221216 | tf_op jit(solution)/shard_map/ppermute | solution.py:279
  71.6 1.0 copy-done.5
  72.6 1.0 copy-done.7
  73.6 1.0 copy-done.9
  74.6 2.1 %shard_map.64 = (f32[384,768]{1,0:T(8,128)S(1)}, f32[384,128]{1,0:T(8,128)S(1)}) custom-call(bf16[144,768]{1,0:T(8,128)(2,1)S(1)} %collective-permute-done.4.refs_0_, bf16[144,768]{1,0:T(8,128)(2,1)S(1)} %collective-permute-done.5.refs_1_, bf16[144,768]{1,0:T(8,128)(2,1)S(1)} %get-tuple-element.57.refs_2_.refs_0_, bf16[256,768]{1,0:T(8,128)(2,1)S(1)} %copy-done.9, ...), custom_call_target="tpu_custom_call" | custom-call | flops 452984832 | bytes 1179648 | tf_op jit(solution)/shard_map/pallas_call | solution.py:155
  76.8 0.0 copy-start.10
  76.8 0.0 collective-permute-done.2.refs_1_.refs_2_
  76.8 0.0 collective-permute-done.3.refs_2_.refs_3_
  76.8 3.9 %shard_map.66 = (bf16[128,896]{1,0:T(8,128)(2,1)}, bf16[128,896]{1,0:T(8,128)(2,1)}) custom-call(bf16[144,768]{1,0:T(8,128)(2,1)S(1)} %collective-permute-done.4.refs_0_, bf16[144,768]{1,0:T(8,128)(2,1)S(1)} %collective-permute-done.5.refs_1_, bf16[768,768]{1,0:T(8,128)(2,1)S(1)} %collective-permute-done.2.refs_1_.refs_2_, ...), custom_call_target="tpu_custom_call" | custom-call | flops 603979776 | bytes 2359296 | tf_op jit(solution)/shard_map/pallas_call | solution.py:155
  80.7 3.2 %collective-permute-start.6 = (bf16[128,896]{1,0:T(8,128)(2,1)}, bf16[128,896]{1,0:T(8,128)(2,1)}, u32[]{:S(2)}, u32[]{:S(2)}) collective-permute-start(bf16[128,896]{1,0:T(8,128)(2,1)} %get-tuple-element.51), channel_id=1, source_target_pairs={{16,0},{17,1},{18,2},{19,3},{20,4},{21,5},{22,6},{23,7},{24,8},{25... | collective-permute-start | bytes 688136 | tf_op jit(solution)/shard_map/ppermute | solution.py:287
  83.9 1.3 collective-permute-start.7
  85.2 0.9 copy-done.3
  86.1 0.9 copy-done.11
  87.0 2.7 %shard_map.65 = (f32[128,768]{1,0:T(8,128)S(1)}, f32[128,128]{1,0:T(8,128)S(1)}) custom-call(bf16[144,768]{1,0:T(8,128)(2,1)S(1)} %copy-done.3, bf16[768,768]{1,0:T(8,128)(2,1)S(1)} %collective-permute-done.2.refs_1_.refs_2_, bf16[768,768]{1,0:T(8,128)(2,1)S(1)} %collective-permute-done.3.refs_2_.refs_3_, f32[384,768]{1,0:T(8,128)S(1)} %get-tuple-element.47.refs_3_.refs_4_, ...), custom_call_target="tpu_custom_call" | custom-call | flops 301989888 | bytes 2359296 | tf_op jit(solution)/shard_map/pallas_call | solution.py:155
  89.8 0.0 copy-start.12
  89.8 0.7 copy-done.12
  90.5 0.6 copy-done.13
  91.1 3.2 %collective-permute-done.6.op = bf16[128,896]{1,0:T(8,128)(2,1)} collective-permute-done((bf16[128,896]{1,0:T(8,128)(2,1)}, bf16[128,896]{1,0:T(8,128)(2,1)}, u32[]{:S(2)}, u32[]{:S(2)}) %collective-permute-start.6) | collective-permute-done | bytes 229408 | tf_op jit(solution)/shard_map/ppermute | solution.py:287
  94.4 2.7 %collective-permute-done.7.om = bf16[128,896]{1,0:T(8,128)(2,1)} collective-permute-done((bf16[128,896]{1,0:T(8,128)(2,1)}, bf16[128,896]{1,0:T(8,128)(2,1)}, u32[]{:S(2)}, u32[]{:S(2)}) %collective-permute-start.7) | collective-permute-done | bytes 229408 | tf_op jit(solution)/shard_map/ppermute | solution.py:288
  97.1 2.4 %shard_map.67 = bf16[128,768]{1,0:T(8,128)(2,1)} custom-call(f32[128,768]{1,0:T(8,128)} %copy-done.12, f32[128,128]{1,0:T(8,128)} %copy-done.13, bf16[128,896]{1,0:T(8,128)(2,1)} %collective-permute-done.6.op, bf16[128,896]{1,0:T(8,128)(2,1)} %collective-permute-done.7.om), custom_call_target="tpu_custom_call" | custom-call | flops 983040 | bytes 1048576 | tf_op jit(solution)/shard_map/pallas_call | solution.py:190
  99.5 19.6 %all_gather.6.rows = bf16[512,768]{1,0:T(8,128)(2,1)S(1)} all-gather(bf16[128,768]{1,0:T(8,128)(2,1)} %shard_map.67), channel_id=1, replica_groups=mesh['z'=8,'y'=8,'x'=4,'head'=2] {'x'}, dimensions={0}, use_global_device_ids=true | all-gather | bytes 983040 | tf_op jit(solution)/shard_map/all_gather | solution.py:291
  119.1 1.4 copy-done
  120.5 0.6 shard_map.69
  121.1 1.9 %collective-permute-start.11 = (bf16[512,512]{1,0:T(8,128)(2,1)S(1)}, bf16[512,512]{1,0:T(8,128)(2,1)S(1)}, u32[]{:S(2)}, u32[]{:S(2)}) collective-permute-start(bf16[512,512]{1,0:T(8,128)(2,1)S(1)} %shard_map.69), channel_id=1, source_target_pairs={{0,1},{1,0},{2,3},{3,2},{4,5},{5,4},{6,7},{7,6},{8,9},{9,8},{10,11... | collective-permute-start | bytes 1572872 | tf_op jit(solution)/shard_map/ppermute | solution.py:293
  123.1 0.6 shard_map.68
  123.7 1.3 collective-permute-done.11
  124.9 0.2 add_convert_fusion
  125.1 13.3 %all_to_all.5.pieces = bf16[4,128,512]{2,1,0:T(8,128)(2,1)} all-to-all(bf16[4,128,512]{2,1,0:T(8,128)(2,1)S(1)} %bitcast.5), channel_id=1, replica_groups=mesh['z'=8,'y'=8,'x'=4,'head'=2] {'x'}, dimensions={0} | all-to-all | bytes 1048576 | tf_op jit(solution)/shard_map/all_to_all | solution.py:296
  138.4 2.3 %shard_map.70 = bf16[128,1536]{1,0:T(8,128)(2,1)} custom-call(bf16[4,128,512]{2,1,0:T(8,128)(2,1)} %all_to_all.5.pieces, bf16[512,384]{1,0:T(8,128)(2,1)} %constant.173.clone.order), custom_call_target="tpu_custom_call" | custom-call | flops 201326592 | bytes 1048576 | tf_op jit(solution)/shard_map/pallas_call | solution.py:250
  (30 shorter events, 0.2 us)
Async XLA Ops:
  6.5 25.4 %copy-start.14 = (bf16[128,768]{1,0:T(8,128)(2,1)S(1)}, bf16[128,768]{1,0:T(8,128)(2,1)}, u32[]{:S(2)}) copy-start(bf16[128,768]{1,0:T(8,128)(2,1)} %param.13) | copy-start | bytes 589828
  6.5 26.1 %copy-start.15 = (bf16[128,768]{1,0:T(8,128)(2,1)S(1)}, bf16[128,768]{1,0:T(8,128)(2,1)}, u32[]{:S(2)}) copy-start(bf16[128,768]{1,0:T(8,128)(2,1)} %param.14) | copy-start | bytes 589828
  6.5 112.6 %all-gather.2.cloned.1.call-start = ((), (), s32[]{:S(2)}) async-start(), calls=%async_computation.1 | async-start | bytes 1769472 | tf_op jit(solution)/shard_map/all_gather | solution.py:275
  7.3 9.6 %collective-permute-start.8 = (bf16[16,768]{1,0:T(8,128)(2,1)S(1)}, bf16[16,768]{1,0:T(8,128)(2,1)S(1)}, u32[]{:S(2)}, u32[]{:S(2)}) collective-permute-start(bf16[16,768]{1,0:T(8,128)(2,1)S(1)} %pad.13), channel_id=1, source_target_pairs={{0,32},{8,40},{16,48},{24,56},{32,0},{40,8},{48,16},{56,24},{1,33}... | collective-permute-start | bytes 73736 | tf_op jit(solution)/shard_map/ppermute | solution.py:263
  17.7 6.9 %collective-permute-start.9 = (bf16[32,768]{1,0:T(8,128)(2,1)S(1)}, bf16[32,768]{1,0:T(8,128)(2,1)S(1)}, u32[]{:S(2)}, u32[]{:S(2)}) collective-permute-start(bf16[32,768]{1,0:T(8,128)(2,1)S(1)} %pad_maximum_fusion.5), channel_id=1, source_target_pairs={{0,16},{8,24},{16,0},{24,8},{32,48},{40,56},{48,32},{56,40},{1,17}... | collective-permute-start | bytes 147464 | tf_op jit(solution)/shard_map/ppermute | solution.py:263
  24.6 16.2 %copy-start.17 = (s32[1,27]{1,0:T(1,128)S(1)}, s32[1,27]{1,0:T(1,128)}, u32[]{:S(2)}) copy-start(s32[1,27]{1,0:T(1,128)} %param.15) | copy-start | bytes 328
  24.7 6.5 %collective-permute-start.10 = (bf16[64,768]{1,0:T(8,128)(2,1)S(1)}, bf16[64,768]{1,0:T(8,128)(2,1)S(1)}, u32[]{:S(2)}, u32[]{:S(2)}) collective-permute-start(bf16[64,768]{1,0:T(8,128)(2,1)S(1)} %pad_maximum_fusion.4), channel_id=1, source_target_pairs={{0,8},{8,0},{16,24},{24,16},{32,40},{40,32},{48,56},{56,48},{1,9},... | collective-permute-start | bytes 294920 | tf_op jit(solution)/shard_map/ppermute | solution.py:263
  32.6 20.9 %copy-start.18 = (pred[16]{0:T(512)(128)(4,1)S(1)}, pred[16]{0:T(512)(128)(4,1)}, u32[]{:S(2)}) copy-start(pred[16]{0:T(512)(128)(4,1)} %constant.153.clone.1) | copy-start | bytes 52
  32.6 21.0 %copy-start.16 = (bf16[128,768]{1,0:T(8,128)(2,1)S(1)}, bf16[128,768]{1,0:T(8,128)(2,1)}, u32[]{:S(2)}) copy-start(bf16[128,768]{1,0:T(8,128)(2,1)} %param.12) | copy-start | bytes 589828
  33.3 12.7 %copy-start.8 = (bf16[256,768]{1,0:T(8,128)(2,1)}, bf16[256,768]{1,0:T(8,128)(2,1)S(1)}, u32[]{:S(2)}) copy-start(bf16[256,768]{1,0:T(8,128)(2,1)S(1)} %get-tuple-element.58.refs_3_) | copy-start | bytes 1179652
  33.3 11.2 %collective-permute-start = (bf16[256,768]{1,0:T(8,128)(2,1)S(1)}, bf16[256,768]{1,0:T(8,128)(2,1)S(1)}, u32[]{:S(2)}, u32[]{:S(2)}) collective-permute-start(bf16[256,768]{1,0:T(8,128)(2,1)S(1)} %get-tuple-element.58.refs_3_), channel_id=1, source_target_pairs={{64,0},{3,1},{66,2},{5,3},{68,4},{7,5},{70,6},{9,7},{72,8},{11,9},... | collective-permute-start | bytes 1179656 | tf_op jit(solution)/shard_map/ppermute | solution.py:273
  35.3 10.8 %collective-permute-start.1 = (bf16[256,768]{1,0:T(8,128)(2,1)S(1)}, bf16[256,768]{1,0:T(8,128)(2,1)S(1)}, u32[]{:S(2)}, u32[]{:S(2)}) collective-permute-start(bf16[256,768]{1,0:T(8,128)(2,1)S(1)} %get-tuple-element.58.refs_3_), channel_id=1, source_target_pairs={{1,3},{3,5},{5,7},{7,9},{9,11},{11,13},{13,15},{17,19},{19,21},{21... | collective-permute-start | bytes 1179656 | tf_op jit(solution)/shard_map/ppermute | solution.py:274
  44.6 1.5 copy-start.4
  46.8 0.7 copy-start.6
  47.6 29.2 %collective-permute-start.2 = (bf16[768,768]{1,0:T(8,128)(2,1)}, bf16[768,768]{1,0:T(8,128)(2,1)S(1)}, u32[]{:S(2)}, u32[]{:S(2)}) collective-permute-start(bf16[768,768]{1,0:T(8,128)(2,1)} %constant_dynamic-update-slice_fusion.2), channel_id=1, source_target_pairs={{2,0},{65,1},{4,2},{67,3},{6,4},{69,5},{8,6},{71,7},{10,8},{73,9},... | collective-permute-start | bytes 3538952 | tf_op jit(solution)/shard_map/ppermute | solution.py:281
  48.9 27.9 %collective-permute-start.3 = (bf16[768,768]{1,0:T(8,128)(2,1)}, bf16[768,768]{1,0:T(8,128)(2,1)S(1)}, u32[]{:S(2)}, u32[]{:S(2)}) collective-permute-start(bf16[768,768]{1,0:T(8,128)(2,1)} %constant_dynamic-update-slice_fusion.2), channel_id=1, source_target_pairs={{0,2},{2,4},{4,6},{6,8},{8,10},{10,12},{12,14},{16,18},{18,20},{20... | collective-permute-start | bytes 3538952 | tf_op jit(solution)/shard_map/ppermute | solution.py:282
  53.8 26.9 %copy-start.2 = (bf16[144,768]{1,0:T(8,128)(2,1)}, bf16[144,768]{1,0:T(8,128)(2,1)S(1)}, u32[]{:S(2)}) copy-start(bf16[144,768]{1,0:T(8,128)(2,1)S(1)} %get-tuple-element.57.refs_2_.refs_0_) | copy-start | bytes 663556
  53.8 10.3 %collective-permute-start.4 = (bf16[144,768]{1,0:T(8,128)(2,1)S(1)}, bf16[144,768]{1,0:T(8,128)(2,1)S(1)}, u32[]{:S(2)}, u32[]{:S(2)}) collective-permute-start(bf16[144,768]{1,0:T(8,128)(2,1)S(1)} %get-tuple-element.56), channel_id=1, source_target_pairs={{16,0},{17,1},{18,2},{19,3},{20,4},{21,5},{22,6},{23,7},{24,8},{25... | collective-permute-start | bytes 663560 | tf_op jit(solution)/shard_map/ppermute | solution.py:278
  58.5 13.1 %collective-permute-start.5 = (bf16[144,768]{1,0:T(8,128)(2,1)S(1)}, bf16[144,768]{1,0:T(8,128)(2,1)S(1)}, u32[]{:S(2)}, u32[]{:S(2)}) collective-permute-start(bf16[144,768]{1,0:T(8,128)(2,1)S(1)} %get-tuple-element.55), channel_id=1, source_target_pairs={{0,16},{1,17},{2,18},{3,19},{4,20},{5,21},{6,22},{7,23},{8,24},{9,... | collective-permute-start | bytes 663560 | tf_op jit(solution)/shard_map/ppermute | solution.py:279
  71.6 1.0 copy-start.5
  72.6 1.0 copy-start.7
  73.6 1.0 copy-start.9
  76.8 3.9 %copy-start.10 = (f32[384,128]{1,0:T(8,128)}, f32[384,128]{1,0:T(8,128)S(1)}, u32[]{:S(2)}) copy-start(f32[384,128]{1,0:T(8,128)S(1)} %get-tuple-element.48.refs_4_.refs_5_) | copy-start | bytes 589828
  80.7 13.7 %collective-permute-start.6 = (bf16[128,896]{1,0:T(8,128)(2,1)}, bf16[128,896]{1,0:T(8,128)(2,1)}, u32[]{:S(2)}, u32[]{:S(2)}) collective-permute-start(bf16[128,896]{1,0:T(8,128)(2,1)} %get-tuple-element.51), channel_id=1, source_target_pairs={{16,0},{17,1},{18,2},{19,3},{20,4},{21,5},{22,6},{23,7},{24,8},{25... | collective-permute-start | bytes 688136 | tf_op jit(solution)/shard_map/ppermute | solution.py:287
  83.9 13.2 %collective-permute-start.7 = (bf16[128,896]{1,0:T(8,128)(2,1)}, bf16[128,896]{1,0:T(8,128)(2,1)}, u32[]{:S(2)}, u32[]{:S(2)}) collective-permute-start(bf16[128,896]{1,0:T(8,128)(2,1)} %get-tuple-element.52), channel_id=1, source_target_pairs={{0,16},{1,17},{2,18},{3,19},{4,20},{5,21},{6,22},{7,23},{8,24},{9,... | collective-permute-start | bytes 688136 | tf_op jit(solution)/shard_map/ppermute | solution.py:288
  85.2 0.9 copy-start.3
  86.1 0.9 copy-start.11
  89.8 0.7 copy-start.12
  90.5 0.6 copy-start.13
  119.1 1.4 copy-start
  120.5 2.5 %copy-start.1 = (bf16[1024,768]{1,0:T(8,128)(2,1)S(1)}, bf16[1024,768]{1,0:T(8,128)(2,1)}, u32[]{:S(2)}) copy-start(bf16[1024,768]{1,0:T(8,128)(2,1)} %all-gather.2.cloned.1.call-done.weight) | copy-start | bytes 4718596
  121.1 3.8 %collective-permute-start.11 = (bf16[512,512]{1,0:T(8,128)(2,1)S(1)}, bf16[512,512]{1,0:T(8,128)(2,1)S(1)}, u32[]{:S(2)}, u32[]{:S(2)}) collective-permute-start(bf16[512,512]{1,0:T(8,128)(2,1)S(1)} %shard_map.69), channel_id=1, source_target_pairs={{0,1},{1,0},{2,3},{3,2},{4,5},{5,4},{6,7},{7,6},{8,9},{9,8},{10,11... | collective-permute-start | bytes 1572872 | tf_op jit(solution)/shard_map/ppermute | solution.py:293
Sparse Core Ops, SparseCore 0:
  32.0 46.1 all-gather.1

commit v3 on v2

--- a/solution.py
+++ b/solution.py
@@ -158,9 +158,9 @@
         out_shape=out_shape,
         in_specs=in_specs,
         out_specs=(VMEM,) * len(out_shape),
-        compiler_params=pltpu.CompilerParams(vmem_limit_bytes=40 * 1024 * 1024),
+        compiler_params=pltpu.CompilerParams(vmem_limit_bytes=12 * 1024 * 1024),
         cost_estimate=pl.CostEstimate(
-            flops=4 * pairs * TILE * TILE * FEAT,
+            flops=160 * pairs * TILE * TILE * FEAT,
             bytes_accessed=len(groups) * 4 * TILE * FEAT,
             transcendentals=pairs * TILE * TILE * HEADS,
         ),
@@ -192,6 +192,7 @@
         out_shape=jax.ShapeDtypeStruct((TILE, FEAT), jnp.bfloat16),
         in_specs=[VMEM] * len(operands),
         out_specs=VMEM,
+        compiler_params=pltpu.CompilerParams(vmem_limit_bytes=12 * 1024 * 1024),
         cost_estimate=pl.CostEstimate(flops=10 * TILE * FEAT, bytes_accessed=2**20, transcendentals=0),
     )(*operands)
 
@@ -217,7 +218,7 @@
             out_specs=pl.BlockSpec((rows.shape[0], half), lambda i, c: (0, 0)),
         ),
         out_shape=jax.ShapeDtypeStruct((rows.shape[0], half), dtype),
-        compiler_params=pltpu.CompilerParams(vmem_limit_bytes=40 * 1024 * 1024),
+        compiler_params=pltpu.CompilerParams(vmem_limit_bytes=12 * 1024 * 1024),
         cost_estimate=pl.CostEstimate(
             flops=2 * rows.shape[0] * half * FEAT, bytes_accessed=3 * 2**20, transcendentals=0
         ),
@@ -252,14 +253,14 @@
         out_shape=jax.ShapeDtypeStruct((TILE, 4 * WIDE), jnp.bfloat16),
         in_specs=[VMEM, VMEM],
         out_specs=VMEM,
+        compiler_params=pltpu.CompilerParams(vmem_limit_bytes=12 * 1024 * 1024),
         cost_estimate=pl.CostEstimate(flops=2 * TILE * 4 * HD * 4 * WIDE, bytes_accessed=2**20, transcendentals=0),
     )(pieces, jnp.asarray(column_order(), jnp.bfloat16))
 
 
-def gathered_weight(out_weight):
-    part = jnp.pad(out_weight.T, ((0, PAD - SHARE), (0, 0)))
+def gathered_weight(part, bits):
     y = lax.axis_index("y")
-    for bit in (4, 2, 1):
+    for bit in bits:
         other = lax.ppermute(part, "y", [(i, i ^ bit) for i in range(8)])
         upper = (y & bit) != 0
         part = jnp.concatenate([jnp.where(upper, other, part), jnp.where(upper, part, other)])
@@ -272,12 +273,14 @@
     kv = jnp.concatenate([keys, values])
     ap = lax.ppermute(kv, ALL, first_axis(1))
     am = lax.ppermute(kv, ALL, first_axis(-1))
-    weight = lax.all_gather(gathered_weight(out_weight), "z", tiled=True)
+    part = gathered_weight(jnp.pad(out_weight.T, ((0, PAD - SHARE), (0, 0))), (4,))
     bias = biases(window, my_tile, core)
     q0 = with_biases(queries, bias[0])
     qp = lax.ppermute(with_biases(queries, bias[2]), ALL, row_axis(1))
     qm = lax.ppermute(with_biases(queries, bias[1]), ALL, row_axis(-1))
+    ap, am, qp, qm, part = lax.optimization_barrier((ap, am, qp, qm, part))
     line = jnp.concatenate([kv, ap, am])
+    weight = lax.all_gather(gathered_weight(part, (2, 1)), "z", tiled=True)
     bp = lax.ppermute(line, ALL, second_axis(1))
     bm = lax.ppermute(line, ALL, second_axis(-1))
     near = [(n, 0, 3 * n) for n in range(3)]

time: 148 us -> 143 us (0.966)
  the two profiles are of different devices: /device:TPU:240 before, /device:TPU:8 now
where the time goes in v3:
time: 143 us; the launch traced here: 142 us
  starting transfers between devices  42.3 us (30%)
  waiting for transfers between devices  35.6 us (25%)
  blocking collectives  27.1 us (19%)
  between operations  13.8 us (10%)
  Pallas kernels  13.5 us (9%)
  local copies, waits for them, and re-layouts  8.36 us (6%)
    all_gather x1, waiting for transfers between devices, body(): weight = lax.all_gather(gathered_weight(part, (2, 1)), 'z', tiled=True)  15.1 us
    ppermute x3, starting transfers between devices, gathered_weight(): other = lax.ppermute(part, 'y', [(i, i ^ bit) for i in range(8)])  14.8 us
    all_to_all x1, blocking collectives, body(): pieces = lax.all_to_all(columns.reshape(4, TILE, -1), 'x', 0, 0)  13.8 us
    all_gather x1, blocking collectives, body(): rows = lax.all_gather(attended, 'x', tiled=True)  13.3 us
    pallas_call x3, Pallas kernels, attention(): pl.pallas_call(functools.partial(attention_kernel, groups, count, state i...  10.6 us
    ppermute x1, waiting for transfers between devices, body(): qp = lax.ppermute(with_biases(queries, bias[2]), ALL, row_axis(1))  8.05 us
    ppermute x3, waiting for transfers between devices, gathered_weight(): other = lax.ppermute(part, 'y', [(i, i ^ bit) for i in range(8)])  6.62 us
    unnamed x22, local copies, waits for them, and re-layouts  6.55 us
  transfers between devices with their start and end apart: 13, of which 6 were waited for; matrix products, arithmetic and copies ran while one was open for 2% of the time, Pallas kernels for 8%

profile of v3, /device:TPU:8, one launch (start us, length us, event | category | flops | bytes accessed | tf_op | source)
XLA Modules:
  0.0 142.0 jit_solution(2122510016398137399)
XLA Ops:
  6.5 0.0 copy-start.9
  6.5 0.0 copy-start.6
  6.5 0.0 copy-start.8
  6.5 0.0 copy-start.5
  6.5 0.0 all-gather.2.cloned.1.call-start
  6.6 1.0 constant_dynamic-update-slice_fusion.1
  7.6 1.0 constant_dynamic-update-slice_fusion
  8.5 0.0 copy-start.7
  8.5 1.0 copy-done.7
  9.6 1.3 collective-permute-start
  10.9 4.9 %collective-permute-start.1 = (bf16[256,768]{1,0:T(8,128)(2,1)S(1)}, bf16[256,768]{1,0:T(8,128)(2,1)S(1)}, u32[]{:S(2)}, u32[]{:S(2)}) collective-permute-start(bf16[256,768]{1,0:T(8,128)(2,1)S(1)} %get-tuple-element.68.refs_3_), channel_id=1, source_target_pairs={{1,3},{3,5},{5,7},{7,9},{9,11},{11,13},{13,15},{17,19},{19,21},{21... | collective-permute-start | bytes 1179656 | tf_op jit(solution)/shard_map/ppermute | solution.py:275
  15.8 0.0 copy-done.6
  15.8 6.8 %collective-permute-start.4 = (bf16[16,768]{1,0:T(8,128)(2,1)S(1)}, bf16[16,768]{1,0:T(8,128)(2,1)S(1)}, u32[]{:S(2)}, u32[]{:S(2)}) collective-permute-start(bf16[16,768]{1,0:T(8,128)(2,1)S(1)} %pad.13), channel_id=1, source_target_pairs={{0,32},{8,40},{16,48},{24,56},{32,0},{40,8},{48,16},{56,24},{1,33}... | collective-permute-start | bytes 73736 | tf_op jit(solution)/shard_map/ppermute | solution.py:264
  22.8 0.0 copy-done.8
  22.8 0.2 compare_reduce_fusion
  23.0 0.1 fusion.4
  23.1 0.0 copy-done.9
  23.1 0.0 copy-done.5
  23.1 0.1 pad_maximum_fusion.1
  23.3 1.3 collective-permute-start.2
  24.6 5.5 %collective-permute-start.3 = (bf16[144,768]{1,0:T(8,128)(2,1)S(1)}, bf16[144,768]{1,0:T(8,128)(2,1)S(1)}, u32[]{:S(2)}, u32[]{:S(2)}) collective-permute-start(bf16[144,768]{1,0:T(8,128)(2,1)S(1)} %get-tuple-element.65), channel_id=1, source_target_pairs={{0,16},{1,17},{2,18},{3,19},{4,20},{5,21},{6,22},{7,23},{8,24},{9,... | collective-permute-start | bytes 663560 | tf_op jit(solution)/shard_map/ppermute | solution.py:280
  30.1 0.0 collective-permute-done.4
  30.1 8.1 %collective-permute-done.2.refs_0_ = bf16[144,768]{1,0:T(8,128)(2,1)S(1)} collective-permute-done((bf16[144,768]{1,0:T(8,128)(2,1)S(1)}, bf16[144,768]{1,0:T(8,128)(2,1)S(1)}, u32[]{:S(2)}, u32[]{:S(2)}) %collective-permute-start.2) | collective-permute-done | bytes 221216 | tf_op jit(solution)/shard_map/ppermute | solution.py:279
  38.2 0.7 collective-permute-done.3.refs_1_
  38.8 0.0 collective-permute-done.refs_4_
  38.8 0.0 collective-permute-done.1.refs_5_
  38.9 5.8 %collective-permute-start.9 = (bf16[32,768]{1,0:T(8,128)(2,1)S(1)}, bf16[32,768]{1,0:T(8,128)(2,1)S(1)}, u32[]{:S(2)}, u32[]{:S(2)}) collective-permute-start(bf16[32,768]{1,0:T(8,128)(2,1)S(1)} %pad_maximum_fusion.5), channel_id=1, source_target_pairs={{0,16},{8,24},{16,0},{24,8},{32,48},{40,56},{48,32},{56,40},{1,17}... | collective-permute-start | bytes 147464 | tf_op jit(solution)/shard_map/ppermute | solution.py:264
  44.6 0.8 constant_dynamic-update-slice_fusion.3
  45.4 0.8 constant_dynamic-update-slice_fusion.2
  46.2 1.9 %collective-permute-start.5 = (bf16[768,768]{1,0:T(8,128)(2,1)}, bf16[768,768]{1,0:T(8,128)(2,1)S(1)}, u32[]{:S(2)}, u32[]{:S(2)}) collective-permute-start(bf16[768,768]{1,0:T(8,128)(2,1)} %constant_dynamic-update-slice_fusion.2), channel_id=1, source_target_pairs={{2,0},{65,1},{4,2},{67,3},{6,4},{69,5},{8,6},{71,7},{10,8},{73,9},... | collective-permute-start | bytes 3538952 | tf_op jit(solution)/shard_map/ppermute | solution.py:284
  48.1 3.9 %collective-permute-start.6 = (bf16[768,768]{1,0:T(8,128)(2,1)}, bf16[768,768]{1,0:T(8,128)(2,1)}, u32[]{:S(2)}, u32[]{:S(2)}) collective-permute-start(bf16[768,768]{1,0:T(8,128)(2,1)} %constant_dynamic-update-slice_fusion.2), channel_id=1, source_target_pairs={{0,2},{2,4},{4,6},{6,8},{8,10},{10,12},{12,14},{16,18},{18,20},{20... | collective-permute-start | bytes 3538952 | tf_op jit(solution)/shard_map/ppermute | solution.py:285
  52.0 0.0 collective-permute-done.9
  52.1 2.2 %collective-permute-start.10 = (bf16[64,768]{1,0:T(8,128)(2,1)S(1)}, bf16[64,768]{1,0:T(8,128)(2,1)S(1)}, u32[]{:S(2)}, u32[]{:S(2)}) collective-permute-start(bf16[64,768]{1,0:T(8,128)(2,1)S(1)} %pad_maximum_fusion.4), channel_id=1, source_target_pairs={{0,8},{8,0},{16,24},{24,16},{32,40},{40,32},{48,56},{56,48},{1,9},... | collective-permute-start | bytes 294920 | tf_op jit(solution)/shard_map/ppermute | solution.py:264
  54.3 2.1 %shard_map.64 = (f32[384,768]{1,0:T(8,128)S(1)}, f32[384,128]{1,0:T(8,128)S(1)}) custom-call(bf16[144,768]{1,0:T(8,128)(2,1)S(1)} %collective-permute-done.2.refs_0_, bf16[144,768]{1,0:T(8,128)(2,1)S(1)} %collective-permute-done.3.refs_1_, bf16[144,768]{1,0:T(8,128)(2,1)S(1)} %get-tuple-element.67.refs_2_.refs_0_, ...), custom_call_target="tpu_custom_call" | custom-call | flops 18119393280 | bytes 1179648 | tf_op jit(solution)/shard_map/pallas_call | solution.py:155
  56.4 0.0 copy-start.3
  56.4 1.0 copy-done.3
  57.5 6.6 %collective-permute-done.10 = bf16[64,768]{1,0:T(8,128)(2,1)S(1)} collective-permute-done((bf16[64,768]{1,0:T(8,128)(2,1)S(1)}, bf16[64,768]{1,0:T(8,128)(2,1)S(1)}, u32[]{:S(2)}, u32[]{:S(2)}) %collective-permute-start.10) | collective-permute-done | bytes 98336 | tf_op jit(solution)/shard_map/ppermute | solution.py:264
  64.1 0.7 pad_maximum_fusion
  64.8 0.0 all-gather.2.cloned.1.call-update
  64.8 0.0 collective-permute-done.5.refs_1_.refs_2_
  64.9 3.8 %collective-permute-done.6.refs_2_.refs_3_ = bf16[768,768]{1,0:T(8,128)(2,1)} collective-permute-done((bf16[768,768]{1,0:T(8,128)(2,1)}, bf16[768,768]{1,0:T(8,128)(2,1)}, u32[]{:S(2)}, u32[]{:S(2)}) %collective-permute-start.6) | collective-permute-done | bytes 1179680 | tf_op jit(solution)/shard_map/ppermute | solution.py:285
  68.7 1.3 copy-done.4
  69.9 4.4 %shard_map.66 = (bf16[128,896]{1,0:T(8,128)(2,1)S(1)}, bf16[128,896]{1,0:T(8,128)(2,1)S(1)}) custom-call(bf16[144,768]{1,0:T(8,128)(2,1)S(1)} %collective-permute-done.2.refs_0_, bf16[144,768]{1,0:T(8,128)(2,1)S(1)} %collective-permute-done.3.refs_1_, bf16[768,768]{1,0:T(8,128)(2,1)S(1)} %collective-permute-done.5.refs_1_.refs_2_, ...), custom_call_target="tpu_custom_call" | custom-call | flops 24159191040 | bytes 2359296 | tf_op jit(solution)/shard_map/pallas_call | solution.py:155
  74.4 1.3 collective-permute-start.7
  75.7 5.5 %collective-permute-start.8 = (bf16[128,896]{1,0:T(8,128)(2,1)S(1)}, bf16[128,896]{1,0:T(8,128)(2,1)S(1)}, u32[]{:S(2)}, u32[]{:S(2)}) collective-permute-start(bf16[128,896]{1,0:T(8,128)(2,1)S(1)} %get-tuple-element.61), channel_id=1, source_target_pairs={{0,16},{1,17},{2,18},{3,19},{4,20},{5,21},{6,22},{7,23},{8,24},{9,... | collective-permute-start | bytes 688136 | tf_op jit(solution)/shard_map/ppermute | solution.py:291
  81.1 4.0 %shard_map.65 = (f32[128,768]{1,0:T(8,128)S(1)}, f32[128,128]{1,0:T(8,128)S(1)}) custom-call(bf16[144,768]{1,0:T(8,128)(2,1)S(1)} %get-tuple-element.67.refs_2_.refs_0_, bf16[768,768]{1,0:T(8,128)(2,1)S(1)} %collective-permute-done.5.refs_1_.refs_2_, bf16[768,768]{1,0:T(8,128)(2,1)} %collective-permute-done.6.refs_2_.refs_3_, f32[384,768]{1,0:T(8,128)S(1)} %copy-done.4, ...), custom_call_target="tpu_custom_call" | custom-call | flops 12079595520 | bytes 2359296 | tf_op jit(solution)/shard_map/pallas_call | solution.py:155
  85.1 0.0 collective-permute-done.7.op
  85.1 0.0 collective-permute-done.8.om
  85.2 0.5 shard_map.67
  85.7 13.3 %all_gather.6.rows = bf16[512,768]{1,0:T(8,128)(2,1)S(1)} all-gather(bf16[128,768]{1,0:T(8,128)(2,1)S(1)} %shard_map.67), channel_id=1, replica_groups=mesh['z'=8,'y'=8,'x'=4,'head'=2] {'x'}, dimensions={0}, use_global_device_ids=true | all-gather | bytes 983040 | tf_op jit(solution)/shard_map/all_gather | solution.py:294
  99.0 15.1 %all-gather.2.cloned.1.call-done.weight = bf16[1024,768]{1,0:T(8,128)(2,1)} async-done(((bf16[128,768]{1,0:T(8,128)(2,1)}), bf16[1024,768]{1,0:T(8,128)(2,1)}) %all-gather.2.cloned.1.call-update) | async-done | bytes 1572880 | tf_op jit(solution)/shard_map/all_gather | solution.py:283
  114.2 0.0 copy-start
  114.2 1.4 copy-done
  115.6 0.0 copy-start.1
  115.6 0.6 shard_map.69
  116.2 1.9 %collective-permute-start.11 = (bf16[512,512]{1,0:T(8,128)(2,1)S(1)}, bf16[512,512]{1,0:T(8,128)(2,1)S(1)}, u32[]{:S(2)}, u32[]{:S(2)}) collective-permute-start(bf16[512,512]{1,0:T(8,128)(2,1)S(1)} %shard_map.69), channel_id=1, source_target_pairs={{0,1},{1,0},{2,3},{3,2},{4,5},{5,4},{6,7},{7,6},{8,9},{9,8},{10,11... | collective-permute-start | bytes 1572872 | tf_op jit(solution)/shard_map/ppermute | solution.py:296
  118.1 0.0 copy-done.1
  118.1 0.6 shard_map.68
  118.7 0.0 copy-start.2
  118.7 1.2 collective-permute-done.11
  120.0 0.2 add_convert_fusion
  120.2 13.8 %all_to_all.5.pieces = bf16[4,128,512]{2,1,0:T(8,128)(2,1)S(1)} all-to-all(bf16[4,128,512]{2,1,0:T(8,128)(2,1)S(1)} %bitcast.5), channel_id=1, replica_groups=mesh['z'=8,'y'=8,'x'=4,'head'=2] {'x'}, dimensions={0} | all-to-all | bytes 1048576 | tf_op jit(solution)/shard_map/all_to_all | solution.py:299
  134.0 0.0 copy-done.2
  134.0 1.2 shard_map.70
  (12 shorter events, 0.2 us)
Async XLA Ops:
  6.5 16.6 %copy-start.9 = (pred[16]{0:T(512)(128)(4,1)S(1)}, pred[16]{0:T(512)(128)(4,1)}, u32[]{:S(2)}) copy-start(pred[16]{0:T(512)(128)(4,1)} %constant.153.clone.1) | copy-start | bytes 52
  6.5 9.3 %copy-start.6 = (bf16[768,12]{0,1:T(8,128)(2,1)S(1)}, bf16[768,12]{0,1:T(8,128)(2,1)}, u32[]{:S(2)}) copy-start(bf16[768,12]{0,1:T(8,128)(2,1)} %param.16) | copy-start | bytes 55300
  6.5 16.2 %copy-start.8 = (s32[1,27]{1,0:T(1,128)S(1)}, s32[1,27]{1,0:T(1,128)}, u32[]{:S(2)}) copy-start(s32[1,27]{1,0:T(1,128)} %param.15) | copy-start | bytes 328
  6.5 16.6 %copy-start.5 = (bf16[128,768]{1,0:T(8,128)(2,1)S(1)}, bf16[128,768]{1,0:T(8,128)(2,1)}, u32[]{:S(2)}) copy-start(bf16[128,768]{1,0:T(8,128)(2,1)} %param.12) | copy-start | bytes 589828
  6.5 107.6 %all-gather.2.cloned.1.call-start = ((), (), s32[]{:S(2)}) async-start(), calls=%async_computation.1 | async-start | bytes 1769472 | tf_op jit(solution)/shard_map/all_gather | solution.py:283
  8.5 1.0 copy-start.7
  9.6 29.3 %collective-permute-start = (bf16[256,768]{1,0:T(8,128)(2,1)S(1)}, bf16[256,768]{1,0:T(8,128)(2,1)S(1)}, u32[]{:S(2)}, u32[]{:S(2)}) collective-permute-start(bf16[256,768]{1,0:T(8,128)(2,1)S(1)} %get-tuple-element.68.refs_3_), channel_id=1, source_target_pairs={{64,0},{3,1},{66,2},{5,3},{68,4},{7,5},{70,6},{9,7},{72,8},{11,9},... | collective-permute-start | bytes 1179656 | tf_op jit(solution)/shard_map/ppermute | solution.py:274
  10.9 28.0 %collective-permute-start.1 = (bf16[256,768]{1,0:T(8,128)(2,1)S(1)}, bf16[256,768]{1,0:T(8,128)(2,1)S(1)}, u32[]{:S(2)}, u32[]{:S(2)}) collective-permute-start(bf16[256,768]{1,0:T(8,128)(2,1)S(1)} %get-tuple-element.68.refs_3_), channel_id=1, source_target_pairs={{1,3},{3,5},{5,7},{7,9},{9,11},{11,13},{13,15},{17,19},{19,21},{21... | collective-permute-start | bytes 1179656 | tf_op jit(solution)/shard_map/ppermute | solution.py:275
  15.8 14.2 %collective-permute-start.4 = (bf16[16,768]{1,0:T(8,128)(2,1)S(1)}, bf16[16,768]{1,0:T(8,128)(2,1)S(1)}, u32[]{:S(2)}, u32[]{:S(2)}) collective-permute-start(bf16[16,768]{1,0:T(8,128)(2,1)S(1)} %pad.13), channel_id=1, source_target_pairs={{0,32},{8,40},{16,48},{24,56},{32,0},{40,8},{48,16},{56,24},{1,33}... | collective-permute-start | bytes 73736 | tf_op jit(solution)/shard_map/ppermute | solution.py:264
  23.3 14.9 %collective-permute-start.2 = (bf16[144,768]{1,0:T(8,128)(2,1)S(1)}, bf16[144,768]{1,0:T(8,128)(2,1)S(1)}, u32[]{:S(2)}, u32[]{:S(2)}) collective-permute-start(bf16[144,768]{1,0:T(8,128)(2,1)S(1)} %get-tuple-element.66), channel_id=1, source_target_pairs={{16,0},{17,1},{18,2},{19,3},{20,4},{21,5},{22,6},{23,7},{24,8},{25... | collective-permute-start | bytes 663560 | tf_op jit(solution)/shard_map/ppermute | solution.py:279
  24.6 14.3 %collective-permute-start.3 = (bf16[144,768]{1,0:T(8,128)(2,1)S(1)}, bf16[144,768]{1,0:T(8,128)(2,1)S(1)}, u32[]{:S(2)}, u32[]{:S(2)}) collective-permute-start(bf16[144,768]{1,0:T(8,128)(2,1)S(1)} %get-tuple-element.65), channel_id=1, source_target_pairs={{0,16},{1,17},{2,18},{3,19},{4,20},{5,21},{6,22},{7,23},{8,24},{9,... | collective-permute-start | bytes 663560 | tf_op jit(solution)/shard_map/ppermute | solution.py:280
  38.9 13.2 %collective-permute-start.9 = (bf16[32,768]{1,0:T(8,128)(2,1)S(1)}, bf16[32,768]{1,0:T(8,128)(2,1)S(1)}, u32[]{:S(2)}, u32[]{:S(2)}) collective-permute-start(bf16[32,768]{1,0:T(8,128)(2,1)S(1)} %pad_maximum_fusion.5), channel_id=1, source_target_pairs={{0,16},{8,24},{16,0},{24,8},{32,48},{40,56},{48,32},{56,40},{1,17}... | collective-permute-start | bytes 147464 | tf_op jit(solution)/shard_map/ppermute | solution.py:264
  46.2 18.7 %collective-permute-start.5 = (bf16[768,768]{1,0:T(8,128)(2,1)}, bf16[768,768]{1,0:T(8,128)(2,1)S(1)}, u32[]{:S(2)}, u32[]{:S(2)}) collective-permute-start(bf16[768,768]{1,0:T(8,128)(2,1)} %constant_dynamic-update-slice_fusion.2), channel_id=1, source_target_pairs={{2,0},{65,1},{4,2},{67,3},{6,4},{69,5},{8,6},{71,7},{10,8},{73,9},... | collective-permute-start | bytes 3538952 | tf_op jit(solution)/shard_map/ppermute | solution.py:284
  48.1 20.6 %collective-permute-start.6 = (bf16[768,768]{1,0:T(8,128)(2,1)}, bf16[768,768]{1,0:T(8,128)(2,1)}, u32[]{:S(2)}, u32[]{:S(2)}) collective-permute-start(bf16[768,768]{1,0:T(8,128)(2,1)} %constant_dynamic-update-slice_fusion.2), channel_id=1, source_target_pairs={{0,2},{2,4},{4,6},{6,8},{8,10},{10,12},{12,14},{16,18},{18,20},{20... | collective-permute-start | bytes 3538952 | tf_op jit(solution)/shard_map/ppermute | solution.py:285
  52.1 12.0 %collective-permute-start.10 = (bf16[64,768]{1,0:T(8,128)(2,1)S(1)}, bf16[64,768]{1,0:T(8,128)(2,1)S(1)}, u32[]{:S(2)}, u32[]{:S(2)}) collective-permute-start(bf16[64,768]{1,0:T(8,128)(2,1)S(1)} %pad_maximum_fusion.4), channel_id=1, source_target_pairs={{0,8},{8,0},{16,24},{24,16},{32,40},{40,32},{48,56},{56,48},{1,9},... | collective-permute-start | bytes 294920 | tf_op jit(solution)/shard_map/ppermute | solution.py:264
  56.4 1.0 copy-start.3
  68.7 1.3 copy-start.4
  74.4 10.8 %collective-permute-start.7 = (bf16[128,896]{1,0:T(8,128)(2,1)S(1)}, bf16[128,896]{1,0:T(8,128)(2,1)S(1)}, u32[]{:S(2)}, u32[]{:S(2)}) collective-permute-start(bf16[128,896]{1,0:T(8,128)(2,1)S(1)} %get-tuple-element.60), channel_id=1, source_target_pairs={{16,0},{17,1},{18,2},{19,3},{20,4},{21,5},{22,6},{23,7},{24,8},{25... | collective-permute-start | bytes 688136 | tf_op jit(solution)/shard_map/ppermute | solution.py:290
  75.7 9.5 %collective-permute-start.8 = (bf16[128,896]{1,0:T(8,128)(2,1)S(1)}, bf16[128,896]{1,0:T(8,128)(2,1)S(1)}, u32[]{:S(2)}, u32[]{:S(2)}) collective-permute-start(bf16[128,896]{1,0:T(8,128)(2,1)S(1)} %get-tuple-element.61), channel_id=1, source_target_pairs={{0,16},{1,17},{2,18},{3,19},{4,20},{5,21},{6,22},{7,23},{8,24},{9,... | collective-permute-start | bytes 688136 | tf_op jit(solution)/shard_map/ppermute | solution.py:291
  114.2 1.4 copy-start
  115.6 2.5 %copy-start.1 = (bf16[1024,768]{1,0:T(8,128)(2,1)S(1)}, bf16[1024,768]{1,0:T(8,128)(2,1)}, u32[]{:S(2)}) copy-start(bf16[1024,768]{1,0:T(8,128)(2,1)} %all-gather.2.cloned.1.call-done.weight) | copy-start | bytes 4718596
  116.2 3.8 %collective-permute-start.11 = (bf16[512,512]{1,0:T(8,128)(2,1)S(1)}, bf16[512,512]{1,0:T(8,128)(2,1)S(1)}, u32[]{:S(2)}, u32[]{:S(2)}) collective-permute-start(bf16[512,512]{1,0:T(8,128)(2,1)S(1)} %shard_map.69), channel_id=1, source_target_pairs={{0,1},{1,0},{2,3},{3,2},{4,5},{5,4},{6,7},{7,6},{8,9},{9,8},{10,11... | collective-permute-start | bytes 1572872 | tf_op jit(solution)/shard_map/ppermute | solution.py:296
  118.7 15.2 %copy-start.2 = (bf16[512,384]{1,0:T(8,128)(2,1)S(1)}, bf16[512,384]{1,0:T(8,128)(2,1)}, u32[]{:S(2)}) copy-start(bf16[512,384]{1,0:T(8,128)(2,1)} %constant.173.clone.order) | copy-start | bytes 1179652
Sparse Core Ops, SparseCore 0:
  65.0 49.1 all-gather.1

commit v4 on v3

--- a/solution.py
+++ b/solution.py
@@ -234,9 +234,8 @@
     order = np.zeros((4, 8, PAD, WIDE), np.float32)
     for x in range(4):
         for p in range(8):
-            y = (p & 1) * 4 + (p & 2) + (p >> 2)
             for j in range(SHARE):
-                order[x, p, j, (y * 4 + x) * SHARE + j] = 1
+                order[x, p, j, (p * 4 + x) * SHARE + j] = 1
     return order.reshape(4 * HD, WIDE)
 
 
@@ -256,15 +255,6 @@
         compiler_params=pltpu.CompilerParams(vmem_limit_bytes=12 * 1024 * 1024),
         cost_estimate=pl.CostEstimate(flops=2 * TILE * 4 * HD * 4 * WIDE, bytes_accessed=2**20, transcendentals=0),
     )(pieces, jnp.asarray(column_order(), jnp.bfloat16))
-
-
-def gathered_weight(part, bits):
-    y = lax.axis_index("y")
-    for bit in bits:
-        other = lax.ppermute(part, "y", [(i, i ^ bit) for i in range(8)])
-        upper = (y & bit) != 0
-        part = jnp.concatenate([jnp.where(upper, other, part), jnp.where(upper, part, other)])
-    return part
 
 
 def body(queries, keys, values, window, out_weight):
@@ -273,14 +263,14 @@
     kv = jnp.concatenate([keys, values])
     ap = lax.ppermute(kv, ALL, first_axis(1))
     am = lax.ppermute(kv, ALL, first_axis(-1))
-    part = gathered_weight(jnp.pad(out_weight.T, ((0, PAD - SHARE), (0, 0))), (4,))
+    part = jnp.pad(out_weight.T, ((0, PAD - SHARE), (0, 0)))
+    weight = lax.all_to_all(jnp.broadcast_to(part, (64, PAD, FEAT)), ("z", "y"), 0, 0).reshape(-1, FEAT)
     bias = biases(window, my_tile, core)
     q0 = with_biases(queries, bias[0])
     qp = lax.ppermute(with_biases(queries, bias[2]), ALL, row_axis(1))
     qm = lax.ppermute(with_biases(queries, bias[1]), ALL, row_axis(-1))
-    ap, am, qp, qm, part = lax.optimization_barrier((ap, am, qp, qm, part))
+    ap, am, qp, qm = lax.optimization_barrier((ap, am, qp, qm))
     line = jnp.concatenate([kv, ap, am])
-    weight = lax.all_gather(gathered_weight(part, (2, 1)), "z", tiled=True)
     bp = lax.ppermute(line, ALL, second_axis(1))
     bm = lax.ppermute(line, ALL, second_axis(-1))
     near = [(n, 0, 3 * n) for n in range(3)]

time: 143 us -> 139 us (0.972)
  the two profiles are of different devices: /device:TPU:8 before, /device:TPU:48 now
where the time goes in v4:
time: 139 us
  blocking collectives  59.2 us (43%)
  starting transfers between devices  42 us (30%)
  waiting for transfers between devices  18.5 us (13%)
  Pallas kernels  10.9 us (8%)
  local copies, waits for them, and re-layouts  6.27 us (5%)
    all_gather x1, blocking collectives, body(): rows = lax.all_gather(attended, 'x', tiled=True)  44.8 us
    all_to_all x1, starting transfers between devices, body(): lax.all_to_all(jnp.broadcast_to(part, (64, PAD, FEAT)), ('z', 'y'), 0, 0)  17.1 us
    all_to_all x1, blocking collectives, body(): pieces = lax.all_to_all(columns.reshape(4, TILE, -1), 'x', 0, 0)  14.4 us
    ppermute x1, waiting for transfers between devices, body(): bp = lax.ppermute(line, ALL, second_axis(1))  10.2 us
    pallas_call x3, Pallas kernels, attention(): pl.pallas_call(functools.partial(attention_kernel, groups, count, state i...  7.99 us
    ppermute x1, starting transfers between devices, body(): am = lax.ppermute(kv, ALL, first_axis(-1))  4.93 us
    ppermute x1, starting transfers between devices, body(): bm = lax.ppermute(line, ALL, second_axis(-1))  4.62 us
    ppermute x1, starting transfers between devices, body(): back_p = lax.ppermute(om, ALL, row_axis(1))  4.28 us
  transfers between devices with their start and end apart: 10, of which 5 were waited for; matrix products, arithmetic and copies ran while one was open for 3% of the time, Pallas kernels for 7%

profile of v4, /device:TPU:48, one launch (start us, length us, event | category | flops | bytes accessed | tf_op | source)
XLA Modules:
  0.0 138.5 jit_solution(18409023643186927655)
XLA Ops:
  0.0 0.0 copy-start.4
  0.0 0.0 copy-start.3
  0.0 0.0 copy-start.1
  0.0 0.0 copy-start.2
  0.0 1.7 %constant_dynamic-update-slice_fusion.1 = (bf16[256,768]{1,0:T(8,128)(2,1)S(1)}, bf16[768,768]{1,0:T(8,128)(2,1)}) fusion(bf16[128,768]{1,0:T(8,128)(2,1)} %param.13), kind=kLoop, calls=%fused_computation.6 | loop fusion | bytes 589824
  1.7 1.6 %constant_dynamic-update-slice_fusion = (bf16[256,768]{1,0:T(8,128)(2,1)S(1)}, bf16[768,768]{1,0:T(8,128)(2,1)}) fusion(bf16[256,768]{1,0:T(8,128)(2,1)S(1)} %get-tuple-element.66, bf16[128,768]{1,0:T(8,128)(2,1)} %param.14, bf16[768,768]{1,0:T(8,128)(2,1)} %get-tuple-element.67), kind=kLoop, calls=%fused_computation.5 | loop fusion | bytes 589824 | tf_op jit(solution)/shard_map/concatenate | solution.py:263
  3.3 1.3 collective-permute-start
  4.6 4.9 %collective-permute-start.1 = (bf16[256,768]{1,0:T(8,128)(2,1)S(1)}, bf16[256,768]{1,0:T(8,128)(2,1)S(1)}, u32[]{:S(2)}, u32[]{:S(2)}) collective-permute-start(bf16[256,768]{1,0:T(8,128)(2,1)S(1)} %get-tuple-element.64.refs_3_), channel_id=1, source_target_pairs={{1,3},{3,5},{5,7},{7,9},{9,11},{11,13},{13,15},{17,19},{19,21},{21... | collective-permute-start | bytes 1179656 | tf_op jit(solution)/shard_map/ppermute | solution.py:265
  9.7 0.0 copy-done.3
  9.7 0.2 compare_reduce_fusion
  9.9 0.1 fusion.4
  10.0 0.0 copy-done.4
  10.0 0.0 copy-done.1
  10.0 0.9 pad_maximum_fusion
  10.9 4.0 %collective-permute-start.2 = (bf16[144,768]{1,0:T(8,128)(2,1)}, bf16[144,768]{1,0:T(8,128)(2,1)S(1)}, u32[]{:S(2)}, u32[]{:S(2)}) collective-permute-start(bf16[144,768]{1,0:T(8,128)(2,1)} %get-tuple-element.62), channel_id=1, source_target_pairs={{16,0},{17,1},{18,2},{19,3},{20,4},{21,5},{22,6},{23,7},{24,8},{25... | collective-permute-start | bytes 663560 | tf_op jit(solution)/shard_map/ppermute | solution.py:270
  15.0 1.3 collective-permute-start.3
  16.3 0.0 copy-done.2
  16.3 1.3 broadcast_in_dim.46
  17.6 17.1 %all-to-all-start = ((bf16[64,16,768]{2,1,0:T(8,128)(2,1)}), bf16[64,16,768]{2,1,0:T(8,128)(2,1)S(1)}, u32[]{:S(2)}, u32[]{:S(2)}) async-start(bf16[64,16,768]{2,1,0:T(8,128)(2,1)} %broadcast_in_dim.46), calls=%async_computation | async-start | bytes 3145728 | tf_op jit(solution)/shard_map/all_to_all | solution.py:267
  34.6 0.0 collective-permute-done.2.refs_0_
  34.6 0.0 collective-permute-done.3.refs_1_
  34.7 0.0 collective-permute-done.refs_4_
  34.7 0.0 collective-permute-done.1.refs_5_
  34.7 0.8 constant_dynamic-update-slice_fusion.3
  35.4 0.8 constant_dynamic-update-slice_fusion.2
  36.2 1.3 collective-permute-start.4
  37.5 4.6 %collective-permute-start.5 = (bf16[768,768]{1,0:T(8,128)(2,1)}, bf16[768,768]{1,0:T(8,128)(2,1)S(1)}, u32[]{:S(2)}, u32[]{:S(2)}) collective-permute-start(bf16[768,768]{1,0:T(8,128)(2,1)} %constant_dynamic-update-slice_fusion.2), channel_id=1, source_target_pairs={{0,2},{2,4},{4,6},{6,8},{8,10},{10,12},{12,14},{16,18},{18,20},{20... | collective-permute-start | bytes 3538952 | tf_op jit(solution)/shard_map/ppermute | solution.py:275
  42.1 2.1 %shard_map.64 = (f32[384,768]{1,0:T(8,128)S(1)}, f32[384,128]{1,0:T(8,128)S(1)}) custom-call(bf16[144,768]{1,0:T(8,128)(2,1)S(1)} %collective-permute-done.2.refs_0_, bf16[144,768]{1,0:T(8,128)(2,1)S(1)} %collective-permute-done.3.refs_1_, bf16[144,768]{1,0:T(8,128)(2,1)S(1)} %get-tuple-element.63.refs_2_.refs_0_, ...), custom_call_target="tpu_custom_call" | custom-call | flops 18119393280 | bytes 1179648 | tf_op jit(solution)/shard_map/pallas_call | solution.py:155
  44.3 10.2 %collective-permute-done.4.refs_1_.refs_2_ = bf16[768,768]{1,0:T(8,128)(2,1)S(1)} collective-permute-done((bf16[768,768]{1,0:T(8,128)(2,1)}, bf16[768,768]{1,0:T(8,128)(2,1)S(1)}, u32[]{:S(2)}, u32[]{:S(2)}) %collective-permute-start.4) | collective-permute-done | bytes 1179680 | tf_op jit(solution)/shard_map/ppermute | solution.py:274
  54.5 1.6 %collective-permute-done.5.refs_2_.refs_3_ = bf16[768,768]{1,0:T(8,128)(2,1)S(1)} collective-permute-done((bf16[768,768]{1,0:T(8,128)(2,1)}, bf16[768,768]{1,0:T(8,128)(2,1)S(1)}, u32[]{:S(2)}, u32[]{:S(2)}) %collective-permute-start.5) | collective-permute-done | bytes 1179680 | tf_op jit(solution)/shard_map/ppermute | solution.py:275
  56.1 3.1 %shard_map.66 = (bf16[128,896]{1,0:T(8,128)(2,1)S(1)}, bf16[128,896]{1,0:T(8,128)(2,1)S(1)}) custom-call(bf16[144,768]{1,0:T(8,128)(2,1)S(1)} %collective-permute-done.2.refs_0_, bf16[144,768]{1,0:T(8,128)(2,1)S(1)} %collective-permute-done.3.refs_1_, bf16[768,768]{1,0:T(8,128)(2,1)S(1)} %collective-permute-done.4.refs_1_.refs_2_, ...), custom_call_target="tpu_custom_call" | custom-call | flops 24159191040 | bytes 2359296 | tf_op jit(solution)/shard_map/pallas_call | solution.py:155
  59.2 4.3 %collective-permute-start.6 = (bf16[128,896]{1,0:T(8,128)(2,1)S(1)}, bf16[128,896]{1,0:T(8,128)(2,1)S(1)}, u32[]{:S(2)}, u32[]{:S(2)}) collective-permute-start(bf16[128,896]{1,0:T(8,128)(2,1)S(1)} %get-tuple-element.59), channel_id=1, source_target_pairs={{16,0},{17,1},{18,2},{19,3},{20,4},{21,5},{22,6},{23,7},{24,8},{25... | collective-permute-start | bytes 688136 | tf_op jit(solution)/shard_map/ppermute | solution.py:280
  63.5 1.3 collective-permute-start.7
  64.8 2.7 %shard_map.65 = (f32[128,768]{1,0:T(8,128)S(1)}, f32[128,128]{1,0:T(8,128)S(1)}) custom-call(bf16[144,768]{1,0:T(8,128)(2,1)S(1)} %get-tuple-element.63.refs_2_.refs_0_, bf16[768,768]{1,0:T(8,128)(2,1)S(1)} %collective-permute-done.4.refs_1_.refs_2_, bf16[768,768]{1,0:T(8,128)(2,1)S(1)} %collective-permute-done.5.refs_2_.refs_3_, ...), custom_call_target="tpu_custom_call" | custom-call | flops 12079595520 | bytes 2359296 | tf_op jit(solution)/shard_map/pallas_call | solution.py:155
  67.5 2.7 %collective-permute-done.6.op = bf16[128,896]{1,0:T(8,128)(2,1)S(1)} collective-permute-done((bf16[128,896]{1,0:T(8,128)(2,1)S(1)}, bf16[128,896]{1,0:T(8,128)(2,1)S(1)}, u32[]{:S(2)}, u32[]{:S(2)}) %collective-permute-start.6) | collective-permute-done | bytes 229408 | tf_op jit(solution)/shard_map/ppermute | solution.py:280
  70.2 2.8 %collective-permute-done.7.om = bf16[128,896]{1,0:T(8,128)(2,1)S(1)} collective-permute-done((bf16[128,896]{1,0:T(8,128)(2,1)S(1)}, bf16[128,896]{1,0:T(8,128)(2,1)S(1)}, u32[]{:S(2)}, u32[]{:S(2)}) %collective-permute-start.7) | collective-permute-done | bytes 229408 | tf_op jit(solution)/shard_map/ppermute | solution.py:281
  73.0 0.5 shard_map.67
  73.5 44.8 %all_gather.3.rows = bf16[512,768]{1,0:T(8,128)(2,1)S(1)} all-gather(bf16[128,768]{1,0:T(8,128)(2,1)S(1)} %shard_map.67), channel_id=1, replica_groups=mesh['z'=8,'y'=8,'x'=4,'head'=2] {'x'}, dimensions={0}, use_global_device_ids=true | all-gather | bytes 983040 | tf_op jit(solution)/shard_map/all_gather | solution.py:284
  118.4 0.0 all-to-all-done
  118.4 0.6 shard_map.69
  119.0 1.9 %collective-permute-start.8 = (bf16[512,512]{1,0:T(8,128)(2,1)S(1)}, bf16[512,512]{1,0:T(8,128)(2,1)S(1)}, u32[]{:S(2)}, u32[]{:S(2)}) collective-permute-start(bf16[512,512]{1,0:T(8,128)(2,1)S(1)} %shard_map.69), channel_id=1, source_target_pairs={{0,1},{1,0},{2,3},{3,2},{4,5},{5,4},{6,7},{7,6},{8,9},{9,8},{10,11... | collective-permute-start | bytes 1572872 | tf_op jit(solution)/shard_map/ppermute | solution.py:286
  120.9 0.6 shard_map.68
  121.5 0.0 copy-start
  121.6 1.3 collective-permute-done.8
  122.8 0.2 add_convert_fusion
  123.0 14.4 %all_to_all.10.pieces = bf16[4,128,512]{2,1,0:T(8,128)(2,1)S(1)} all-to-all(bf16[4,128,512]{2,1,0:T(8,128)(2,1)S(1)} %bitcast.8), channel_id=1, replica_groups=mesh['z'=8,'y'=8,'x'=4,'head'=2] {'x'}, dimensions={0} | all-to-all | bytes 1048576 | tf_op jit(solution)/shard_map/all_to_all | solution.py:289
  137.3 0.0 copy-done
  137.3 1.2 shard_map.70
  (6 shorter events, 0.1 us)
Async XLA Ops:
  0.0 10.0 %copy-start.4 = (pred[16]{0:T(512)(128)(4,1)S(1)}, pred[16]{0:T(512)(128)(4,1)}, u32[]{:S(2)}) copy-start(pred[16]{0:T(512)(128)(4,1)} %constant.152.clone.1) | copy-start | bytes 52
  0.0 9.7 %copy-start.3 = (s32[1,27]{1,0:T(1,128)S(1)}, s32[1,27]{1,0:T(1,128)}, u32[]{:S(2)}) copy-start(s32[1,27]{1,0:T(1,128)} %param.15) | copy-start | bytes 328
  0.0 10.0 %copy-start.1 = (bf16[128,768]{1,0:T(8,128)(2,1)S(1)}, bf16[128,768]{1,0:T(8,128)(2,1)}, u32[]{:S(2)}) copy-start(bf16[128,768]{1,0:T(8,128)(2,1)} %param.12) | copy-start | bytes 589828
  0.0 16.3 %copy-start.2 = (bf16[768,12]{0,1:T(8,128)(2,1)S(1)}, bf16[768,12]{0,1:T(8,128)(2,1)}, u32[]{:S(2)}) copy-start(bf16[768,12]{0,1:T(8,128)(2,1)} %param.16) | copy-start | bytes 55300
  3.3 31.3 %collective-permute-start = (bf16[256,768]{1,0:T(8,128)(2,1)S(1)}, bf16[256,768]{1,0:T(8,128)(2,1)S(1)}, u32[]{:S(2)}, u32[]{:S(2)}) collective-permute-start(bf16[256,768]{1,0:T(8,128)(2,1)S(1)} %get-tuple-element.64.refs_3_), channel_id=1, source_target_pairs={{64,0},{3,1},{66,2},{5,3},{68,4},{7,5},{70,6},{9,7},{72,8},{11,9},... | collective-permute-start | bytes 1179656 | tf_op jit(solution)/shard_map/ppermute | solution.py:264
  4.6 30.0 %collective-permute-start.1 = (bf16[256,768]{1,0:T(8,128)(2,1)S(1)}, bf16[256,768]{1,0:T(8,128)(2,1)S(1)}, u32[]{:S(2)}, u32[]{:S(2)}) collective-permute-start(bf16[256,768]{1,0:T(8,128)(2,1)S(1)} %get-tuple-element.64.refs_3_), channel_id=1, source_target_pairs={{1,3},{3,5},{5,7},{7,9},{9,11},{11,13},{13,15},{17,19},{19,21},{21... | collective-permute-start | bytes 1179656 | tf_op jit(solution)/shard_map/ppermute | solution.py:265
  10.9 23.7 %collective-permute-start.2 = (bf16[144,768]{1,0:T(8,128)(2,1)}, bf16[144,768]{1,0:T(8,128)(2,1)S(1)}, u32[]{:S(2)}, u32[]{:S(2)}) collective-permute-start(bf16[144,768]{1,0:T(8,128)(2,1)} %get-tuple-element.62), channel_id=1, source_target_pairs={{16,0},{17,1},{18,2},{19,3},{20,4},{21,5},{22,6},{23,7},{24,8},{25... | collective-permute-start | bytes 663560 | tf_op jit(solution)/shard_map/ppermute | solution.py:270
  15.0 19.7 %collective-permute-start.3 = (bf16[144,768]{1,0:T(8,128)(2,1)}, bf16[144,768]{1,0:T(8,128)(2,1)S(1)}, u32[]{:S(2)}, u32[]{:S(2)}) collective-permute-start(bf16[144,768]{1,0:T(8,128)(2,1)} %get-tuple-element.61), channel_id=1, source_target_pairs={{0,16},{1,17},{2,18},{3,19},{4,20},{5,21},{6,22},{7,23},{8,24},{9,... | collective-permute-start | bytes 663560 | tf_op jit(solution)/shard_map/ppermute | solution.py:271
  17.6 100.8 %all-to-all-start = ((bf16[64,16,768]{2,1,0:T(8,128)(2,1)}), bf16[64,16,768]{2,1,0:T(8,128)(2,1)S(1)}, u32[]{:S(2)}, u32[]{:S(2)}) async-start(bf16[64,16,768]{2,1,0:T(8,128)(2,1)} %broadcast_in_dim.46), calls=%async_computation | async-start | bytes 3145728 | tf_op jit(solution)/shard_map/all_to_all | solution.py:267
  36.2 18.3 %collective-permute-start.4 = (bf16[768,768]{1,0:T(8,128)(2,1)}, bf16[768,768]{1,0:T(8,128)(2,1)S(1)}, u32[]{:S(2)}, u32[]{:S(2)}) collective-permute-start(bf16[768,768]{1,0:T(8,128)(2,1)} %constant_dynamic-update-slice_fusion.2), channel_id=1, source_target_pairs={{2,0},{65,1},{4,2},{67,3},{6,4},{69,5},{8,6},{71,7},{10,8},{73,9},... | collective-permute-start | bytes 3538952 | tf_op jit(solution)/shard_map/ppermute | solution.py:274
  37.5 18.6 %collective-permute-start.5 = (bf16[768,768]{1,0:T(8,128)(2,1)}, bf16[768,768]{1,0:T(8,128)(2,1)S(1)}, u32[]{:S(2)}, u32[]{:S(2)}) collective-permute-start(bf16[768,768]{1,0:T(8,128)(2,1)} %constant_dynamic-update-slice_fusion.2), channel_id=1, source_target_pairs={{0,2},{2,4},{4,6},{6,8},{8,10},{10,12},{12,14},{16,18},{18,20},{20... | collective-permute-start | bytes 3538952 | tf_op jit(solution)/shard_map/ppermute | solution.py:275
  59.2 11.0 %collective-permute-start.6 = (bf16[128,896]{1,0:T(8,128)(2,1)S(1)}, bf16[128,896]{1,0:T(8,128)(2,1)S(1)}, u32[]{:S(2)}, u32[]{:S(2)}) collective-permute-start(bf16[128,896]{1,0:T(8,128)(2,1)S(1)} %get-tuple-element.59), channel_id=1, source_target_pairs={{16,0},{17,1},{18,2},{19,3},{20,4},{21,5},{22,6},{23,7},{24,8},{25... | collective-permute-start | bytes 688136 | tf_op jit(solution)/shard_map/ppermute | solution.py:280
  63.5 9.5 %collective-permute-start.7 = (bf16[128,896]{1,0:T(8,128)(2,1)S(1)}, bf16[128,896]{1,0:T(8,128)(2,1)S(1)}, u32[]{:S(2)}, u32[]{:S(2)}) collective-permute-start(bf16[128,896]{1,0:T(8,128)(2,1)S(1)} %get-tuple-element.60), channel_id=1, source_target_pairs={{0,16},{1,17},{2,18},{3,19},{4,20},{5,21},{6,22},{7,23},{8,24},{9,... | collective-permute-start | bytes 688136 | tf_op jit(solution)/shard_map/ppermute | solution.py:281
  119.0 3.8 %collective-permute-start.8 = (bf16[512,512]{1,0:T(8,128)(2,1)S(1)}, bf16[512,512]{1,0:T(8,128)(2,1)S(1)}, u32[]{:S(2)}, u32[]{:S(2)}) collective-permute-start(bf16[512,512]{1,0:T(8,128)(2,1)S(1)} %shard_map.69), channel_id=1, source_target_pairs={{0,1},{1,0},{2,3},{3,2},{4,5},{5,4},{6,7},{7,6},{8,9},{9,8},{10,11... | collective-permute-start | bytes 1572872 | tf_op jit(solution)/shard_map/ppermute | solution.py:286
  121.5 15.8 %copy-start = (bf16[512,384]{1,0:T(8,128)(2,1)S(1)}, bf16[512,384]{1,0:T(8,128)(2,1)}, u32[]{:S(2)}) copy-start(bf16[512,384]{1,0:T(8,128)(2,1)} %constant.172.clone.order) | copy-start | bytes 1179652

commit v5 on v4

--- a/solution.py
+++ b/solution.py
@@ -167,6 +167,25 @@
     )(*operands)
 
 
+def stack_kernel(*refs):
+    low = 0
+    for ref in refs[:-1]:
+        refs[-1][low : low + ref.shape[0], :] = ref[...]
+        low += ref.shape[0]
+
+
+def stacked(*arrays):
+    rows = sum(a.shape[0] for a in arrays)
+    return pl.pallas_call(
+        stack_kernel,
+        out_shape=jax.ShapeDtypeStruct((rows, arrays[0].shape[1]), arrays[0].dtype),
+        in_specs=[VMEM] * len(arrays),
+        out_specs=VMEM,
+        compiler_params=pltpu.CompilerParams(vmem_limit_bytes=12 * 1024 * 1024),
+        cost_estimate=pl.CostEstimate(flops=0, bytes_accessed=4 * rows * FEAT, transcendentals=0),
+    )(*arrays)
+
+
 def merge_kernel(o0, s0, op, om, out):
     own = s0[...]
     peaks, totals, sums = [own], [pltpu.roll(own, HD - 8, 1)], [o0]
@@ -260,17 +279,18 @@
 def body(queries, keys, values, window, out_weight):
     my_tile = lax.axis_index(TOK)
     core = lax.axis_index("head")
-    kv = jnp.concatenate([keys, values])
+    kv = stacked(keys, values)
     ap = lax.ppermute(kv, ALL, first_axis(1))
     am = lax.ppermute(kv, ALL, first_axis(-1))
     part = jnp.pad(out_weight.T, ((0, PAD - SHARE), (0, 0)))
-    weight = lax.all_to_all(jnp.broadcast_to(part, (64, PAD, FEAT)), ("z", "y"), 0, 0).reshape(-1, FEAT)
+    line_y = lax.all_to_all(jnp.broadcast_to(part, (8, PAD, FEAT)), "y", 0, 0)
+    weight = lax.all_gather(line_y.reshape(-1, FEAT), "z", tiled=True)
     bias = biases(window, my_tile, core)
     q0 = with_biases(queries, bias[0])
     qp = lax.ppermute(with_biases(queries, bias[2]), ALL, row_axis(1))
     qm = lax.ppermute(with_biases(queries, bias[1]), ALL, row_axis(-1))
     ap, am, qp, qm = lax.optimization_barrier((ap, am, qp, qm))
-    line = jnp.concatenate([kv, ap, am])
+    line = stacked(kv, ap, am)
     bp = lax.ppermute(line, ALL, second_axis(1))
     bm = lax.ppermute(line, ALL, second_axis(-1))
     near = [(n, 0, 3 * n) for n in range(3)]

time: 139 us -> 134 us (0.964)
  the two profiles are of different devices: /device:TPU:48 before, /device:TPU:240 now
where the time goes in v5:
time: 134 us; the launch traced here: 133 us
  starting transfers between devices  44 us (33%)
  blocking collectives  29.7 us (22%)
  waiting for transfers between devices  28.5 us (21%)
  between operations  13.6 us (10%)
  Pallas kernels  11.1 us (8%)
  local copies, waits for them, and re-layouts  5.49 us (4%)
    all_gather x1, blocking collectives, body(): rows = lax.all_gather(attended, 'x', tiled=True)  15.7 us
    all_to_all x1, blocking collectives, body(): pieces = lax.all_to_all(columns.reshape(4, TILE, -1), 'x', 0, 0)  14 us
    ppermute x1, starting transfers between devices, body(): received = lax.ppermute(other, 'head', [(0, 1), (1, 0)])  13.1 us
    ppermute x1, waiting for transfers between devices, body(): bp = lax.ppermute(line, ALL, second_axis(1))  10 us
    pallas_call x3, Pallas kernels, attention(): pl.pallas_call(functools.partial(attention_kernel, groups, count, state i...  8.07 us
    all_to_all x1, starting transfers between devices, body(): line_y = lax.all_to_all(jnp.broadcast_to(part, (8, PAD, FEAT)), 'y', 0, 0)  6.98 us
    ppermute x1, waiting for transfers between devices, body(): qp = lax.ppermute(with_biases(queries, bias[2]), ALL, row_axis(1))  6.02 us
    ppermute x1, starting transfers between devices, body(): am = lax.ppermute(kv, ALL, first_axis(-1))  5.49 us
  transfers between devices with their start and end apart: 11, of which 6 were waited for; matrix products, arithmetic and copies ran while one was open for 1% of the time, Pallas kernels for 7%

profile of v5, /device:TPU:240, one launch (start us, length us, event | category | flops | bytes accessed | tf_op | source)
XLA Modules:
  0.0 133.0 jit_solution(15072720022044296846)
XLA Ops:
  6.5 0.0 copy-start.8
  6.5 0.0 copy-start.3
  6.5 0.9 copy-done.3
  7.5 0.0 copy-start.4
  7.5 0.9 copy-done.4
  8.4 0.0 copy-start.7
  8.4 0.0 copy-start.6
  8.4 2.1 %collective-permute-start = (bf16[256,768]{1,0:T(8,128)(2,1)S(1)}, bf16[256,768]{1,0:T(8,128)(2,1)S(1)}, u32[]{:S(2)}, u32[]{:S(2)}) collective-permute-start(bf16[256,768]{1,0:T(8,128)(2,1)S(1)} %shard_map.64.refs_0_.refs_3_), channel_id=1, source_target_pairs={{64,0},{3,1},{66,2},{5,3},{68,4},{7,5},{70,6},{9,7},{72,8},{11,9},... | collective-permute-start | bytes 1179656 | tf_op jit(solution)/shard_map/ppermute | solution.py:283
  10.5 5.5 %collective-permute-start.1 = (bf16[256,768]{1,0:T(8,128)(2,1)S(1)}, bf16[256,768]{1,0:T(8,128)(2,1)S(1)}, u32[]{:S(2)}, u32[]{:S(2)}) collective-permute-start(bf16[256,768]{1,0:T(8,128)(2,1)S(1)} %shard_map.64.refs_0_.refs_3_), channel_id=1, source_target_pairs={{1,3},{3,5},{5,7},{7,9},{9,11},{11,13},{13,15},{17,19},{19,21},{21... | collective-permute-start | bytes 1179656 | tf_op jit(solution)/shard_map/ppermute | solution.py:284
  16.0 0.7 pad.13
  16.7 0.7 broadcast_in_dim.46
  17.4 7.0 %all-to-all-start = ((bf16[8,16,768]{2,1,0:T(8,128)(2,1)}), bf16[8,16,768]{2,1,0:T(8,128)(2,1)S(1)}, u32[]{:S(2)}, u32[]{:S(2)}) async-start(bf16[8,16,768]{2,1,0:T(8,128)(2,1)} %broadcast_in_dim.46), calls=%async_computation | async-start | bytes 393216 | tf_op jit(solution)/shard_map/all_to_all | solution.py:286
  24.4 0.0 all-gather.2.cloned.1.call-start
  24.5 0.0 copy-done.7
  24.5 0.2 compare_reduce_fusion
  24.7 0.1 fusion.4
  24.8 0.0 copy-done.8
  24.8 0.0 copy-done.6
  24.8 0.1 pad_maximum_fusion
  25.0 4.3 %collective-permute-start.2 = (bf16[144,768]{1,0:T(8,128)(2,1)S(1)}, bf16[144,768]{1,0:T(8,128)(2,1)S(1)}, u32[]{:S(2)}, u32[]{:S(2)}) collective-permute-start(bf16[144,768]{1,0:T(8,128)(2,1)S(1)} %get-tuple-element.62), channel_id=1, source_target_pairs={{16,0},{17,1},{18,2},{19,3},{20,4},{21,5},{22,6},{23,7},{24,8},{25... | collective-permute-start | bytes 663560 | tf_op jit(solution)/shard_map/ppermute | solution.py:290
  29.3 1.3 collective-permute-start.3
  30.6 0.0 all-to-all-done
  30.6 0.0 copy-start.5
  30.6 0.7 copy-done.5
  31.3 0.0 all-gather.2.cloned.1.call-update
  31.3 6.0 %collective-permute-done.2.refs_0_ = bf16[144,768]{1,0:T(8,128)(2,1)S(1)} collective-permute-done((bf16[144,768]{1,0:T(8,128)(2,1)S(1)}, bf16[144,768]{1,0:T(8,128)(2,1)S(1)}, u32[]{:S(2)}, u32[]{:S(2)}) %collective-permute-start.2) | collective-permute-done | bytes 221216 | tf_op jit(solution)/shard_map/ppermute | solution.py:290
  37.3 5.3 %collective-permute-done.3.refs_1_ = bf16[144,768]{1,0:T(8,128)(2,1)S(1)} collective-permute-done((bf16[144,768]{1,0:T(8,128)(2,1)S(1)}, bf16[144,768]{1,0:T(8,128)(2,1)S(1)}, u32[]{:S(2)}, u32[]{:S(2)}) %collective-permute-start.3) | collective-permute-done | bytes 221216 | tf_op jit(solution)/shard_map/ppermute | solution.py:291
  42.6 0.0 collective-permute-done.refs_1_.refs_4_
  42.6 0.0 collective-permute-done.1.refs_2_.refs_5_
  42.6 0.1 shard_map.65
  42.7 1.3 collective-permute-start.4
  44.0 4.6 %collective-permute-start.5 = (bf16[768,768]{1,0:T(8,128)(2,1)S(1)}, bf16[768,768]{1,0:T(8,128)(2,1)S(1)}, u32[]{:S(2)}, u32[]{:S(2)}) collective-permute-start(bf16[768,768]{1,0:T(8,128)(2,1)S(1)} %shard_map.65), channel_id=1, source_target_pairs={{0,2},{2,4},{4,6},{6,8},{8,10},{10,12},{12,14},{16,18},{18,20},{20... | collective-permute-start | bytes 3538952 | tf_op jit(solution)/shard_map/ppermute | solution.py:295
  48.6 2.1 %shard_map.66 = (f32[384,768]{1,0:T(8,128)S(1)}, f32[384,128]{1,0:T(8,128)S(1)}) custom-call(bf16[144,768]{1,0:T(8,128)(2,1)S(1)} %collective-permute-done.2.refs_0_, bf16[144,768]{1,0:T(8,128)(2,1)S(1)} %collective-permute-done.3.refs_1_, bf16[144,768]{1,0:T(8,128)(2,1)S(1)} %get-tuple-element.63.refs_2_.refs_0_, ...), custom_call_target="tpu_custom_call" | custom-call | flops 18119393280 | bytes 1179648 | tf_op jit(solution)/shard_map/pallas_call | solution.py:155
  50.8 10.0 %collective-permute-done.4.refs_1_.refs_2_ = bf16[768,768]{1,0:T(8,128)(2,1)S(1)} collective-permute-done((bf16[768,768]{1,0:T(8,128)(2,1)S(1)}, bf16[768,768]{1,0:T(8,128)(2,1)S(1)}, u32[]{:S(2)}, u32[]{:S(2)}) %collective-permute-start.4) | collective-permute-done | bytes 1179680 | tf_op jit(solution)/shard_map/ppermute | solution.py:294
  60.8 1.5 %collective-permute-done.5.refs_2_.refs_3_ = bf16[768,768]{1,0:T(8,128)(2,1)S(1)} collective-permute-done((bf16[768,768]{1,0:T(8,128)(2,1)S(1)}, bf16[768,768]{1,0:T(8,128)(2,1)S(1)}, u32[]{:S(2)}, u32[]{:S(2)}) %collective-permute-start.5) | collective-permute-done | bytes 1179680 | tf_op jit(solution)/shard_map/ppermute | solution.py:295
  62.3 3.2 %shard_map.68 = (bf16[128,896]{1,0:T(8,128)(2,1)S(1)}, bf16[128,896]{1,0:T(8,128)(2,1)S(1)}) custom-call(bf16[144,768]{1,0:T(8,128)(2,1)S(1)} %collective-permute-done.2.refs_0_, bf16[144,768]{1,0:T(8,128)(2,1)S(1)} %collective-permute-done.3.refs_1_, bf16[768,768]{1,0:T(8,128)(2,1)S(1)} %collective-permute-done.4.refs_1_.refs_2_, ...), custom_call_target="tpu_custom_call" | custom-call | flops 24159191040 | bytes 2359296 | tf_op jit(solution)/shard_map/pallas_call | solution.py:155
  65.4 3.6 %collective-permute-start.6 = (bf16[128,896]{1,0:T(8,128)(2,1)S(1)}, bf16[128,896]{1,0:T(8,128)(2,1)S(1)}, u32[]{:S(2)}, u32[]{:S(2)}) collective-permute-start(bf16[128,896]{1,0:T(8,128)(2,1)S(1)} %get-tuple-element.59), channel_id=1, source_target_pairs={{16,0},{17,1},{18,2},{19,3},{20,4},{21,5},{22,6},{23,7},{24,8},{25... | collective-permute-start | bytes 688136 | tf_op jit(solution)/shard_map/ppermute | solution.py:300
  69.1 1.3 collective-permute-start.7
  70.4 2.8 %shard_map.67 = (f32[128,768]{1,0:T(8,128)S(1)}, f32[128,128]{1,0:T(8,128)S(1)}) custom-call(bf16[144,768]{1,0:T(8,128)(2,1)S(1)} %get-tuple-element.63.refs_2_.refs_0_, bf16[768,768]{1,0:T(8,128)(2,1)S(1)} %collective-permute-done.4.refs_1_.refs_2_, bf16[768,768]{1,0:T(8,128)(2,1)S(1)} %collective-permute-done.5.refs_2_.refs_3_, ...), custom_call_target="tpu_custom_call" | custom-call | flops 12079595520 | bytes 2359296 | tf_op jit(solution)/shard_map/pallas_call | solution.py:155
  73.1 0.0 collective-permute-done.6.op
  73.1 4.7 %collective-permute-done.7.om = bf16[128,896]{1,0:T(8,128)(2,1)S(1)} collective-permute-done((bf16[128,896]{1,0:T(8,128)(2,1)S(1)}, bf16[128,896]{1,0:T(8,128)(2,1)S(1)}, u32[]{:S(2)}, u32[]{:S(2)}) %collective-permute-start.7) | collective-permute-done | bytes 229408 | tf_op jit(solution)/shard_map/ppermute | solution.py:301
  77.9 0.5 shard_map.69
  78.4 15.7 %all_gather.6.rows = bf16[512,768]{1,0:T(8,128)(2,1)S(1)} all-gather(bf16[128,768]{1,0:T(8,128)(2,1)S(1)} %shard_map.69), channel_id=1, replica_groups=mesh['z'=8,'y'=8,'x'=4,'head'=2] {'x'}, dimensions={0}, use_global_device_ids=true | all-gather | bytes 983040 | tf_op jit(solution)/shard_map/all_gather | solution.py:304
  94.1 0.0 all-gather.2.cloned.1.call-done.weight
  94.1 0.0 copy-start
  94.1 1.4 %copy-done = bf16[1024,768]{1,0:T(8,128)(2,1)S(1)} copy-done((bf16[1024,768]{1,0:T(8,128)(2,1)S(1)}, bf16[1024,768]{1,0:T(8,128)(2,1)}, u32[]{:S(2)}) %copy-start) | copy-done | bytes 1572888
  95.5 0.0 copy-start.1
  95.5 0.6 shard_map.71
  96.2 13.1 %collective-permute-start.8 = (bf16[512,512]{1,0:T(8,128)(2,1)S(1)}, bf16[512,512]{1,0:T(8,128)(2,1)S(1)}, u32[]{:S(2)}, u32[]{:S(2)}) collective-permute-start(bf16[512,512]{1,0:T(8,128)(2,1)S(1)} %shard_map.71), channel_id=1, source_target_pairs={{0,1},{1,0},{2,3},{3,2},{4,5},{5,4},{6,7},{7,6},{8,9},{9,8},{10,11... | collective-permute-start | bytes 1572872 | tf_op jit(solution)/shard_map/ppermute | solution.py:306
  109.2 0.0 copy-done.1
  109.2 0.6 shard_map.70
  109.9 0.0 copy-start.2
  109.9 0.9 collective-permute-done.8
  110.8 0.2 add_convert_fusion
  110.9 14.0 %all_to_all.10.pieces = bf16[4,128,512]{2,1,0:T(8,128)(2,1)S(1)} all-to-all(bf16[4,128,512]{2,1,0:T(8,128)(2,1)S(1)} %bitcast.6), channel_id=1, replica_groups=mesh['z'=8,'y'=8,'x'=4,'head'=2] {'x'}, dimensions={0} | all-to-all | bytes 1048576 | tf_op jit(solution)/shard_map/all_to_all | solution.py:309
  124.9 0.0 copy-done.2
  124.9 1.2 shard_map.72
  (6 shorter events, 0.1 us)
Async XLA Ops:
  6.5 18.2 %copy-start.8 = (pred[16]{0:T(512)(128)(4,1)S(1)}, pred[16]{0:T(512)(128)(4,1)}, u32[]{:S(2)}) copy-start(pred[16]{0:T(512)(128)(4,1)} %constant.152.clone.1) | copy-start | bytes 52
  6.5 0.9 copy-start.3
  7.5 0.9 copy-start.4
  8.4 16.1 %copy-start.7 = (s32[1,27]{1,0:T(1,128)S(1)}, s32[1,27]{1,0:T(1,128)}, u32[]{:S(2)}) copy-start(s32[1,27]{1,0:T(1,128)} %param.15) | copy-start | bytes 328
  8.4 16.4 %copy-start.6 = (bf16[128,768]{1,0:T(8,128)(2,1)S(1)}, bf16[128,768]{1,0:T(8,128)(2,1)}, u32[]{:S(2)}) copy-start(bf16[128,768]{1,0:T(8,128)(2,1)} %param.12) | copy-start | bytes 589828
  8.4 34.2 %collective-permute-start = (bf16[256,768]{1,0:T(8,128)(2,1)S(1)}, bf16[256,768]{1,0:T(8,128)(2,1)S(1)}, u32[]{:S(2)}, u32[]{:S(2)}) collective-permute-start(bf16[256,768]{1,0:T(8,128)(2,1)S(1)} %shard_map.64.refs_0_.refs_3_), channel_id=1, source_target_pairs={{64,0},{3,1},{66,2},{5,3},{68,4},{7,5},{70,6},{9,7},{72,8},{11,9},... | collective-permute-start | bytes 1179656 | tf_op jit(solution)/shard_map/ppermute | solution.py:283
  10.5 32.1 %collective-permute-start.1 = (bf16[256,768]{1,0:T(8,128)(2,1)S(1)}, bf16[256,768]{1,0:T(8,128)(2,1)S(1)}, u32[]{:S(2)}, u32[]{:S(2)}) collective-permute-start(bf16[256,768]{1,0:T(8,128)(2,1)S(1)} %shard_map.64.refs_0_.refs_3_), channel_id=1, source_target_pairs={{1,3},{3,5},{5,7},{7,9},{9,11},{11,13},{13,15},{17,19},{19,21},{21... | collective-permute-start | bytes 1179656 | tf_op jit(solution)/shard_map/ppermute | solution.py:284
  17.4 13.1 %all-to-all-start = ((bf16[8,16,768]{2,1,0:T(8,128)(2,1)}), bf16[8,16,768]{2,1,0:T(8,128)(2,1)S(1)}, u32[]{:S(2)}, u32[]{:S(2)}) async-start(bf16[8,16,768]{2,1,0:T(8,128)(2,1)} %broadcast_in_dim.46), calls=%async_computation | async-start | bytes 393216 | tf_op jit(solution)/shard_map/all_to_all | solution.py:286
  24.4 69.7 %all-gather.2.cloned.1.call-start = ((), (), s32[]{:S(2)}) async-start(), calls=%async_computation.2 | async-start | bytes 1769472 | tf_op jit(solution)/shard_map/all_gather | solution.py:287
  25.0 12.3 %collective-permute-start.2 = (bf16[144,768]{1,0:T(8,128)(2,1)S(1)}, bf16[144,768]{1,0:T(8,128)(2,1)S(1)}, u32[]{:S(2)}, u32[]{:S(2)}) collective-permute-start(bf16[144,768]{1,0:T(8,128)(2,1)S(1)} %get-tuple-element.62), channel_id=1, source_target_pairs={{16,0},{17,1},{18,2},{19,3},{20,4},{21,5},{22,6},{23,7},{24,8},{25... | collective-permute-start | bytes 663560 | tf_op jit(solution)/shard_map/ppermute | solution.py:290
  29.3 13.4 %collective-permute-start.3 = (bf16[144,768]{1,0:T(8,128)(2,1)S(1)}, bf16[144,768]{1,0:T(8,128)(2,1)S(1)}, u32[]{:S(2)}, u32[]{:S(2)}) collective-permute-start(bf16[144,768]{1,0:T(8,128)(2,1)S(1)} %get-tuple-element.61), channel_id=1, source_target_pairs={{0,16},{1,17},{2,18},{3,19},{4,20},{5,21},{6,22},{7,23},{8,24},{9,... | collective-permute-start | bytes 663560 | tf_op jit(solution)/shard_map/ppermute | solution.py:291
  30.6 0.7 copy-start.5
  42.7 18.1 %collective-permute-start.4 = (bf16[768,768]{1,0:T(8,128)(2,1)S(1)}, bf16[768,768]{1,0:T(8,128)(2,1)S(1)}, u32[]{:S(2)}, u32[]{:S(2)}) collective-permute-start(bf16[768,768]{1,0:T(8,128)(2,1)S(1)} %shard_map.65), channel_id=1, source_target_pairs={{2,0},{65,1},{4,2},{67,3},{6,4},{69,5},{8,6},{71,7},{10,8},{73,9},... | collective-permute-start | bytes 3538952 | tf_op jit(solution)/shard_map/ppermute | solution.py:294
  44.0 18.3 %collective-permute-start.5 = (bf16[768,768]{1,0:T(8,128)(2,1)S(1)}, bf16[768,768]{1,0:T(8,128)(2,1)S(1)}, u32[]{:S(2)}, u32[]{:S(2)}) collective-permute-start(bf16[768,768]{1,0:T(8,128)(2,1)S(1)} %shard_map.65), channel_id=1, source_target_pairs={{0,2},{2,4},{4,6},{6,8},{8,10},{10,12},{12,14},{16,18},{18,20},{20... | collective-permute-start | bytes 3538952 | tf_op jit(solution)/shard_map/ppermute | solution.py:295
  65.4 7.7 %collective-permute-start.6 = (bf16[128,896]{1,0:T(8,128)(2,1)S(1)}, bf16[128,896]{1,0:T(8,128)(2,1)S(1)}, u32[]{:S(2)}, u32[]{:S(2)}) collective-permute-start(bf16[128,896]{1,0:T(8,128)(2,1)S(1)} %get-tuple-element.59), channel_id=1, source_target_pairs={{16,0},{17,1},{18,2},{19,3},{20,4},{21,5},{22,6},{23,7},{24,8},{25... | collective-permute-start | bytes 688136 | tf_op jit(solution)/shard_map/ppermute | solution.py:300
  69.1 8.8 %collective-permute-start.7 = (bf16[128,896]{1,0:T(8,128)(2,1)S(1)}, bf16[128,896]{1,0:T(8,128)(2,1)S(1)}, u32[]{:S(2)}, u32[]{:S(2)}) collective-permute-start(bf16[128,896]{1,0:T(8,128)(2,1)S(1)} %get-tuple-element.60), channel_id=1, source_target_pairs={{0,16},{1,17},{2,18},{3,19},{4,20},{5,21},{6,22},{7,23},{8,24},{9,... | collective-permute-start | bytes 688136 | tf_op jit(solution)/shard_map/ppermute | solution.py:301
  94.1 1.4 %copy-start = (bf16[1024,768]{1,0:T(8,128)(2,1)S(1)}, bf16[1024,768]{1,0:T(8,128)(2,1)}, u32[]{:S(2)}) copy-start(bf16[1024,768]{1,0:T(8,128)(2,1)} %all-gather.2.cloned.1.call-done.weight) | copy-start | bytes 4718596
  95.5 13.7 %copy-start.1 = (bf16[1024,768]{1,0:T(8,128)(2,1)S(1)}, bf16[1024,768]{1,0:T(8,128)(2,1)}, u32[]{:S(2)}) copy-start(bf16[1024,768]{1,0:T(8,128)(2,1)} %all-gather.2.cloned.1.call-done.weight) | copy-start | bytes 4718596
  96.2 14.6 %collective-permute-start.8 = (bf16[512,512]{1,0:T(8,128)(2,1)S(1)}, bf16[512,512]{1,0:T(8,128)(2,1)S(1)}, u32[]{:S(2)}, u32[]{:S(2)}) collective-permute-start(bf16[512,512]{1,0:T(8,128)(2,1)S(1)} %shard_map.71), channel_id=1, source_target_pairs={{0,1},{1,0},{2,3},{3,2},{4,5},{5,4},{6,7},{7,6},{8,9},{9,8},{10,11... | collective-permute-start | bytes 1572872 | tf_op jit(solution)/shard_map/ppermute | solution.py:306
  109.9 15.1 %copy-start.2 = (bf16[512,384]{1,0:T(8,128)(2,1)S(1)}, bf16[512,384]{1,0:T(8,128)(2,1)}, u32[]{:S(2)}) copy-start(bf16[512,384]{1,0:T(8,128)(2,1)} %constant.172.clone.order) | copy-start | bytes 1179652
Sparse Core Ops, SparseCore 0:
  31.4 46.8 all-gather.1

commit v6 on v5

--- a/solution.py
+++ b/solution.py
@@ -160,28 +160,35 @@
         out_specs=(VMEM,) * len(out_shape),
         compiler_params=pltpu.CompilerParams(vmem_limit_bytes=12 * 1024 * 1024),
         cost_estimate=pl.CostEstimate(
-            flops=160 * pairs * TILE * TILE * FEAT,
+            flops=60 * pairs * TILE * TILE * FEAT,
             bytes_accessed=len(groups) * 4 * TILE * FEAT,
             transcendentals=pairs * TILE * TILE * HEADS,
         ),
     )(*operands)
 
 
-def stack_kernel(*refs):
+def stack_kernel(count, *refs):
+    arrays, (out, done) = refs[:count], refs[count:]
+    copies = []
     low = 0
-    for ref in refs[:-1]:
-        refs[-1][low : low + ref.shape[0], :] = ref[...]
+    for n, ref in enumerate(arrays):
+        copies.append(pltpu.make_async_copy(ref, out.at[pl.ds(low, ref.shape[0])], done.at[n]))
+        copies[-1].start()
         low += ref.shape[0]
+    for copy in copies:
+        copy.wait()
 
 
 def stacked(*arrays):
     rows = sum(a.shape[0] for a in arrays)
-    return pl.pallas_call(
-        stack_kernel,
+    anywhere = pl.BlockSpec(memory_space=pltpu.HBM if arrays[0].shape[0] == TILE else pl.ANY)
+    return pl.pallas_call(
+        functools.partial(stack_kernel, len(arrays)),
         out_shape=jax.ShapeDtypeStruct((rows, arrays[0].shape[1]), arrays[0].dtype),
-        in_specs=[VMEM] * len(arrays),
-        out_specs=VMEM,
-        compiler_params=pltpu.CompilerParams(vmem_limit_bytes=12 * 1024 * 1024),
+        in_specs=[anywhere] * len(arrays),
+        out_specs=pl.BlockSpec(memory_space=pl.ANY),
+        scratch_shapes=[pltpu.SemaphoreType.DMA((len(arrays),))],
+        compiler_params=pltpu.CompilerParams(vmem_limit_bytes=2**20),
         cost_estimate=pl.CostEstimate(flops=0, bytes_accessed=4 * rows * FEAT, transcendentals=0),
     )(*arrays)
 
@@ -289,7 +296,6 @@
     q0 = with_biases(queries, bias[0])
     qp = lax.ppermute(with_biases(queries, bias[2]), ALL, row_axis(1))
     qm = lax.ppermute(with_biases(queries, bias[1]), ALL, row_axis(-1))
-    ap, am, qp, qm = lax.optimization_barrier((ap, am, qp, qm))
     line = stacked(kv, ap, am)
     bp = lax.ppermute(line, ALL, second_axis(1))
     bm = lax.ppermute(line, ALL, second_axis(-1))

time: 134 us -> 131 us (0.978)
  the two profiles are of different devices: /device:TPU:240 before, /device:TPU:224 now
where the time goes in v6:
time: 131 us
  blocking collectives  40.2 us (31%)
  starting transfers between devices  36.9 us (28%)
  waiting for transfers between devices  18.4 us (14%)
  Pallas kernels  15.3 us (12%)
  between operations  13.7 us (10%)
  local copies, waits for them, and re-layouts  5.5 us (4%)
    all_gather x1, blocking collectives, body(): rows = lax.all_gather(attended, 'x', tiled=True)  26.1 us
    all_to_all x1, blocking collectives, body(): pieces = lax.all_to_all(columns.reshape(4, TILE, -1), 'x', 0, 0)  14 us
    pallas_call x3, Pallas kernels, attention(): pl.pallas_call(functools.partial(attention_kernel, groups, count, state i...  11.3 us
    all_to_all x1, starting transfers between devices, body(): line_y = lax.all_to_all(jnp.broadcast_to(part, (8, PAD, FEAT)), 'y', 0, 0)  7.21 us
    ppermute x1, starting transfers between devices, body(): bm = lax.ppermute(line, ALL, second_axis(-1))  5.58 us
    ppermute x1, starting transfers between devices, body(): am = lax.ppermute(kv, ALL, first_axis(-1))  5.49 us
    ppermute x1, waiting for transfers between devices, body(): qp = lax.ppermute(with_biases(queries, bias[2]), ALL, row_axis(1))  5.32 us
    ppermute x1, starting transfers between devices, body(): qp = lax.ppermute(with_biases(queries, bias[2]), ALL, row_axis(1))  4.68 us
  transfers between devices with their start and end apart: 11, of which 6 were waited for; matrix products, arithmetic and copies ran while one was open for 1% of the time, Pallas kernels for 10%

profile of v6, /device:TPU:224, one launch (start us, length us, event | category | flops | bytes accessed | tf_op | source)
XLA Modules:
  0.0 130.6 jit_solution(11174139878157509302)
XLA Ops:
  6.5 0.0 copy-start.8
  6.5 0.0 copy-start.3
  6.5 0.9 copy-done.3
  7.5 0.0 copy-start.4
  7.5 0.9 copy-done.4
  8.4 0.0 copy-start.7
  8.4 0.5 shard_map.64.refs_0_.refs_3_
  8.9 1.9 %collective-permute-start = (bf16[256,768]{1,0:T(8,128)(2,1)S(1)}, bf16[256,768]{1,0:T(8,128)(2,1)S(1)}, u32[]{:S(2)}, u32[]{:S(2)}) collective-permute-start(bf16[256,768]{1,0:T(8,128)(2,1)S(1)} %shard_map.64.refs_0_.refs_3_), channel_id=1, source_target_pairs={{64,0},{3,1},{66,2},{5,3},{68,4},{7,5},{70,6},{9,7},{72,8},{11,9},... | collective-permute-start | bytes 1179656 | tf_op jit(solution)/shard_map/ppermute | solution.py:290
  10.8 5.5 %collective-permute-start.1 = (bf16[256,768]{1,0:T(8,128)(2,1)S(1)}, bf16[256,768]{1,0:T(8,128)(2,1)S(1)}, u32[]{:S(2)}, u32[]{:S(2)}) collective-permute-start(bf16[256,768]{1,0:T(8,128)(2,1)S(1)} %shard_map.64.refs_0_.refs_3_), channel_id=1, source_target_pairs={{1,3},{3,5},{5,7},{7,9},{9,11},{11,13},{13,15},{17,19},{19,21},{21... | collective-permute-start | bytes 1179656 | tf_op jit(solution)/shard_map/ppermute | solution.py:291
  16.3 0.7 pad.13
  17.1 0.7 broadcast_in_dim.46
  17.8 7.2 %all-to-all-start = ((bf16[8,16,768]{2,1,0:T(8,128)(2,1)}), bf16[8,16,768]{2,1,0:T(8,128)(2,1)S(1)}, u32[]{:S(2)}, u32[]{:S(2)}) async-start(bf16[8,16,768]{2,1,0:T(8,128)(2,1)} %broadcast_in_dim.46), calls=%async_computation | async-start | bytes 393216 | tf_op jit(solution)/shard_map/all_to_all | solution.py:293
  25.0 0.0 all-gather.2.cloned.1.call-start
  25.0 0.0 copy-done.7
  25.0 0.2 compare_reduce_fusion
  25.3 0.0 copy-done.8
  25.3 0.1 fusion.4
  25.4 4.0 %all-to-all-done = bf16[8,16,768]{2,1,0:T(8,128)(2,1)S(1)} async-done(((bf16[8,16,768]{2,1,0:T(8,128)(2,1)}), bf16[8,16,768]{2,1,0:T(8,128)(2,1)S(1)}, u32[]{:S(2)}, u32[]{:S(2)}) %all-to-all-start) | async-done | bytes 196640 | tf_op jit(solution)/shard_map/all_to_all | solution.py:293
  29.4 0.0 copy-start.5
  29.4 0.7 copy-done.5
  30.1 0.0 all-gather.2.cloned.1.call-update
  30.1 0.0 copy-start.6
  30.1 0.0 collective-permute-done.refs_1_.refs_4_
  30.1 0.0 collective-permute-done.1.refs_2_.refs_5_
  30.1 0.6 shard_map.65
  30.7 1.3 collective-permute-start.2
  32.0 5.6 %collective-permute-start.3 = (bf16[768,768]{1,0:T(8,128)(2,1)S(1)}, bf16[768,768]{1,0:T(8,128)(2,1)}, u32[]{:S(2)}, u32[]{:S(2)}) collective-permute-start(bf16[768,768]{1,0:T(8,128)(2,1)S(1)} %shard_map.65), channel_id=1, source_target_pairs={{0,2},{2,4},{4,6},{6,8},{8,10},{10,12},{12,14},{16,18},{18,20},{20... | collective-permute-start | bytes 3538952 | tf_op jit(solution)/shard_map/ppermute | solution.py:301
  37.6 0.0 copy-done.6
  37.6 0.1 pad_maximum_fusion
  37.8 4.7 %collective-permute-start.4 = (bf16[144,768]{1,0:T(8,128)(2,1)S(1)}, bf16[144,768]{1,0:T(8,128)(2,1)S(1)}, u32[]{:S(2)}, u32[]{:S(2)}) collective-permute-start(bf16[144,768]{1,0:T(8,128)(2,1)S(1)} %get-tuple-element.54), channel_id=1, source_target_pairs={{16,0},{17,1},{18,2},{19,3},{20,4},{21,5},{22,6},{23,7},{24,8},{25... | collective-permute-start | bytes 663560 | tf_op jit(solution)/shard_map/ppermute | solution.py:297
  42.5 2.1 %collective-permute-start.5 = (bf16[144,768]{1,0:T(8,128)(2,1)S(1)}, bf16[144,768]{1,0:T(8,128)(2,1)S(1)}, u32[]{:S(2)}, u32[]{:S(2)}) collective-permute-start(bf16[144,768]{1,0:T(8,128)(2,1)S(1)} %get-tuple-element.53), channel_id=1, source_target_pairs={{0,16},{1,17},{2,18},{3,19},{4,20},{5,21},{6,22},{7,23},{8,24},{9,... | collective-permute-start | bytes 663560 | tf_op jit(solution)/shard_map/ppermute | solution.py:298
  44.5 5.3 %collective-permute-done.4.refs_0_ = bf16[144,768]{1,0:T(8,128)(2,1)S(1)} collective-permute-done((bf16[144,768]{1,0:T(8,128)(2,1)S(1)}, bf16[144,768]{1,0:T(8,128)(2,1)S(1)}, u32[]{:S(2)}, u32[]{:S(2)}) %collective-permute-start.4) | collective-permute-done | bytes 221216 | tf_op jit(solution)/shard_map/ppermute | solution.py:297
  49.9 3.6 %collective-permute-done.5.refs_1_ = bf16[144,768]{1,0:T(8,128)(2,1)S(1)} collective-permute-done((bf16[144,768]{1,0:T(8,128)(2,1)S(1)}, bf16[144,768]{1,0:T(8,128)(2,1)S(1)}, u32[]{:S(2)}, u32[]{:S(2)}) %collective-permute-start.5) | collective-permute-done | bytes 221216 | tf_op jit(solution)/shard_map/ppermute | solution.py:298
  53.4 2.1 %shard_map.66 = (f32[384,768]{1,0:T(8,128)S(1)}, f32[384,128]{1,0:T(8,128)S(1)}) custom-call(bf16[144,768]{1,0:T(8,128)(2,1)S(1)} %collective-permute-done.4.refs_0_, bf16[144,768]{1,0:T(8,128)(2,1)S(1)} %collective-permute-done.5.refs_1_, bf16[144,768]{1,0:T(8,128)(2,1)S(1)} %get-tuple-element.55.refs_2_.refs_0_, ...), custom_call_target="tpu_custom_call" | custom-call | flops 6794772480 | bytes 1179648 | tf_op jit(solution)/shard_map/pallas_call | solution.py:155
  55.6 0.0 collective-permute-done.2.refs_1_.refs_2_
  55.6 0.0 collective-permute-done.3.refs_2_.refs_3_
  55.6 4.8 %shard_map.68 = (bf16[128,896]{1,0:T(8,128)(2,1)S(1)}, bf16[128,896]{1,0:T(8,128)(2,1)S(1)}) custom-call(bf16[144,768]{1,0:T(8,128)(2,1)S(1)} %collective-permute-done.4.refs_0_, bf16[144,768]{1,0:T(8,128)(2,1)S(1)} %collective-permute-done.5.refs_1_, bf16[768,768]{1,0:T(8,128)(2,1)} %collective-permute-done.2.refs_1_.refs_2_, ...), custom_call_target="tpu_custom_call" | custom-call | flops 9059696640 | bytes 2359296 | tf_op jit(solution)/shard_map/pallas_call | solution.py:155
  60.4 2.8 %collective-permute-start.6 = (bf16[128,896]{1,0:T(8,128)(2,1)S(1)}, bf16[128,896]{1,0:T(8,128)(2,1)S(1)}, u32[]{:S(2)}, u32[]{:S(2)}) collective-permute-start(bf16[128,896]{1,0:T(8,128)(2,1)S(1)} %get-tuple-element.51), channel_id=1, source_target_pairs={{16,0},{17,1},{18,2},{19,3},{20,4},{21,5},{22,6},{23,7},{24,8},{25... | collective-permute-start | bytes 688136 | tf_op jit(solution)/shard_map/ppermute | solution.py:306
  63.3 3.9 %collective-permute-start.7 = (bf16[128,896]{1,0:T(8,128)(2,1)S(1)}, bf16[128,896]{1,0:T(8,128)(2,1)S(1)}, u32[]{:S(2)}, u32[]{:S(2)}) collective-permute-start(bf16[128,896]{1,0:T(8,128)(2,1)S(1)} %get-tuple-element.52), channel_id=1, source_target_pairs={{0,16},{1,17},{2,18},{3,19},{4,20},{5,21},{6,22},{7,23},{8,24},{9,... | collective-permute-start | bytes 688136 | tf_op jit(solution)/shard_map/ppermute | solution.py:307
  67.2 4.4 %shard_map.67 = (f32[128,768]{1,0:T(8,128)S(1)}, f32[128,128]{1,0:T(8,128)S(1)}) custom-call(bf16[144,768]{1,0:T(8,128)(2,1)S(1)} %get-tuple-element.55.refs_2_.refs_0_, bf16[768,768]{1,0:T(8,128)(2,1)} %collective-permute-done.2.refs_1_.refs_2_, bf16[768,768]{1,0:T(8,128)(2,1)} %collective-permute-done.3.refs_2_.refs_3_, ...), custom_call_target="tpu_custom_call" | custom-call | flops 4529848320 | bytes 2359296 | tf_op jit(solution)/shard_map/pallas_call | solution.py:155
  71.6 2.1 %collective-permute-done.6.op = bf16[128,896]{1,0:T(8,128)(2,1)S(1)} collective-permute-done((bf16[128,896]{1,0:T(8,128)(2,1)S(1)}, bf16[128,896]{1,0:T(8,128)(2,1)S(1)}, u32[]{:S(2)}, u32[]{:S(2)}) %collective-permute-start.6) | collective-permute-done | bytes 229408 | tf_op jit(solution)/shard_map/ppermute | solution.py:306
  73.7 2.2 %collective-permute-done.7.om = bf16[128,896]{1,0:T(8,128)(2,1)S(1)} collective-permute-done((bf16[128,896]{1,0:T(8,128)(2,1)S(1)}, bf16[128,896]{1,0:T(8,128)(2,1)S(1)}, u32[]{:S(2)}, u32[]{:S(2)}) %collective-permute-start.7) | collective-permute-done | bytes 229408 | tf_op jit(solution)/shard_map/ppermute | solution.py:307
  75.8 0.5 shard_map.69
  76.4 26.1 %all_gather.6.rows = bf16[512,768]{1,0:T(8,128)(2,1)S(1)} all-gather(bf16[128,768]{1,0:T(8,128)(2,1)S(1)} %shard_map.69), channel_id=1, replica_groups=mesh['z'=8,'y'=8,'x'=4,'head'=2] {'x'}, dimensions={0}, use_global_device_ids=true | all-gather | bytes 983040 | tf_op jit(solution)/shard_map/all_gather | solution.py:310
  102.5 0.0 all-gather.2.cloned.1.call-done.weight
  102.5 0.0 copy-start
  102.5 1.4 %copy-done = bf16[1024,768]{1,0:T(8,128)(2,1)S(1)} copy-done((bf16[1024,768]{1,0:T(8,128)(2,1)S(1)}, bf16[1024,768]{1,0:T(8,128)(2,1)}, u32[]{:S(2)}) %copy-start) | copy-done | bytes 1572888
  103.9 0.0 copy-start.1
  103.9 0.6 shard_map.71
  104.5 1.9 %collective-permute-start.8 = (bf16[512,512]{1,0:T(8,128)(2,1)S(1)}, bf16[512,512]{1,0:T(8,128)(2,1)S(1)}, u32[]{:S(2)}, u32[]{:S(2)}) collective-permute-start(bf16[512,512]{1,0:T(8,128)(2,1)S(1)} %shard_map.71), channel_id=1, source_target_pairs={{0,1},{1,0},{2,3},{3,2},{4,5},{5,4},{6,7},{7,6},{8,9},{9,8},{10,11... | collective-permute-start | bytes 1572872 | tf_op jit(solution)/shard_map/ppermute | solution.py:312
  106.4 0.0 copy-done.1
  106.5 0.6 shard_map.70
  107.1 0.0 copy-start.2
  107.1 1.2 collective-permute-done.8
  108.3 0.2 add_convert_fusion
  108.5 14.0 %all_to_all.10.pieces = bf16[4,128,512]{2,1,0:T(8,128)(2,1)S(1)} all-to-all(bf16[4,128,512]{2,1,0:T(8,128)(2,1)S(1)} %bitcast.6), channel_id=1, replica_groups=mesh['z'=8,'y'=8,'x'=4,'head'=2] {'x'}, dimensions={0} | all-to-all | bytes 1048576 | tf_op jit(solution)/shard_map/all_to_all | solution.py:315
  122.5 0.0 copy-done.2
  122.5 1.2 shard_map.72
  (5 shorter events, 0.1 us)
Async XLA Ops:
  6.5 18.7 %copy-start.8 = (pred[16]{0:T(512)(128)(4,1)S(1)}, pred[16]{0:T(512)(128)(4,1)}, u32[]{:S(2)}) copy-start(pred[16]{0:T(512)(128)(4,1)} %constant.152.clone.1) | copy-start | bytes 52
  6.5 0.9 copy-start.3
  7.5 0.9 copy-start.4
  8.4 16.6 %copy-start.7 = (s32[1,27]{1,0:T(1,128)S(1)}, s32[1,27]{1,0:T(1,128)}, u32[]{:S(2)}) copy-start(s32[1,27]{1,0:T(1,128)} %param.15) | copy-start | bytes 328
  8.9 21.2 %collective-permute-start = (bf16[256,768]{1,0:T(8,128)(2,1)S(1)}, bf16[256,768]{1,0:T(8,128)(2,1)S(1)}, u32[]{:S(2)}, u32[]{:S(2)}) collective-permute-start(bf16[256,768]{1,0:T(8,128)(2,1)S(1)} %shard_map.64.refs_0_.refs_3_), channel_id=1, source_target_pairs={{64,0},{3,1},{66,2},{5,3},{68,4},{7,5},{70,6},{9,7},{72,8},{11,9},... | collective-permute-start | bytes 1179656 | tf_op jit(solution)/shard_map/ppermute | solution.py:290
  10.8 19.3 %collective-permute-start.1 = (bf16[256,768]{1,0:T(8,128)(2,1)S(1)}, bf16[256,768]{1,0:T(8,128)(2,1)S(1)}, u32[]{:S(2)}, u32[]{:S(2)}) collective-permute-start(bf16[256,768]{1,0:T(8,128)(2,1)S(1)} %shard_map.64.refs_0_.refs_3_), channel_id=1, source_target_pairs={{1,3},{3,5},{5,7},{7,9},{9,11},{11,13},{13,15},{17,19},{19,21},{21... | collective-permute-start | bytes 1179656 | tf_op jit(solution)/shard_map/ppermute | solution.py:291
  17.8 11.6 %all-to-all-start = ((bf16[8,16,768]{2,1,0:T(8,128)(2,1)}), bf16[8,16,768]{2,1,0:T(8,128)(2,1)S(1)}, u32[]{:S(2)}, u32[]{:S(2)}) async-start(bf16[8,16,768]{2,1,0:T(8,128)(2,1)} %broadcast_in_dim.46), calls=%async_computation | async-start | bytes 393216 | tf_op jit(solution)/shard_map/all_to_all | solution.py:293
  25.0 77.5 %all-gather.2.cloned.1.call-start = ((), (), s32[]{:S(2)}) async-start(), calls=%async_computation.2 | async-start | bytes 1769472 | tf_op jit(solution)/shard_map/all_gather | solution.py:294
  29.4 0.7 copy-start.5
  30.1 7.5 %copy-start.6 = (bf16[128,768]{1,0:T(8,128)(2,1)S(1)}, bf16[128,768]{1,0:T(8,128)(2,1)}, u32[]{:S(2)}) copy-start(bf16[128,768]{1,0:T(8,128)(2,1)} %param.12) | copy-start | bytes 589828
  30.7 24.9 %collective-permute-start.2 = (bf16[768,768]{1,0:T(8,128)(2,1)S(1)}, bf16[768,768]{1,0:T(8,128)(2,1)}, u32[]{:S(2)}, u32[]{:S(2)}) collective-permute-start(bf16[768,768]{1,0:T(8,128)(2,1)S(1)} %shard_map.65), channel_id=1, source_target_pairs={{2,0},{65,1},{4,2},{67,3},{6,4},{69,5},{8,6},{71,7},{10,8},{73,9},... | collective-permute-start | bytes 3538952 | tf_op jit(solution)/shard_map/ppermute | solution.py:300
  32.0 23.6 %collective-permute-start.3 = (bf16[768,768]{1,0:T(8,128)(2,1)S(1)}, bf16[768,768]{1,0:T(8,128)(2,1)}, u32[]{:S(2)}, u32[]{:S(2)}) collective-permute-start(bf16[768,768]{1,0:T(8,128)(2,1)S(1)} %shard_map.65), channel_id=1, source_target_pairs={{0,2},{2,4},{4,6},{6,8},{8,10},{10,12},{12,14},{16,18},{18,20},{20... | collective-permute-start | bytes 3538952 | tf_op jit(solution)/shard_map/ppermute | solution.py:301
  37.8 12.1 %collective-permute-start.4 = (bf16[144,768]{1,0:T(8,128)(2,1)S(1)}, bf16[144,768]{1,0:T(8,128)(2,1)S(1)}, u32[]{:S(2)}, u32[]{:S(2)}) collective-permute-start(bf16[144,768]{1,0:T(8,128)(2,1)S(1)} %get-tuple-element.54), channel_id=1, source_target_pairs={{16,0},{17,1},{18,2},{19,3},{20,4},{21,5},{22,6},{23,7},{24,8},{25... | collective-permute-start | bytes 663560 | tf_op jit(solution)/shard_map/ppermute | solution.py:297
  42.5 11.0 %collective-permute-start.5 = (bf16[144,768]{1,0:T(8,128)(2,1)S(1)}, bf16[144,768]{1,0:T(8,128)(2,1)S(1)}, u32[]{:S(2)}, u32[]{:S(2)}) collective-permute-start(bf16[144,768]{1,0:T(8,128)(2,1)S(1)} %get-tuple-element.53), channel_id=1, source_target_pairs={{0,16},{1,17},{2,18},{3,19},{4,20},{5,21},{6,22},{7,23},{8,24},{9,... | collective-permute-start | bytes 663560 | tf_op jit(solution)/shard_map/ppermute | solution.py:298
  60.4 13.3 %collective-permute-start.6 = (bf16[128,896]{1,0:T(8,128)(2,1)S(1)}, bf16[128,896]{1,0:T(8,128)(2,1)S(1)}, u32[]{:S(2)}, u32[]{:S(2)}) collective-permute-start(bf16[128,896]{1,0:T(8,128)(2,1)S(1)} %get-tuple-element.51), channel_id=1, source_target_pairs={{16,0},{17,1},{18,2},{19,3},{20,4},{21,5},{22,6},{23,7},{24,8},{25... | collective-permute-start | bytes 688136 | tf_op jit(solution)/shard_map/ppermute | solution.py:306
  63.3 12.6 %collective-permute-start.7 = (bf16[128,896]{1,0:T(8,128)(2,1)S(1)}, bf16[128,896]{1,0:T(8,128)(2,1)S(1)}, u32[]{:S(2)}, u32[]{:S(2)}) collective-permute-start(bf16[128,896]{1,0:T(8,128)(2,1)S(1)} %get-tuple-element.52), channel_id=1, source_target_pairs={{0,16},{1,17},{2,18},{3,19},{4,20},{5,21},{6,22},{7,23},{8,24},{9,... | collective-permute-start | bytes 688136 | tf_op jit(solution)/shard_map/ppermute | solution.py:307
  102.5 1.4 %copy-start = (bf16[1024,768]{1,0:T(8,128)(2,1)S(1)}, bf16[1024,768]{1,0:T(8,128)(2,1)}, u32[]{:S(2)}) copy-start(bf16[1024,768]{1,0:T(8,128)(2,1)} %all-gather.2.cloned.1.call-done.weight) | copy-start | bytes 4718596
  103.9 2.5 %copy-start.1 = (bf16[1024,768]{1,0:T(8,128)(2,1)S(1)}, bf16[1024,768]{1,0:T(8,128)(2,1)}, u32[]{:S(2)}) copy-start(bf16[1024,768]{1,0:T(8,128)(2,1)} %all-gather.2.cloned.1.call-done.weight) | copy-start | bytes 4718596
  104.5 3.8 %collective-permute-start.8 = (bf16[512,512]{1,0:T(8,128)(2,1)S(1)}, bf16[512,512]{1,0:T(8,128)(2,1)S(1)}, u32[]{:S(2)}, u32[]{:S(2)}) collective-permute-start(bf16[512,512]{1,0:T(8,128)(2,1)S(1)} %shard_map.71), channel_id=1, source_target_pairs={{0,1},{1,0},{2,3},{3,2},{4,5},{5,4},{6,7},{7,6},{8,9},{9,8},{10,11... | collective-permute-start | bytes 1572872 | tf_op jit(solution)/shard_map/ppermute | solution.py:312
  107.1 15.5 %copy-start.2 = (bf16[512,384]{1,0:T(8,128)(2,1)S(1)}, bf16[512,384]{1,0:T(8,128)(2,1)}, u32[]{:S(2)}) copy-start(bf16[512,384]{1,0:T(8,128)(2,1)} %constant.172.clone.order) | copy-start | bytes 1179652
Sparse Core Ops, SparseCore 0:
  30.2 44.6 all-gather.1

commit v7 on v6

--- a/solution.py
+++ b/solution.py
@@ -160,7 +160,7 @@
         out_specs=(VMEM,) * len(out_shape),
         compiler_params=pltpu.CompilerParams(vmem_limit_bytes=12 * 1024 * 1024),
         cost_estimate=pl.CostEstimate(
-            flops=60 * pairs * TILE * TILE * FEAT,
+            flops=36 * pairs * TILE * TILE * FEAT,
             bytes_accessed=len(groups) * 4 * TILE * FEAT,
             transcendentals=pairs * TILE * TILE * HEADS,
         ),
@@ -179,7 +179,7 @@
         copy.wait()
 
 
-def stacked(*arrays):
+def stacked(vmem_limit, *arrays):
     rows = sum(a.shape[0] for a in arrays)
     anywhere = pl.BlockSpec(memory_space=pltpu.HBM if arrays[0].shape[0] == TILE else pl.ANY)
     return pl.pallas_call(
@@ -188,7 +188,7 @@
         in_specs=[anywhere] * len(arrays),
         out_specs=pl.BlockSpec(memory_space=pl.ANY),
         scratch_shapes=[pltpu.SemaphoreType.DMA((len(arrays),))],
-        compiler_params=pltpu.CompilerParams(vmem_limit_bytes=2**20),
+        compiler_params=pltpu.CompilerParams(vmem_limit_bytes=vmem_limit),
         cost_estimate=pl.CostEstimate(flops=0, bytes_accessed=4 * rows * FEAT, transcendentals=0),
     )(*arrays)
 
@@ -286,17 +286,16 @@
 def body(queries, keys, values, window, out_weight):
     my_tile = lax.axis_index(TOK)
     core = lax.axis_index("head")
-    kv = stacked(keys, values)
+    kv = stacked(56 * 2**20, keys, values)
     ap = lax.ppermute(kv, ALL, first_axis(1))
     am = lax.ppermute(kv, ALL, first_axis(-1))
     part = jnp.pad(out_weight.T, ((0, PAD - SHARE), (0, 0)))
-    line_y = lax.all_to_all(jnp.broadcast_to(part, (8, PAD, FEAT)), "y", 0, 0)
-    weight = lax.all_gather(line_y.reshape(-1, FEAT), "z", tiled=True)
+    weight = lax.all_gather(part, ("z", "y"), tiled=True)
     bias = biases(window, my_tile, core)
     q0 = with_biases(queries, bias[0])
     qp = lax.ppermute(with_biases(queries, bias[2]), ALL, row_axis(1))
     qm = lax.ppermute(with_biases(queries, bias[1]), ALL, row_axis(-1))
-    line = stacked(kv, ap, am)
+    line = stacked(2**20, kv, ap, am)
     bp = lax.ppermute(line, ALL, second_axis(1))
     bm = lax.ppermute(line, ALL, second_axis(-1))
     near = [(n, 0, 3 * n) for n in range(3)]

time: 131 us -> 134 us (1.023)
  the two profiles are of different devices: /device:TPU:224 before, /device:TPU:304 now
where the time goes in v7:
time: 134 us
  blocking collectives  38.9 us (29%)
  Pallas kernels  27.8 us (21%)
  starting transfers between devices  24 us (18%)
  waiting for transfers between devices  23.5 us (18%)
  between operations  13.6 us (10%)
  local copies, waits for them, and re-layouts  3.85 us (3%)
  other arithmetic  1.87 us (1%)
    all_gather x1, blocking collectives, body(): rows = lax.all_gather(attended, 'x', tiled=True)  24.9 us
    all_to_all x1, blocking collectives, body(): pieces = lax.all_to_all(columns.reshape(4, TILE, -1), 'x', 0, 0)  14.1 us
    pallas_call x2, Pallas kernels, stacked(): pl.pallas_call(functools.partial(stack_kernel, len(arrays)), out_shape=ja...  13.6 us
    pallas_call x3, Pallas kernels, attention(): pl.pallas_call(functools.partial(attention_kernel, groups, count, state i...  11.3 us
    ppermute x1, waiting for transfers between devices, body(): qm = lax.ppermute(with_biases(queries, bias[1]), ALL, row_axis(-1))  8.32 us
    ppermute x1, starting transfers between devices, body(): bm = lax.ppermute(line, ALL, second_axis(-1))  5.57 us
    ppermute x1, starting transfers between devices, body(): qp = lax.ppermute(with_biases(queries, bias[2]), ALL, row_axis(1))  4.05 us
    ppermute x1, waiting for transfers between devices, body(): back_m = lax.ppermute(op, ALL, row_axis(-1))  4.03 us
  transfers between devices with their start and end apart: 10, of which 7 were waited for; matrix products, arithmetic and copies ran while one was open for 1% of the time, Pallas kernels for 19%

profile of v7, /device:TPU:304, one launch (start us, length us, event | category | flops | bytes accessed | tf_op | source)
XLA Modules:
  0.0 133.7 jit_solution(10042939514697819812)
XLA Ops:
  6.5 0.0 all-gather.2.cloned.1.call-start
  6.5 1.3 %pad.13 = bf16[16,768]{1,0:T(8,128)(2,1)} pad(bf16[12,768]{1,0:T(8,128)(2,1)} %bitcast.6, bf16[]{:T(256)} %constant.171.clone.1), padding=0_4x0_0 | pad | bytes 43010 | tf_op jit(solution)/shard_map/jit(_pad)/pad | solution.py:292
  7.9 0.0 all-gather.2.cloned.1.call-update
  7.9 13.0 %shard_map.64.refs_0_.refs_3_ = bf16[256,768]{1,0:T(8,128)(2,1)} custom-call(bf16[128,768]{1,0:T(8,128)(2,1)} %refs_0_.1, bf16[128,768]{1,0:T(8,128)(2,1)} %refs_1_.1), custom_call_target="tpu_custom_call" | custom-call | bytes 786432 | tf_op jit(solution)/shard_map/pallas_call | solution.py:185
  20.9 1.9 %collective-permute-start = (bf16[256,768]{1,0:T(8,128)(2,1)}, bf16[256,768]{1,0:T(8,128)(2,1)S(1)}, u32[]{:S(2)}, u32[]{:S(2)}) collective-permute-start(bf16[256,768]{1,0:T(8,128)(2,1)} %shard_map.64.refs_0_.refs_3_), channel_id=1, source_target_pairs={{64,0},{3,1},{66,2},{5,3},{68,4},{7,5},{70,6},{9,7},{72,8},{11,9},... | collective-permute-start | bytes 1179656 | tf_op jit(solution)/shard_map/ppermute | solution.py:290
  22.9 3.9 %collective-permute-start.1 = (bf16[256,768]{1,0:T(8,128)(2,1)}, bf16[256,768]{1,0:T(8,128)(2,1)S(1)}, u32[]{:S(2)}, u32[]{:S(2)}) collective-permute-start(bf16[256,768]{1,0:T(8,128)(2,1)} %shard_map.64.refs_0_.refs_3_), channel_id=1, source_target_pairs={{1,3},{3,5},{5,7},{7,9},{9,11},{11,13},{13,15},{17,19},{19,21},{21... | collective-permute-start | bytes 1179656 | tf_op jit(solution)/shard_map/ppermute | solution.py:291
  26.9 0.8 compare_reduce_fusion
  27.8 0.7 slice_select_fusion
  28.4 2.5 %collective-permute-done.refs_1_.refs_4_ = bf16[256,768]{1,0:T(8,128)(2,1)S(1)} collective-permute-done((bf16[256,768]{1,0:T(8,128)(2,1)}, bf16[256,768]{1,0:T(8,128)(2,1)S(1)}, u32[]{:S(2)}, u32[]{:S(2)}) %collective-permute-start) | collective-permute-done | bytes 393248 | tf_op jit(solution)/shard_map/ppermute | solution.py:290
  31.0 3.2 %collective-permute-done.1.refs_2_.refs_5_ = bf16[256,768]{1,0:T(8,128)(2,1)S(1)} collective-permute-done((bf16[256,768]{1,0:T(8,128)(2,1)}, bf16[256,768]{1,0:T(8,128)(2,1)S(1)}, u32[]{:S(2)}, u32[]{:S(2)}) %collective-permute-start.1) | collective-permute-done | bytes 393248 | tf_op jit(solution)/shard_map/ppermute | solution.py:291
  34.1 0.0 copy-start.2
  34.1 1.0 copy-done.2
  35.1 0.0 copy-start.5
  35.1 0.0 copy-start.3
  35.1 0.6 shard_map.65
  35.7 1.3 collective-permute-start.2
  37.0 5.6 %collective-permute-start.3 = (bf16[768,768]{1,0:T(8,128)(2,1)S(1)}, bf16[768,768]{1,0:T(8,128)(2,1)}, u32[]{:S(2)}, u32[]{:S(2)}) collective-permute-start(bf16[768,768]{1,0:T(8,128)(2,1)S(1)} %shard_map.65), channel_id=1, source_target_pairs={{0,2},{2,4},{4,6},{6,8},{8,10},{10,12},{12,14},{16,18},{18,20},{20... | collective-permute-start | bytes 3538952 | tf_op jit(solution)/shard_map/ppermute | solution.py:300
  42.6 0.1 fusion.4
  42.7 0.0 copy-done.5
  42.7 0.1 pad_maximum_fusion
  42.8 4.1 %collective-permute-start.4 = (bf16[144,768]{1,0:T(8,128)(2,1)S(1)}, bf16[144,768]{1,0:T(8,128)(2,1)S(1)}, u32[]{:S(2)}, u32[]{:S(2)}) collective-permute-start(bf16[144,768]{1,0:T(8,128)(2,1)S(1)} %get-tuple-element.54), channel_id=1, source_target_pairs={{16,0},{17,1},{18,2},{19,3},{20,4},{21,5},{22,6},{23,7},{24,8},{25... | collective-permute-start | bytes 663560 | tf_op jit(solution)/shard_map/ppermute | solution.py:296
  46.9 1.3 collective-permute-start.5
  48.2 3.8 %collective-permute-done.4.refs_0_ = bf16[144,768]{1,0:T(8,128)(2,1)S(1)} collective-permute-done((bf16[144,768]{1,0:T(8,128)(2,1)S(1)}, bf16[144,768]{1,0:T(8,128)(2,1)S(1)}, u32[]{:S(2)}, u32[]{:S(2)}) %collective-permute-start.4) | collective-permute-done | bytes 221216 | tf_op jit(solution)/shard_map/ppermute | solution.py:296
  52.0 8.3 %collective-permute-done.5.refs_1_ = bf16[144,768]{1,0:T(8,128)(2,1)S(1)} collective-permute-done((bf16[144,768]{1,0:T(8,128)(2,1)S(1)}, bf16[144,768]{1,0:T(8,128)(2,1)S(1)}, u32[]{:S(2)}, u32[]{:S(2)}) %collective-permute-start.5) | collective-permute-done | bytes 221216 | tf_op jit(solution)/shard_map/ppermute | solution.py:297
  60.3 0.0 copy-done.3
  60.4 2.1 %shard_map.66 = (f32[384,768]{1,0:T(8,128)S(1)}, f32[384,128]{1,0:T(8,128)S(1)}) custom-call(bf16[144,768]{1,0:T(8,128)(2,1)S(1)} %collective-permute-done.4.refs_0_, bf16[144,768]{1,0:T(8,128)(2,1)S(1)} %collective-permute-done.5.refs_1_, bf16[144,768]{1,0:T(8,128)(2,1)S(1)} %get-tuple-element.55.refs_2_.refs_0_, bf16[256,768]{1,0:T(8,128)(2,1)S(1)} %copy-done.3, ...), custom_call_target="tpu_custom_call" | custom-call | flops 4076863488 | bytes 1179648 | tf_op jit(solution)/shard_map/pallas_call | solution.py:155
  62.5 0.0 collective-permute-done.2.refs_1_.refs_2_
  62.5 0.0 collective-permute-done.3.refs_2_.refs_3_
  62.5 4.8 %shard_map.68 = (bf16[128,896]{1,0:T(8,128)(2,1)S(1)}, bf16[128,896]{1,0:T(8,128)(2,1)S(1)}) custom-call(bf16[144,768]{1,0:T(8,128)(2,1)S(1)} %collective-permute-done.4.refs_0_, bf16[144,768]{1,0:T(8,128)(2,1)S(1)} %collective-permute-done.5.refs_1_, bf16[768,768]{1,0:T(8,128)(2,1)} %collective-permute-done.2.refs_1_.refs_2_, ...), custom_call_target="tpu_custom_call" | custom-call | flops 5435817984 | bytes 2359296 | tf_op jit(solution)/shard_map/pallas_call | solution.py:155
  67.3 2.8 %collective-permute-start.6 = (bf16[128,896]{1,0:T(8,128)(2,1)S(1)}, bf16[128,896]{1,0:T(8,128)(2,1)S(1)}, u32[]{:S(2)}, u32[]{:S(2)}) collective-permute-start(bf16[128,896]{1,0:T(8,128)(2,1)S(1)} %get-tuple-element.51), channel_id=1, source_target_pairs={{16,0},{17,1},{18,2},{19,3},{20,4},{21,5},{22,6},{23,7},{24,8},{25... | collective-permute-start | bytes 688136 | tf_op jit(solution)/shard_map/ppermute | solution.py:305
  70.1 1.3 collective-permute-start.7
  71.4 4.4 %shard_map.67 = (f32[128,768]{1,0:T(8,128)S(1)}, f32[128,128]{1,0:T(8,128)S(1)}) custom-call(bf16[144,768]{1,0:T(8,128)(2,1)S(1)} %get-tuple-element.55.refs_2_.refs_0_, bf16[768,768]{1,0:T(8,128)(2,1)} %collective-permute-done.2.refs_1_.refs_2_, bf16[768,768]{1,0:T(8,128)(2,1)} %collective-permute-done.3.refs_2_.refs_3_, ...), custom_call_target="tpu_custom_call" | custom-call | flops 2717908992 | bytes 2359296 | tf_op jit(solution)/shard_map/pallas_call | solution.py:155
  75.8 0.4 collective-permute-done.6.op
  76.2 4.0 %collective-permute-done.7.om = bf16[128,896]{1,0:T(8,128)(2,1)S(1)} collective-permute-done((bf16[128,896]{1,0:T(8,128)(2,1)S(1)}, bf16[128,896]{1,0:T(8,128)(2,1)S(1)}, u32[]{:S(2)}, u32[]{:S(2)}) %collective-permute-start.7) | collective-permute-done | bytes 229408 | tf_op jit(solution)/shard_map/ppermute | solution.py:306
  80.2 0.5 shard_map.69
  80.7 24.9 %all_gather.6.rows = bf16[512,768]{1,0:T(8,128)(2,1)S(1)} all-gather(bf16[128,768]{1,0:T(8,128)(2,1)S(1)} %shard_map.69), channel_id=1, replica_groups=mesh['z'=8,'y'=8,'x'=4,'head'=2] {'x'}, dimensions={0}, use_global_device_ids=true | all-gather | bytes 983040 | tf_op jit(solution)/shard_map/all_gather | solution.py:309
  105.6 0.0 all-gather.2.cloned.1.call-done.weight
  105.6 0.0 copy-start
  105.6 1.4 %copy-done = bf16[1024,768]{1,0:T(8,128)(2,1)S(1)} copy-done((bf16[1024,768]{1,0:T(8,128)(2,1)S(1)}, bf16[1024,768]{1,0:T(8,128)(2,1)}, u32[]{:S(2)}) %copy-start) | copy-done | bytes 1572888
  107.0 0.0 copy-start.1
  107.0 0.6 shard_map.71
  107.7 1.9 %collective-permute-start.8 = (bf16[512,512]{1,0:T(8,128)(2,1)S(1)}, bf16[512,512]{1,0:T(8,128)(2,1)S(1)}, u32[]{:S(2)}, u32[]{:S(2)}) collective-permute-start(bf16[512,512]{1,0:T(8,128)(2,1)S(1)} %shard_map.71), channel_id=1, source_target_pairs={{0,1},{1,0},{2,3},{3,2},{4,5},{5,4},{6,7},{7,6},{8,9},{9,8},{10,11... | collective-permute-start | bytes 1572872 | tf_op jit(solution)/shard_map/ppermute | solution.py:311
  109.6 0.0 copy-done.1
  109.6 0.6 shard_map.70
  110.2 0.0 copy-start.4
  110.2 1.2 collective-permute-done.8
  111.5 0.2 add_convert_fusion
  111.6 14.1 %all_to_all.5.pieces = bf16[4,128,512]{2,1,0:T(8,128)(2,1)S(1)} all-to-all(bf16[4,128,512]{2,1,0:T(8,128)(2,1)S(1)} %bitcast.5), channel_id=1, replica_groups=mesh['z'=8,'y'=8,'x'=4,'head'=2] {'x'}, dimensions={0} | all-to-all | bytes 1048576 | tf_op jit(solution)/shard_map/all_to_all | solution.py:314
  125.7 0.0 copy-done.4
  125.7 1.2 shard_map.72
  (4 shorter events, 0.1 us)
Async XLA Ops:
  6.5 99.1 %all-gather.2.cloned.1.call-start = ((), (), s32[]{:S(2)}) async-start(), calls=%async_computation.1 | async-start | bytes 1597440 | tf_op jit(solution)/shard_map/all_gather | solution.py:293
  20.9 10.0 %collective-permute-start = (bf16[256,768]{1,0:T(8,128)(2,1)}, bf16[256,768]{1,0:T(8,128)(2,1)S(1)}, u32[]{:S(2)}, u32[]{:S(2)}) collective-permute-start(bf16[256,768]{1,0:T(8,128)(2,1)} %shard_map.64.refs_0_.refs_3_), channel_id=1, source_target_pairs={{64,0},{3,1},{66,2},{5,3},{68,4},{7,5},{70,6},{9,7},{72,8},{11,9},... | collective-permute-start | bytes 1179656 | tf_op jit(solution)/shard_map/ppermute | solution.py:290
  22.9 11.2 %collective-permute-start.1 = (bf16[256,768]{1,0:T(8,128)(2,1)}, bf16[256,768]{1,0:T(8,128)(2,1)S(1)}, u32[]{:S(2)}, u32[]{:S(2)}) collective-permute-start(bf16[256,768]{1,0:T(8,128)(2,1)} %shard_map.64.refs_0_.refs_3_), channel_id=1, source_target_pairs={{1,3},{3,5},{5,7},{7,9},{9,11},{11,13},{13,15},{17,19},{19,21},{21... | collective-permute-start | bytes 1179656 | tf_op jit(solution)/shard_map/ppermute | solution.py:291
  34.1 1.0 copy-start.2
  35.1 7.6 %copy-start.5 = (bf16[128,768]{1,0:T(8,128)(2,1)S(1)}, bf16[128,768]{1,0:T(8,128)(2,1)}, u32[]{:S(2)}) copy-start(bf16[128,768]{1,0:T(8,128)(2,1)} %param.12) | copy-start | bytes 589828
  35.1 25.2 %copy-start.3 = (bf16[256,768]{1,0:T(8,128)(2,1)S(1)}, bf16[256,768]{1,0:T(8,128)(2,1)}, u32[]{:S(2)}) copy-start(bf16[256,768]{1,0:T(8,128)(2,1)} %shard_map.64.refs_0_.refs_3_) | copy-start | bytes 1179652
  35.7 26.8 %collective-permute-start.2 = (bf16[768,768]{1,0:T(8,128)(2,1)S(1)}, bf16[768,768]{1,0:T(8,128)(2,1)}, u32[]{:S(2)}, u32[]{:S(2)}) collective-permute-start(bf16[768,768]{1,0:T(8,128)(2,1)S(1)} %shard_map.65), channel_id=1, source_target_pairs={{2,0},{65,1},{4,2},{67,3},{6,4},{69,5},{8,6},{71,7},{10,8},{73,9},... | collective-permute-start | bytes 3538952 | tf_op jit(solution)/shard_map/ppermute | solution.py:299
  37.0 25.5 %collective-permute-start.3 = (bf16[768,768]{1,0:T(8,128)(2,1)S(1)}, bf16[768,768]{1,0:T(8,128)(2,1)}, u32[]{:S(2)}, u32[]{:S(2)}) collective-permute-start(bf16[768,768]{1,0:T(8,128)(2,1)S(1)} %shard_map.65), channel_id=1, source_target_pairs={{0,2},{2,4},{4,6},{6,8},{8,10},{10,12},{12,14},{16,18},{18,20},{20... | collective-permute-start | bytes 3538952 | tf_op jit(solution)/shard_map/ppermute | solution.py:300
  42.8 9.2 %collective-permute-start.4 = (bf16[144,768]{1,0:T(8,128)(2,1)S(1)}, bf16[144,768]{1,0:T(8,128)(2,1)S(1)}, u32[]{:S(2)}, u32[]{:S(2)}) collective-permute-start(bf16[144,768]{1,0:T(8,128)(2,1)S(1)} %get-tuple-element.54), channel_id=1, source_target_pairs={{16,0},{17,1},{18,2},{19,3},{20,4},{21,5},{22,6},{23,7},{24,8},{25... | collective-permute-start | bytes 663560 | tf_op jit(solution)/shard_map/ppermute | solution.py:296
  46.9 13.5 %collective-permute-start.5 = (bf16[144,768]{1,0:T(8,128)(2,1)S(1)}, bf16[144,768]{1,0:T(8,128)(2,1)S(1)}, u32[]{:S(2)}, u32[]{:S(2)}) collective-permute-start(bf16[144,768]{1,0:T(8,128)(2,1)S(1)} %get-tuple-element.53), channel_id=1, source_target_pairs={{0,16},{1,17},{2,18},{3,19},{4,20},{5,21},{6,22},{7,23},{8,24},{9,... | collective-permute-start | bytes 663560 | tf_op jit(solution)/shard_map/ppermute | solution.py:297
  67.3 8.9 %collective-permute-start.6 = (bf16[128,896]{1,0:T(8,128)(2,1)S(1)}, bf16[128,896]{1,0:T(8,128)(2,1)S(1)}, u32[]{:S(2)}, u32[]{:S(2)}) collective-permute-start(bf16[128,896]{1,0:T(8,128)(2,1)S(1)} %get-tuple-element.51), channel_id=1, source_target_pairs={{16,0},{17,1},{18,2},{19,3},{20,4},{21,5},{22,6},{23,7},{24,8},{25... | collective-permute-start | bytes 688136 | tf_op jit(solution)/shard_map/ppermute | solution.py:305
  70.1 10.1 %collective-permute-start.7 = (bf16[128,896]{1,0:T(8,128)(2,1)S(1)}, bf16[128,896]{1,0:T(8,128)(2,1)S(1)}, u32[]{:S(2)}, u32[]{:S(2)}) collective-permute-start(bf16[128,896]{1,0:T(8,128)(2,1)S(1)} %get-tuple-element.52), channel_id=1, source_target_pairs={{0,16},{1,17},{2,18},{3,19},{4,20},{5,21},{6,22},{7,23},{8,24},{9,... | collective-permute-start | bytes 688136 | tf_op jit(solution)/shard_map/ppermute | solution.py:306
  105.6 1.4 %copy-start = (bf16[1024,768]{1,0:T(8,128)(2,1)S(1)}, bf16[1024,768]{1,0:T(8,128)(2,1)}, u32[]{:S(2)}) copy-start(bf16[1024,768]{1,0:T(8,128)(2,1)} %all-gather.2.cloned.1.call-done.weight) | copy-start | bytes 4718596
  107.0 2.5 %copy-start.1 = (bf16[1024,768]{1,0:T(8,128)(2,1)S(1)}, bf16[1024,768]{1,0:T(8,128)(2,1)}, u32[]{:S(2)}) copy-start(bf16[1024,768]{1,0:T(8,128)(2,1)} %all-gather.2.cloned.1.call-done.weight) | copy-start | bytes 4718596
  107.7 3.8 %collective-permute-start.8 = (bf16[512,512]{1,0:T(8,128)(2,1)S(1)}, bf16[512,512]{1,0:T(8,128)(2,1)S(1)}, u32[]{:S(2)}, u32[]{:S(2)}) collective-permute-start(bf16[512,512]{1,0:T(8,128)(2,1)S(1)} %shard_map.71), channel_id=1, source_target_pairs={{0,1},{1,0},{2,3},{3,2},{4,5},{5,4},{6,7},{7,6},{8,9},{9,8},{10,11... | collective-permute-start | bytes 1572872 | tf_op jit(solution)/shard_map/ppermute | solution.py:311
  110.2 15.5 %copy-start.4 = (bf16[512,384]{1,0:T(8,128)(2,1)S(1)}, bf16[512,384]{1,0:T(8,128)(2,1)}, u32[]{:S(2)}) copy-start(bf16[512,384]{1,0:T(8,128)(2,1)} %constant.172.clone.order) | copy-start | bytes 1179652
Sparse Core Ops, SparseCore 0:
  10.4 85.3 all-gather.1

commit v8 on v6

--- a/solution.py
+++ b/solution.py
@@ -289,14 +289,15 @@
     kv = stacked(keys, values)
     ap = lax.ppermute(kv, ALL, first_axis(1))
     am = lax.ppermute(kv, ALL, first_axis(-1))
-    part = jnp.pad(out_weight.T, ((0, PAD - SHARE), (0, 0)))
-    line_y = lax.all_to_all(jnp.broadcast_to(part, (8, PAD, FEAT)), "y", 0, 0)
-    weight = lax.all_gather(line_y.reshape(-1, FEAT), "z", tiled=True)
+    line_y = lax.all_to_all(jnp.broadcast_to(out_weight.T, (8, SHARE, FEAT)), "y", 0, 0)
     bias = biases(window, my_tile, core)
     q0 = with_biases(queries, bias[0])
     qp = lax.ppermute(with_biases(queries, bias[2]), ALL, row_axis(1))
     qm = lax.ppermute(with_biases(queries, bias[1]), ALL, row_axis(-1))
     line = stacked(kv, ap, am)
+    line_y, _ = lax.optimization_barrier((line_y, line))
+    line_y = jnp.pad(line_y, ((0, 0), (0, PAD - SHARE), (0, 0)))
+    weight = lax.all_gather(line_y.reshape(-1, FEAT), "z", tiled=True)
     bp = lax.ppermute(line, ALL, second_axis(1))
     bm = lax.ppermute(line, ALL, second_axis(-1))
     near = [(n, 0, 3 * n) for n in range(3)]

time: 131 us -> 120 us (0.916)
  the two profiles are of different devices: /device:TPU:224 before, /device:TPU:240 now
where the time goes in v8:
time: 120 us; the launch traced here: 119 us
  starting transfers between devices  36.2 us (30%)
  blocking collectives  33.4 us (28%)
  Pallas kernels  15.3 us (13%)
  waiting for transfers between devices  14.8 us (12%)
  between operations  13.6 us (11%)
  local copies, waits for them, and re-layouts  5.51 us (5%)
    all_gather x1, blocking collectives, body(): rows = lax.all_gather(attended, 'x', tiled=True)  19.3 us
    all_to_all x1, blocking collectives, body(): pieces = lax.all_to_all(columns.reshape(4, TILE, -1), 'x', 0, 0)  14.1 us
    pallas_call x3, Pallas kernels, attention(): pl.pallas_call(functools.partial(attention_kernel, groups, count, state i...  11.3 us
    all_to_all x1, starting transfers between devices, body(): lax.all_to_all(jnp.broadcast_to(out_weight.T, (8, SHARE, FEAT)), 'y', 0, 0)  6.98 us
    ppermute x1, starting transfers between devices, body(): back_p = lax.ppermute(om, ALL, row_axis(1))  6.19 us
    ppermute x1, starting transfers between devices, body(): bm = lax.ppermute(line, ALL, second_axis(-1))  5.59 us
    ppermute x1, starting transfers between devices, body(): am = lax.ppermute(kv, ALL, first_axis(-1))  5.49 us
    ppermute x1, waiting for transfers between devices, body(): qm = lax.ppermute(with_biases(queries, bias[1]), ALL, row_axis(-1))  4.63 us
  transfers between devices with their start and end apart: 11, of which 4 were waited for; matrix products, arithmetic and copies ran while one was open for 2% of the time, Pallas kernels for 11%

profile of v8, /device:TPU:240, one launch (start us, length us, event | category | flops | bytes accessed | tf_op | source)
XLA Modules:
  0.0 119.5 jit_solution(1134062012749046600)
XLA Ops:
  6.5 0.0 copy-start.7
  6.5 0.0 copy-start.3
  6.5 0.9 copy-done.3
  7.5 0.0 copy-start.4
  7.5 0.9 copy-done.4
  8.4 0.0 copy-start.6
  8.4 0.5 shard_map.64.refs_0_.refs_3_
  8.9 1.9 %collective-permute-start = (bf16[256,768]{1,0:T(8,128)(2,1)S(1)}, bf16[256,768]{1,0:T(8,128)(2,1)S(1)}, u32[]{:S(2)}, u32[]{:S(2)}) collective-permute-start(bf16[256,768]{1,0:T(8,128)(2,1)S(1)} %shard_map.64.refs_0_.refs_3_), channel_id=1, source_target_pairs={{64,0},{3,1},{66,2},{5,3},{68,4},{7,5},{70,6},{9,7},{72,8},{11,9},... | collective-permute-start | bytes 1179656 | tf_op jit(solution)/shard_map/ppermute | solution.py:290
  10.8 5.5 %collective-permute-start.1 = (bf16[256,768]{1,0:T(8,128)(2,1)S(1)}, bf16[256,768]{1,0:T(8,128)(2,1)S(1)}, u32[]{:S(2)}, u32[]{:S(2)}) collective-permute-start(bf16[256,768]{1,0:T(8,128)(2,1)S(1)} %shard_map.64.refs_0_.refs_3_), channel_id=1, source_target_pairs={{1,3},{3,5},{5,7},{7,9},{9,11},{11,13},{13,15},{17,19},{19,21},{21... | collective-permute-start | bytes 1179656 | tf_op jit(solution)/shard_map/ppermute | solution.py:291
  16.3 1.4 %broadcast_in_dim.46 = bf16[8,12,768]{2,1,0:T(8,128)(2,1)} broadcast(bf16[12,768]{1,0:T(8,128)(2,1)} %bitcast.8), dimensions={1,2} | broadcast | bytes 165888 | tf_op jit(solution)/shard_map/broadcast_in_dim | solution.py:292
  17.8 7.0 %all-to-all-start = ((bf16[8,12,768]{2,1,0:T(8,128)(2,1)}), bf16[8,12,768]{2,1,0:T(8,128)(2,1)S(1)}, u32[]{:S(2)}, u32[]{:S(2)}) async-start(bf16[8,12,768]{2,1,0:T(8,128)(2,1)} %broadcast_in_dim.46), calls=%async_computation | async-start | bytes 393216 | tf_op jit(solution)/shard_map/all_to_all | solution.py:292
  24.8 0.0 all-gather.2.cloned.1.call-start
  24.8 0.0 copy-done.6
  24.8 0.2 compare_reduce_fusion
  25.0 0.0 copy-done.7
  25.1 0.1 fusion.4
  25.1 0.0 copy-start.5
  25.1 0.0 collective-permute-done.refs_1_.refs_4_
  25.1 0.0 collective-permute-done.1.refs_2_.refs_5_
  25.2 0.6 shard_map.65
  25.8 1.3 %collective-permute-start.2 = (bf16[768,768]{1,0:T(8,128)(2,1)S(1)}, bf16[768,768]{1,0:T(8,128)(2,1)}, u32[]{:S(2)}, u32[]{:S(2)}) collective-permute-start(bf16[768,768]{1,0:T(8,128)(2,1)S(1)} %shard_map.65), channel_id=1, source_target_pairs={{2,0},{65,1},{4,2},{67,3},{6,4},{69,5},{8,6},{71,7},{10,8},{73,9},... | collective-permute-start | bytes 3538952 | tf_op jit(solution)/shard_map/ppermute | solution.py:301
  27.1 5.6 %collective-permute-start.3 = (bf16[768,768]{1,0:T(8,128)(2,1)S(1)}, bf16[768,768]{1,0:T(8,128)(2,1)}, u32[]{:S(2)}, u32[]{:S(2)}) collective-permute-start(bf16[768,768]{1,0:T(8,128)(2,1)S(1)} %shard_map.65), channel_id=1, source_target_pairs={{0,2},{2,4},{4,6},{6,8},{8,10},{10,12},{12,14},{16,18},{18,20},{20... | collective-permute-start | bytes 3538952 | tf_op jit(solution)/shard_map/ppermute | solution.py:302
  32.6 0.0 all-to-all-done
  32.7 0.7 pad.13
  33.3 0.0 all-gather.2.cloned.1.call-update
  33.4 0.0 copy-done.5
  33.4 0.1 pad_maximum_fusion
  33.5 4.3 %collective-permute-start.4 = (bf16[144,768]{1,0:T(8,128)(2,1)S(1)}, bf16[144,768]{1,0:T(8,128)(2,1)S(1)}, u32[]{:S(2)}, u32[]{:S(2)}) collective-permute-start(bf16[144,768]{1,0:T(8,128)(2,1)S(1)} %get-tuple-element.56), channel_id=1, source_target_pairs={{16,0},{17,1},{18,2},{19,3},{20,4},{21,5},{22,6},{23,7},{24,8},{25... | collective-permute-start | bytes 663560 | tf_op jit(solution)/shard_map/ppermute | solution.py:295
  37.8 1.3 %collective-permute-start.5 = (bf16[144,768]{1,0:T(8,128)(2,1)S(1)}, bf16[144,768]{1,0:T(8,128)(2,1)S(1)}, u32[]{:S(2)}, u32[]{:S(2)}) collective-permute-start(bf16[144,768]{1,0:T(8,128)(2,1)S(1)} %get-tuple-element.55), channel_id=1, source_target_pairs={{0,16},{1,17},{2,18},{3,19},{4,20},{5,21},{6,22},{7,23},{8,24},{9,... | collective-permute-start | bytes 663560 | tf_op jit(solution)/shard_map/ppermute | solution.py:296
  39.1 4.4 %collective-permute-done.4.refs_0_ = bf16[144,768]{1,0:T(8,128)(2,1)S(1)} collective-permute-done((bf16[144,768]{1,0:T(8,128)(2,1)S(1)}, bf16[144,768]{1,0:T(8,128)(2,1)S(1)}, u32[]{:S(2)}, u32[]{:S(2)}) %collective-permute-start.4) | collective-permute-done | bytes 221216 | tf_op jit(solution)/shard_map/ppermute | solution.py:295
  43.5 4.6 %collective-permute-done.5.refs_1_ = bf16[144,768]{1,0:T(8,128)(2,1)S(1)} collective-permute-done((bf16[144,768]{1,0:T(8,128)(2,1)S(1)}, bf16[144,768]{1,0:T(8,128)(2,1)S(1)}, u32[]{:S(2)}, u32[]{:S(2)}) %collective-permute-start.5) | collective-permute-done | bytes 221216 | tf_op jit(solution)/shard_map/ppermute | solution.py:296
  48.1 2.1 %shard_map.66 = (f32[384,768]{1,0:T(8,128)S(1)}, f32[384,128]{1,0:T(8,128)S(1)}) custom-call(bf16[144,768]{1,0:T(8,128)(2,1)S(1)} %collective-permute-done.4.refs_0_, bf16[144,768]{1,0:T(8,128)(2,1)S(1)} %collective-permute-done.5.refs_1_, bf16[144,768]{1,0:T(8,128)(2,1)S(1)} %get-tuple-element.57.refs_2_.refs_0_, ...), custom_call_target="tpu_custom_call" | custom-call | flops 6794772480 | bytes 1179648 | tf_op jit(solution)/shard_map/pallas_call | solution.py:155
  50.3 0.0 collective-permute-done.2.refs_1_.refs_2_
  50.3 0.0 collective-permute-done.3.refs_2_.refs_3_
  50.3 4.8 %shard_map.68 = (bf16[128,896]{1,0:T(8,128)(2,1)S(1)}, bf16[128,896]{1,0:T(8,128)(2,1)S(1)}) custom-call(bf16[144,768]{1,0:T(8,128)(2,1)S(1)} %collective-permute-done.4.refs_0_, bf16[144,768]{1,0:T(8,128)(2,1)S(1)} %collective-permute-done.5.refs_1_, bf16[768,768]{1,0:T(8,128)(2,1)} %collective-permute-done.2.refs_1_.refs_2_, ...), custom_call_target="tpu_custom_call" | custom-call | flops 9059696640 | bytes 2359296 | tf_op jit(solution)/shard_map/pallas_call | solution.py:155
  55.1 6.2 %collective-permute-start.6 = (bf16[128,896]{1,0:T(8,128)(2,1)S(1)}, bf16[128,896]{1,0:T(8,128)(2,1)S(1)}, u32[]{:S(2)}, u32[]{:S(2)}) collective-permute-start(bf16[128,896]{1,0:T(8,128)(2,1)S(1)} %get-tuple-element.52), channel_id=1, source_target_pairs={{16,0},{17,1},{18,2},{19,3},{20,4},{21,5},{22,6},{23,7},{24,8},{25... | collective-permute-start | bytes 688136 | tf_op jit(solution)/shard_map/ppermute | solution.py:307
  61.3 1.3 %collective-permute-start.7 = (bf16[128,896]{1,0:T(8,128)(2,1)S(1)}, bf16[128,896]{1,0:T(8,128)(2,1)S(1)}, u32[]{:S(2)}, u32[]{:S(2)}) collective-permute-start(bf16[128,896]{1,0:T(8,128)(2,1)S(1)} %get-tuple-element.53), channel_id=1, source_target_pairs={{0,16},{1,17},{2,18},{3,19},{4,20},{5,21},{6,22},{7,23},{8,24},{9,... | collective-permute-start | bytes 688136 | tf_op jit(solution)/shard_map/ppermute | solution.py:308
  62.6 4.4 %shard_map.67 = (f32[128,768]{1,0:T(8,128)S(1)}, f32[128,128]{1,0:T(8,128)S(1)}) custom-call(bf16[144,768]{1,0:T(8,128)(2,1)S(1)} %get-tuple-element.57.refs_2_.refs_0_, bf16[768,768]{1,0:T(8,128)(2,1)} %collective-permute-done.2.refs_1_.refs_2_, bf16[768,768]{1,0:T(8,128)(2,1)} %collective-permute-done.3.refs_2_.refs_3_, ...), custom_call_target="tpu_custom_call" | custom-call | flops 4529848320 | bytes 2359296 | tf_op jit(solution)/shard_map/pallas_call | solution.py:155
  67.0 0.0 collective-permute-done.6.op
  67.0 4.6 %collective-permute-done.7.om = bf16[128,896]{1,0:T(8,128)(2,1)S(1)} collective-permute-done((bf16[128,896]{1,0:T(8,128)(2,1)S(1)}, bf16[128,896]{1,0:T(8,128)(2,1)S(1)}, u32[]{:S(2)}, u32[]{:S(2)}) %collective-permute-start.7) | collective-permute-done | bytes 229408 | tf_op jit(solution)/shard_map/ppermute | solution.py:308
  71.5 0.5 shard_map.69
  72.1 19.3 %all_gather.6.rows = bf16[512,768]{1,0:T(8,128)(2,1)S(1)} all-gather(bf16[128,768]{1,0:T(8,128)(2,1)S(1)} %shard_map.69), channel_id=1, replica_groups=mesh['z'=8,'y'=8,'x'=4,'head'=2] {'x'}, dimensions={0}, use_global_device_ids=true | all-gather | bytes 983040 | tf_op jit(solution)/shard_map/all_gather | solution.py:311
  91.4 0.0 all-gather.2.cloned.1.call-done.weight
  91.4 0.0 copy-start
  91.4 1.4 %copy-done = bf16[1024,768]{1,0:T(8,128)(2,1)S(1)} copy-done((bf16[1024,768]{1,0:T(8,128)(2,1)S(1)}, bf16[1024,768]{1,0:T(8,128)(2,1)}, u32[]{:S(2)}) %copy-start) | copy-done | bytes 1572888
  92.8 0.0 copy-start.1
  92.8 0.6 shard_map.71
  93.4 1.9 %collective-permute-start.8 = (bf16[512,512]{1,0:T(8,128)(2,1)S(1)}, bf16[512,512]{1,0:T(8,128)(2,1)S(1)}, u32[]{:S(2)}, u32[]{:S(2)}) collective-permute-start(bf16[512,512]{1,0:T(8,128)(2,1)S(1)} %shard_map.71), channel_id=1, source_target_pairs={{0,1},{1,0},{2,3},{3,2},{4,5},{5,4},{6,7},{7,6},{8,9},{9,8},{10,11... | collective-permute-start | bytes 1572872 | tf_op jit(solution)/shard_map/ppermute | solution.py:313
  95.3 0.0 copy-done.1
  95.3 0.6 shard_map.70
  96.0 0.0 copy-start.2
  96.0 1.2 %collective-permute-done.8 = bf16[512,512]{1,0:T(8,128)(2,1)S(1)} collective-permute-done((bf16[512,512]{1,0:T(8,128)(2,1)S(1)}, bf16[512,512]{1,0:T(8,128)(2,1)S(1)}, u32[]{:S(2)}, u32[]{:S(2)}) %collective-permute-start.8) | collective-permute-done | bytes 524320 | tf_op jit(solution)/shard_map/ppermute | solution.py:313
  97.2 0.2 add_convert_fusion
  97.4 14.1 %all_to_all.10.pieces = bf16[4,128,512]{2,1,0:T(8,128)(2,1)S(1)} all-to-all(bf16[4,128,512]{2,1,0:T(8,128)(2,1)S(1)} %bitcast.6), channel_id=1, replica_groups=mesh['z'=8,'y'=8,'x'=4,'head'=2] {'x'}, dimensions={0} | all-to-all | bytes 1048576 | tf_op jit(solution)/shard_map/all_to_all | solution.py:316
  111.4 0.0 copy-done.2
  111.4 1.2 shard_map.72
  (5 shorter events, 0.1 us)
Async XLA Ops:
  6.5 18.5 %copy-start.7 = (pred[16]{0:T(512)(128)(4,1)S(1)}, pred[16]{0:T(512)(128)(4,1)}, u32[]{:S(2)}) copy-start(pred[16]{0:T(512)(128)(4,1)} %constant.152.clone.1) | copy-start | bytes 52
  6.5 0.9 copy-start.3
  7.5 0.9 copy-start.4
  8.4 16.4 %copy-start.6 = (s32[1,27]{1,0:T(1,128)S(1)}, s32[1,27]{1,0:T(1,128)}, u32[]{:S(2)}) copy-start(s32[1,27]{1,0:T(1,128)} %param.15) | copy-start | bytes 328
  8.9 16.2 %collective-permute-start = (bf16[256,768]{1,0:T(8,128)(2,1)S(1)}, bf16[256,768]{1,0:T(8,128)(2,1)S(1)}, u32[]{:S(2)}, u32[]{:S(2)}) collective-permute-start(bf16[256,768]{1,0:T(8,128)(2,1)S(1)} %shard_map.64.refs_0_.refs_3_), channel_id=1, source_target_pairs={{64,0},{3,1},{66,2},{5,3},{68,4},{7,5},{70,6},{9,7},{72,8},{11,9},... | collective-permute-start | bytes 1179656 | tf_op jit(solution)/shard_map/ppermute | solution.py:290
  10.8 14.3 %collective-permute-start.1 = (bf16[256,768]{1,0:T(8,128)(2,1)S(1)}, bf16[256,768]{1,0:T(8,128)(2,1)S(1)}, u32[]{:S(2)}, u32[]{:S(2)}) collective-permute-start(bf16[256,768]{1,0:T(8,128)(2,1)S(1)} %shard_map.64.refs_0_.refs_3_), channel_id=1, source_target_pairs={{1,3},{3,5},{5,7},{7,9},{9,11},{11,13},{13,15},{17,19},{19,21},{21... | collective-permute-start | bytes 1179656 | tf_op jit(solution)/shard_map/ppermute | solution.py:291
  17.8 14.9 %all-to-all-start = ((bf16[8,12,768]{2,1,0:T(8,128)(2,1)}), bf16[8,12,768]{2,1,0:T(8,128)(2,1)S(1)}, u32[]{:S(2)}, u32[]{:S(2)}) async-start(bf16[8,12,768]{2,1,0:T(8,128)(2,1)} %broadcast_in_dim.46), calls=%async_computation | async-start | bytes 393216 | tf_op jit(solution)/shard_map/all_to_all | solution.py:292
  24.8 66.6 %all-gather.2.cloned.1.call-start = ((), (), s32[]{:S(2)}) async-start(), calls=%async_computation.2 | async-start | bytes 1769472 | tf_op jit(solution)/shard_map/all_gather | solution.py:300
  25.1 8.2 %copy-start.5 = (bf16[128,768]{1,0:T(8,128)(2,1)S(1)}, bf16[128,768]{1,0:T(8,128)(2,1)}, u32[]{:S(2)}) copy-start(bf16[128,768]{1,0:T(8,128)(2,1)} %param.12) | copy-start | bytes 589828
  25.8 24.5 %collective-permute-start.2 = (bf16[768,768]{1,0:T(8,128)(2,1)S(1)}, bf16[768,768]{1,0:T(8,128)(2,1)}, u32[]{:S(2)}, u32[]{:S(2)}) collective-permute-start(bf16[768,768]{1,0:T(8,128)(2,1)S(1)} %shard_map.65), channel_id=1, source_target_pairs={{2,0},{65,1},{4,2},{67,3},{6,4},{69,5},{8,6},{71,7},{10,8},{73,9},... | collective-permute-start | bytes 3538952 | tf_op jit(solution)/shard_map/ppermute | solution.py:301
  27.1 23.2 %collective-permute-start.3 = (bf16[768,768]{1,0:T(8,128)(2,1)S(1)}, bf16[768,768]{1,0:T(8,128)(2,1)}, u32[]{:S(2)}, u32[]{:S(2)}) collective-permute-start(bf16[768,768]{1,0:T(8,128)(2,1)S(1)} %shard_map.65), channel_id=1, source_target_pairs={{0,2},{2,4},{4,6},{6,8},{8,10},{10,12},{12,14},{16,18},{18,20},{20... | collective-permute-start | bytes 3538952 | tf_op jit(solution)/shard_map/ppermute | solution.py:302
  33.5 10.0 %collective-permute-start.4 = (bf16[144,768]{1,0:T(8,128)(2,1)S(1)}, bf16[144,768]{1,0:T(8,128)(2,1)S(1)}, u32[]{:S(2)}, u32[]{:S(2)}) collective-permute-start(bf16[144,768]{1,0:T(8,128)(2,1)S(1)} %get-tuple-element.56), channel_id=1, source_target_pairs={{16,0},{17,1},{18,2},{19,3},{20,4},{21,5},{22,6},{23,7},{24,8},{25... | collective-permute-start | bytes 663560 | tf_op jit(solution)/shard_map/ppermute | solution.py:295
  37.8 10.3 %collective-permute-start.5 = (bf16[144,768]{1,0:T(8,128)(2,1)S(1)}, bf16[144,768]{1,0:T(8,128)(2,1)S(1)}, u32[]{:S(2)}, u32[]{:S(2)}) collective-permute-start(bf16[144,768]{1,0:T(8,128)(2,1)S(1)} %get-tuple-element.55), channel_id=1, source_target_pairs={{0,16},{1,17},{2,18},{3,19},{4,20},{5,21},{6,22},{7,23},{8,24},{9,... | collective-permute-start | bytes 663560 | tf_op jit(solution)/shard_map/ppermute | solution.py:296
  55.1 11.9 %collective-permute-start.6 = (bf16[128,896]{1,0:T(8,128)(2,1)S(1)}, bf16[128,896]{1,0:T(8,128)(2,1)S(1)}, u32[]{:S(2)}, u32[]{:S(2)}) collective-permute-start(bf16[128,896]{1,0:T(8,128)(2,1)S(1)} %get-tuple-element.52), channel_id=1, source_target_pairs={{16,0},{17,1},{18,2},{19,3},{20,4},{21,5},{22,6},{23,7},{24,8},{25... | collective-permute-start | bytes 688136 | tf_op jit(solution)/shard_map/ppermute | solution.py:307
  61.3 10.2 %collective-permute-start.7 = (bf16[128,896]{1,0:T(8,128)(2,1)S(1)}, bf16[128,896]{1,0:T(8,128)(2,1)S(1)}, u32[]{:S(2)}, u32[]{:S(2)}) collective-permute-start(bf16[128,896]{1,0:T(8,128)(2,1)S(1)} %get-tuple-element.53), channel_id=1, source_target_pairs={{0,16},{1,17},{2,18},{3,19},{4,20},{5,21},{6,22},{7,23},{8,24},{9,... | collective-permute-start | bytes 688136 | tf_op jit(solution)/shard_map/ppermute | solution.py:308
  91.4 1.4 %copy-start = (bf16[1024,768]{1,0:T(8,128)(2,1)S(1)}, bf16[1024,768]{1,0:T(8,128)(2,1)}, u32[]{:S(2)}) copy-start(bf16[1024,768]{1,0:T(8,128)(2,1)} %all-gather.2.cloned.1.call-done.weight) | copy-start | bytes 4718596
  92.8 2.5 %copy-start.1 = (bf16[1024,768]{1,0:T(8,128)(2,1)S(1)}, bf16[1024,768]{1,0:T(8,128)(2,1)}, u32[]{:S(2)}) copy-start(bf16[1024,768]{1,0:T(8,128)(2,1)} %all-gather.2.cloned.1.call-done.weight) | copy-start | bytes 4718596
  93.4 3.8 %collective-permute-start.8 = (bf16[512,512]{1,0:T(8,128)(2,1)S(1)}, bf16[512,512]{1,0:T(8,128)(2,1)S(1)}, u32[]{:S(2)}, u32[]{:S(2)}) collective-permute-start(bf16[512,512]{1,0:T(8,128)(2,1)S(1)} %shard_map.71), channel_id=1, source_target_pairs={{0,1},{1,0},{2,3},{3,2},{4,5},{5,4},{6,7},{7,6},{8,9},{9,8},{10,11... | collective-permute-start | bytes 1572872 | tf_op jit(solution)/shard_map/ppermute | solution.py:313
  96.0 15.5 %copy-start.2 = (bf16[512,384]{1,0:T(8,128)(2,1)S(1)}, bf16[512,384]{1,0:T(8,128)(2,1)}, u32[]{:S(2)}) copy-start(bf16[512,384]{1,0:T(8,128)(2,1)} %constant.172.clone.order) | copy-start | bytes 1179652
Sparse Core Ops, SparseCore 0:
  33.5 43.8 all-gather.1

commit v9 on v8

--- a/solution.py
+++ b/solution.py
@@ -123,40 +123,39 @@
                 refs[i][:, cols] = summed[i * TILE : (i + 1) * TILE].astype(jnp.bfloat16)
         else:
             stats = jnp.where(lane == h + 8, total, stats)
-            refs[0][:, cols] = summed
+            low = 0
+            for ref in refs[::2]:
+                ref[:, cols] = summed[low : low + ref.shape[0]]
+                low += ref.shape[0]
     if message:
         for i in range(query_count):
             refs[i][:, FEAT:] = stats[i * TILE : (i + 1) * TILE].astype(jnp.bfloat16)
     else:
-        refs[1][...] = stats
+        low = 0
+        for ref in refs[1::2]:
+            ref[...] = stats[low : low + ref.shape[0]]
+            low += ref.shape[0]
 
 
 VMEM = pl.BlockSpec(memory_space=pltpu.VMEM)
 
 
-def attention(queries, pieces, groups, state=None, message=False):
+def attention(queries, pieces, groups, state=(), message=False, parts=None):
     count = len(queries)
-    rows = count * TILE
     if message:
         out_shape = (jax.ShapeDtypeStruct((TILE, FEAT + HD), jnp.bfloat16),) * count
     else:
-        out_shape = (
-            jax.ShapeDtypeStruct((rows, FEAT), jnp.float32),
-            jax.ShapeDtypeStruct((rows, HD), jnp.float32),
+        out_shape = tuple(
+            jax.ShapeDtypeStruct((part * TILE, width), jnp.float32)
+            for part in parts or (count,)
+            for width in (FEAT, HD)
         )
-    in_specs = [VMEM] * (count + len(pieces))
-    operands = [*queries, *pieces]
-    if state is not None:
-        (total_rows, which), arrays = state
-        for array in arrays:
-            in_specs.append(pl.BlockSpec((rows, array.shape[1]), lambda i: (which, 0)))
-            operands.append(array)
+    operands = (*queries, *pieces, *state)
     pairs = count * len(groups)
     return pl.pallas_call(
-        functools.partial(attention_kernel, groups, count, state is not None, message),
-        grid=(1,),
+        functools.partial(attention_kernel, groups, count, bool(state), message),
         out_shape=out_shape,
-        in_specs=in_specs,
+        in_specs=[VMEM] * len(operands),
         out_specs=(VMEM,) * len(out_shape),
         compiler_params=pltpu.CompilerParams(vmem_limit_bytes=12 * 1024 * 1024),
         cost_estimate=pl.CostEstimate(
@@ -244,7 +243,7 @@
             out_specs=pl.BlockSpec((rows.shape[0], half), lambda i, c: (0, 0)),
         ),
         out_shape=jax.ShapeDtypeStruct((rows.shape[0], half), dtype),
-        compiler_params=pltpu.CompilerParams(vmem_limit_bytes=12 * 1024 * 1024),
+        compiler_params=pltpu.CompilerParams(vmem_limit_bytes=56 * 2**20),
         cost_estimate=pl.CostEstimate(
             flops=2 * rows.shape[0] * half * FEAT, bytes_accessed=3 * 2**20, transcendentals=0
         ),
@@ -302,11 +301,11 @@
     bm = lax.ppermute(line, ALL, second_axis(-1))
     near = [(n, 0, 3 * n) for n in range(3)]
     far = [(n, 2 * TILE * a, 3 * a + n + 1) for n in range(2) for a in range(3)]
-    state = attention((qp, qm, q0), (kv, ap, am), near)
-    op, om = attention((qp, qm), (bp, bm), far, ((3, 0), state), message=True)
+    *far_state, own_sum, own_stats = attention((qp, qm, q0), (kv, ap, am), near, parts=(2, 1))
+    op, om = attention((qp, qm), (bp, bm), far, far_state, message=True)
     back_p = lax.ppermute(om, ALL, row_axis(1))
     back_m = lax.ppermute(op, ALL, row_axis(-1))
-    o0, s0 = attention((q0,), (bp, bm), far, ((3, 2), state))
+    o0, s0 = attention((q0,), (bp, bm), far, (own_sum, own_stats))
     attended = merge(o0, s0, back_p, back_m)
     rows = lax.all_gather(attended, "x", tiled=True)
     other = project(rows, weight, 1 - core, jnp.bfloat16)

time: 120 us -> 125 us (1.042)
  Pallas kernels: 15.3 us -> 19.7 us
  other arithmetic: 0.56 us -> 2.51 us
  local copies, waits for them, and re-layouts: 5.51 us -> 4.08 us
    pallas_call x2, Pallas kernels: 1.21 us -> 5.7 us  [project(): pl.pallas_call(project_kernel, grid_spec=pltpu.PrefetchScalarGridSpec(num...]
    unnamed x16 -> x12, local copies, waits for them, and re-layouts: 3.3 us -> 1.88 us
    convert_element_type x1, other arithmetic: 0.16 us -> 1.43 us  [body(): columns = (mine + received.astype(jnp.float32)).astype(jnp.bfloat16)]
  transfers between devices with their start and end apart: 11 -> 11, of which waited for: 4 -> 3; matrix products, arithmetic and copies ran while one was open for 2% -> 3% of each run, Pallas kernels for 11% -> 12%
where the time goes in v9:
time: 125 us; the launch traced here: 124 us
  starting transfers between devices  36.3 us (29%)
  blocking collectives  34.1 us (27%)
  Pallas kernels  19.7 us (16%)
  waiting for transfers between devices  13.6 us (11%)
  between operations  13.6 us (11%)
  local copies, waits for them, and re-layouts  4.08 us (3%)
  other arithmetic  2.51 us (2%)
    all_gather x1, blocking collectives, body(): rows = lax.all_gather(attended, 'x', tiled=True)  19.9 us
    all_to_all x1, blocking collectives, body(): pieces = lax.all_to_all(columns.reshape(4, TILE, -1), 'x', 0, 0)  14.2 us
    pallas_call x3, Pallas kernels, attention(): pl.pallas_call(functools.partial(attention_kernel, groups, count, bool(st...  11.2 us
    all_to_all x1, starting transfers between devices, body(): lax.all_to_all(jnp.broadcast_to(out_weight.T, (8, SHARE, FEAT)), 'y', 0, 0)  6.98 us
    ppermute x1, starting transfers between devices, body(): back_p = lax.ppermute(om, ALL, row_axis(1))  6.23 us
    pallas_call x2, Pallas kernels, project(): pl.pallas_call(project_kernel, grid_spec=pltpu.PrefetchScalarGridSpec(num...  5.7 us
    ppermute x1, starting transfers between devices, body(): bm = lax.ppermute(line, ALL, second_axis(-1))  5.58 us
    ppermute x1, starting transfers between devices, body(): am = lax.ppermute(kv, ALL, first_axis(-1))  5.49 us
  transfers between devices with their start and end apart: 11, of which 3 were waited for; matrix products, arithmetic and copies ran while one was open for 3% of the time, Pallas kernels for 12%

profile of v9, /device:TPU:240, one launch (start us, length us, event | category | flops | bytes accessed | tf_op | source)
XLA Modules:
  0.0 124.0 jit_solution(12482501856708601136)
XLA Ops:
  6.5 0.0 copy-start.5
  6.5 0.0 copy-start.1
  6.5 0.9 copy-done.1
  7.5 0.0 copy-start.2
  7.5 0.9 copy-done.2
  8.4 0.0 copy-start.4
  8.4 0.5 shard_map.64.refs_0_.refs_3_
  8.9 1.9 %collective-permute-start = (bf16[256,768]{1,0:T(8,128)(2,1)S(1)}, bf16[256,768]{1,0:T(8,128)(2,1)S(1)}, u32[]{:S(2)}, u32[]{:S(2)}) collective-permute-start(bf16[256,768]{1,0:T(8,128)(2,1)S(1)} %shard_map.64.refs_0_.refs_3_), channel_id=1, source_target_pairs={{64,0},{3,1},{66,2},{5,3},{68,4},{7,5},{70,6},{9,7},{72,8},{11,9},... | collective-permute-start | bytes 1179656 | tf_op jit(solution)/shard_map/ppermute | solution.py:289
  10.8 5.5 %collective-permute-start.1 = (bf16[256,768]{1,0:T(8,128)(2,1)S(1)}, bf16[256,768]{1,0:T(8,128)(2,1)S(1)}, u32[]{:S(2)}, u32[]{:S(2)}) collective-permute-start(bf16[256,768]{1,0:T(8,128)(2,1)S(1)} %shard_map.64.refs_0_.refs_3_), channel_id=1, source_target_pairs={{1,3},{3,5},{5,7},{7,9},{9,11},{11,13},{13,15},{17,19},{19,21},{21... | collective-permute-start | bytes 1179656 | tf_op jit(solution)/shard_map/ppermute | solution.py:290
  16.3 1.4 %broadcast_in_dim.46 = bf16[8,12,768]{2,1,0:T(8,128)(2,1)} broadcast(bf16[12,768]{1,0:T(8,128)(2,1)} %bitcast.8), dimensions={1,2} | broadcast | bytes 165888 | tf_op jit(solution)/shard_map/broadcast_in_dim | solution.py:291
  17.8 7.0 %all-to-all-start = ((bf16[8,12,768]{2,1,0:T(8,128)(2,1)}), bf16[8,12,768]{2,1,0:T(8,128)(2,1)S(1)}, u32[]{:S(2)}, u32[]{:S(2)}) async-start(bf16[8,12,768]{2,1,0:T(8,128)(2,1)} %broadcast_in_dim.46), calls=%async_computation | async-start | bytes 393216 | tf_op jit(solution)/shard_map/all_to_all | solution.py:291
  24.8 0.0 all-gather.2.cloned.1.call-start
  24.8 0.0 copy-done.4
  24.8 0.2 compare_reduce_fusion
  25.0 0.0 copy-done.5
  25.1 0.1 fusion.4
  25.1 0.0 copy-start.3
  25.1 0.0 collective-permute-done.refs_1_.refs_4_
  25.1 0.0 collective-permute-done.1.refs_2_.refs_5_
  25.2 0.6 shard_map.65
  25.8 1.3 %collective-permute-start.2 = (bf16[768,768]{1,0:T(8,128)(2,1)S(1)}, bf16[768,768]{1,0:T(8,128)(2,1)}, u32[]{:S(2)}, u32[]{:S(2)}) collective-permute-start(bf16[768,768]{1,0:T(8,128)(2,1)S(1)} %shard_map.65), channel_id=1, source_target_pairs={{2,0},{65,1},{4,2},{67,3},{6,4},{69,5},{8,6},{71,7},{10,8},{73,9},... | collective-permute-start | bytes 3538952 | tf_op jit(solution)/shard_map/ppermute | solution.py:300
  27.1 5.6 %collective-permute-start.3 = (bf16[768,768]{1,0:T(8,128)(2,1)S(1)}, bf16[768,768]{1,0:T(8,128)(2,1)}, u32[]{:S(2)}, u32[]{:S(2)}) collective-permute-start(bf16[768,768]{1,0:T(8,128)(2,1)S(1)} %shard_map.65), channel_id=1, source_target_pairs={{0,2},{2,4},{4,6},{6,8},{8,10},{10,12},{12,14},{16,18},{18,20},{20... | collective-permute-start | bytes 3538952 | tf_op jit(solution)/shard_map/ppermute | solution.py:301
  32.6 0.0 all-to-all-done
  32.6 0.7 pad.13
  33.3 0.0 all-gather.2.cloned.1.call-update
  33.4 0.0 copy-done.3
  33.4 0.8 pad_maximum_fusion
  34.2 4.3 %collective-permute-start.4 = (bf16[144,768]{1,0:T(8,128)(2,1)}, bf16[144,768]{1,0:T(8,128)(2,1)S(1)}, u32[]{:S(2)}, u32[]{:S(2)}) collective-permute-start(bf16[144,768]{1,0:T(8,128)(2,1)} %get-tuple-element.60), channel_id=1, source_target_pairs={{16,0},{17,1},{18,2},{19,3},{20,4},{21,5},{22,6},{23,7},{24,8},{25... | collective-permute-start | bytes 663560 | tf_op jit(solution)/shard_map/ppermute | solution.py:294
  38.5 1.3 %collective-permute-start.5 = (bf16[144,768]{1,0:T(8,128)(2,1)S(1)}, bf16[144,768]{1,0:T(8,128)(2,1)S(1)}, u32[]{:S(2)}, u32[]{:S(2)}) collective-permute-start(bf16[144,768]{1,0:T(8,128)(2,1)S(1)} %get-tuple-element.59), channel_id=1, source_target_pairs={{0,16},{1,17},{2,18},{3,19},{4,20},{5,21},{6,22},{7,23},{8,24},{9,... | collective-permute-start | bytes 663560 | tf_op jit(solution)/shard_map/ppermute | solution.py:295
  39.8 4.7 %collective-permute-done.4.refs_0_ = bf16[144,768]{1,0:T(8,128)(2,1)S(1)} collective-permute-done((bf16[144,768]{1,0:T(8,128)(2,1)}, bf16[144,768]{1,0:T(8,128)(2,1)S(1)}, u32[]{:S(2)}, u32[]{:S(2)}) %collective-permute-start.4) | collective-permute-done | bytes 221216 | tf_op jit(solution)/shard_map/ppermute | solution.py:294
  44.5 4.3 %collective-permute-done.5.refs_1_ = bf16[144,768]{1,0:T(8,128)(2,1)S(1)} collective-permute-done((bf16[144,768]{1,0:T(8,128)(2,1)S(1)}, bf16[144,768]{1,0:T(8,128)(2,1)S(1)}, u32[]{:S(2)}, u32[]{:S(2)}) %collective-permute-start.5) | collective-permute-done | bytes 221216 | tf_op jit(solution)/shard_map/ppermute | solution.py:295
  48.8 2.1 %shard_map.66 = (f32[256,768]{1,0:T(8,128)S(1)}, f32[256,128]{1,0:T(8,128)S(1)}, f32[128,768]{1,0:T(8,128)S(1)}, f32[128,128]{1,0:T(8,128)S(1)}) custom-call(bf16[144,768]{1,0:T(8,128)(2,1)S(1)} %collective-permute-done.4.refs_0_, bf16[144,768]{1,0:T(8,128)(2,1)S(1)} %collective-permute-done.5.refs_1_, ...), custom_call_target="tpu_custom_call" | custom-call | flops 6794772480 | bytes 1179648 | tf_op jit(solution)/shard_map/pallas_call | solution.py:155
  50.9 0.0 collective-permute-done.2.refs_1_.refs_2_
  51.0 0.0 collective-permute-done.3.refs_2_.refs_3_
  51.0 4.8 %shard_map.68 = (bf16[128,896]{1,0:T(8,128)(2,1)S(1)}, bf16[128,896]{1,0:T(8,128)(2,1)S(1)}) custom-call(bf16[144,768]{1,0:T(8,128)(2,1)S(1)} %collective-permute-done.4.refs_0_, bf16[144,768]{1,0:T(8,128)(2,1)S(1)} %collective-permute-done.5.refs_1_, bf16[768,768]{1,0:T(8,128)(2,1)} %collective-permute-done.2.refs_1_.refs_2_, ...), custom_call_target="tpu_custom_call" | custom-call | flops 9059696640 | bytes 2359296 | tf_op jit(solution)/shard_map/pallas_call | solution.py:155
  55.7 6.2 %collective-permute-start.6 = (bf16[128,896]{1,0:T(8,128)(2,1)S(1)}, bf16[128,896]{1,0:T(8,128)(2,1)S(1)}, u32[]{:S(2)}, u32[]{:S(2)}) collective-permute-start(bf16[128,896]{1,0:T(8,128)(2,1)S(1)} %get-tuple-element.56), channel_id=1, source_target_pairs={{16,0},{17,1},{18,2},{19,3},{20,4},{21,5},{22,6},{23,7},{24,8},{25... | collective-permute-start | bytes 688136 | tf_op jit(solution)/shard_map/ppermute | solution.py:306
  62.0 1.3 %collective-permute-start.7 = (bf16[128,896]{1,0:T(8,128)(2,1)S(1)}, bf16[128,896]{1,0:T(8,128)(2,1)S(1)}, u32[]{:S(2)}, u32[]{:S(2)}) collective-permute-start(bf16[128,896]{1,0:T(8,128)(2,1)S(1)} %get-tuple-element.57), channel_id=1, source_target_pairs={{0,16},{1,17},{2,18},{3,19},{4,20},{5,21},{6,22},{7,23},{8,24},{9,... | collective-permute-start | bytes 688136 | tf_op jit(solution)/shard_map/ppermute | solution.py:307
  63.3 4.4 %shard_map.67 = (f32[128,768]{1,0:T(8,128)S(1)}, f32[128,128]{1,0:T(8,128)S(1)}) custom-call(bf16[144,768]{1,0:T(8,128)(2,1)S(1)} %get-tuple-element.61.refs_2_.refs_0_, bf16[768,768]{1,0:T(8,128)(2,1)} %collective-permute-done.2.refs_1_.refs_2_, bf16[768,768]{1,0:T(8,128)(2,1)} %collective-permute-done.3.refs_2_.refs_3_, ...), custom_call_target="tpu_custom_call" | custom-call | flops 4529848320 | bytes 2359296 | tf_op jit(solution)/shard_map/pallas_call | solution.py:155
  67.6 0.0 collective-permute-done.6.op
  67.6 4.6 %collective-permute-done.7.om = bf16[128,896]{1,0:T(8,128)(2,1)S(1)} collective-permute-done((bf16[128,896]{1,0:T(8,128)(2,1)S(1)}, bf16[128,896]{1,0:T(8,128)(2,1)S(1)}, u32[]{:S(2)}, u32[]{:S(2)}) %collective-permute-start.7) | collective-permute-done | bytes 229408 | tf_op jit(solution)/shard_map/ppermute | solution.py:307
  72.2 0.5 shard_map.69
  72.8 19.9 %all_gather.6.rows = bf16[512,768]{1,0:T(8,128)(2,1)} all-gather(bf16[128,768]{1,0:T(8,128)(2,1)S(1)} %shard_map.69), channel_id=1, replica_groups=mesh['z'=8,'y'=8,'x'=4,'head'=2] {'x'}, dimensions={0}, use_global_device_ids=true | all-gather | bytes 983040 | tf_op jit(solution)/shard_map/all_gather | solution.py:310
  92.7 0.0 all-gather.2.cloned.1.call-done.weight
  92.7 2.8 %shard_map.71 = bf16[512,512]{1,0:T(8,128)(2,1)} custom-call(s32[1]{0:T(128)} %bitcast.4._, bf16[512,768]{1,0:T(8,128)(2,1)} %all_gather.6.rows, bf16[1024,768]{1,0:T(8,128)(2,1)} %all-gather.2.cloned.1.call-done.weight), custom_call_target="tpu_custom_call" | custom-call | flops 402653184 | bytes 3145728 | tf_op jit(solution)/shard_map/pallas_call | solution.py:234
  95.5 1.9 %collective-permute-start.8 = (bf16[512,512]{1,0:T(8,128)(2,1)}, bf16[512,512]{1,0:T(8,128)(2,1)S(1)}, u32[]{:S(2)}, u32[]{:S(2)}) collective-permute-start(bf16[512,512]{1,0:T(8,128)(2,1)} %shard_map.71), channel_id=1, source_target_pairs={{0,1},{1,0},{2,3},{3,2},{4,5},{5,4},{6,7},{7,6},{8,9},{9,8},{10,11... | collective-permute-start | bytes 1572872 | tf_op jit(solution)/shard_map/ppermute | solution.py:312
  97.4 2.9 %shard_map.70 = f32[512,512]{1,0:T(8,128)} custom-call(s32[1]{0:T(128)} %bitcast._, bf16[512,768]{1,0:T(8,128)(2,1)} %all_gather.6.rows, bf16[1024,768]{1,0:T(8,128)(2,1)} %all-gather.2.cloned.1.call-done.weight), custom_call_target="tpu_custom_call" | custom-call | flops 402653184 | bytes 3145728 | tf_op jit(solution)/shard_map/pallas_call | solution.py:234
  100.3 0.0 copy-start
  100.3 0.0 collective-permute-done.8
  100.3 1.4 %add_convert_fusion = bf16[512,512]{1,0:T(8,128)(2,1)S(1)} fusion(f32[512,512]{1,0:T(8,128)} %shard_map.70, bf16[512,512]{1,0:T(8,128)(2,1)S(1)} %collective-permute-done.8), kind=kLoop, calls=%fused_computation | loop fusion | flops 786432 | bytes 2097152 | tf_op jit(solution)/shard_map/convert_element_type | solution.py:314
  101.8 14.2 %all_to_all.10.pieces = bf16[4,128,512]{2,1,0:T(8,128)(2,1)S(1)} all-to-all(bf16[4,128,512]{2,1,0:T(8,128)(2,1)S(1)} %bitcast.6), channel_id=1, replica_groups=mesh['z'=8,'y'=8,'x'=4,'head'=2] {'x'}, dimensions={0} | all-to-all | bytes 1048576 | tf_op jit(solution)/shard_map/all_to_all | solution.py:315
  116.0 0.0 copy-done
  116.0 1.2 shard_map.72
  (5 shorter events, 0.1 us)
Async XLA Ops:
  6.5 18.5 %copy-start.5 = (pred[16]{0:T(512)(128)(4,1)S(1)}, pred[16]{0:T(512)(128)(4,1)}, u32[]{:S(2)}) copy-start(pred[16]{0:T(512)(128)(4,1)} %constant.152.clone.1) | copy-start | bytes 52
  6.5 0.9 copy-start.1
  7.5 0.9 copy-start.2
  8.4 16.4 %copy-start.4 = (s32[1,27]{1,0:T(1,128)S(1)}, s32[1,27]{1,0:T(1,128)}, u32[]{:S(2)}) copy-start(s32[1,27]{1,0:T(1,128)} %param.15) | copy-start | bytes 328
  8.9 16.2 %collective-permute-start = (bf16[256,768]{1,0:T(8,128)(2,1)S(1)}, bf16[256,768]{1,0:T(8,128)(2,1)S(1)}, u32[]{:S(2)}, u32[]{:S(2)}) collective-permute-start(bf16[256,768]{1,0:T(8,128)(2,1)S(1)} %shard_map.64.refs_0_.refs_3_), channel_id=1, source_target_pairs={{64,0},{3,1},{66,2},{5,3},{68,4},{7,5},{70,6},{9,7},{72,8},{11,9},... | collective-permute-start | bytes 1179656 | tf_op jit(solution)/shard_map/ppermute | solution.py:289
  10.8 14.3 %collective-permute-start.1 = (bf16[256,768]{1,0:T(8,128)(2,1)S(1)}, bf16[256,768]{1,0:T(8,128)(2,1)S(1)}, u32[]{:S(2)}, u32[]{:S(2)}) collective-permute-start(bf16[256,768]{1,0:T(8,128)(2,1)S(1)} %shard_map.64.refs_0_.refs_3_), channel_id=1, source_target_pairs={{1,3},{3,5},{5,7},{7,9},{9,11},{11,13},{13,15},{17,19},{19,21},{21... | collective-permute-start | bytes 1179656 | tf_op jit(solution)/shard_map/ppermute | solution.py:290
  17.8 14.9 %all-to-all-start = ((bf16[8,12,768]{2,1,0:T(8,128)(2,1)}), bf16[8,12,768]{2,1,0:T(8,128)(2,1)S(1)}, u32[]{:S(2)}, u32[]{:S(2)}) async-start(bf16[8,12,768]{2,1,0:T(8,128)(2,1)} %broadcast_in_dim.46), calls=%async_computation | async-start | bytes 393216 | tf_op jit(solution)/shard_map/all_to_all | solution.py:291
  24.8 68.0 %all-gather.2.cloned.1.call-start = ((), (), s32[]{:S(2)}) async-start(), calls=%async_computation.2 | async-start | bytes 1769472 | tf_op jit(solution)/shard_map/all_gather | solution.py:299
  25.1 8.2 %copy-start.3 = (bf16[128,768]{1,0:T(8,128)(2,1)S(1)}, bf16[128,768]{1,0:T(8,128)(2,1)}, u32[]{:S(2)}) copy-start(bf16[128,768]{1,0:T(8,128)(2,1)} %param.12) | copy-start | bytes 589828
  25.8 25.2 %collective-permute-start.2 = (bf16[768,768]{1,0:T(8,128)(2,1)S(1)}, bf16[768,768]{1,0:T(8,128)(2,1)}, u32[]{:S(2)}, u32[]{:S(2)}) collective-permute-start(bf16[768,768]{1,0:T(8,128)(2,1)S(1)} %shard_map.65), channel_id=1, source_target_pairs={{2,0},{65,1},{4,2},{67,3},{6,4},{69,5},{8,6},{71,7},{10,8},{73,9},... | collective-permute-start | bytes 3538952 | tf_op jit(solution)/shard_map/ppermute | solution.py:300
  27.1 23.9 %collective-permute-start.3 = (bf16[768,768]{1,0:T(8,128)(2,1)S(1)}, bf16[768,768]{1,0:T(8,128)(2,1)}, u32[]{:S(2)}, u32[]{:S(2)}) collective-permute-start(bf16[768,768]{1,0:T(8,128)(2,1)S(1)} %shard_map.65), channel_id=1, source_target_pairs={{0,2},{2,4},{4,6},{6,8},{8,10},{10,12},{12,14},{16,18},{18,20},{20... | collective-permute-start | bytes 3538952 | tf_op jit(solution)/shard_map/ppermute | solution.py:301
  34.2 10.3 %collective-permute-start.4 = (bf16[144,768]{1,0:T(8,128)(2,1)}, bf16[144,768]{1,0:T(8,128)(2,1)S(1)}, u32[]{:S(2)}, u32[]{:S(2)}) collective-permute-start(bf16[144,768]{1,0:T(8,128)(2,1)} %get-tuple-element.60), channel_id=1, source_target_pairs={{16,0},{17,1},{18,2},{19,3},{20,4},{21,5},{22,6},{23,7},{24,8},{25... | collective-permute-start | bytes 663560 | tf_op jit(solution)/shard_map/ppermute | solution.py:294
  38.5 10.3 %collective-permute-start.5 = (bf16[144,768]{1,0:T(8,128)(2,1)S(1)}, bf16[144,768]{1,0:T(8,128)(2,1)S(1)}, u32[]{:S(2)}, u32[]{:S(2)}) collective-permute-start(bf16[144,768]{1,0:T(8,128)(2,1)S(1)} %get-tuple-element.59), channel_id=1, source_target_pairs={{0,16},{1,17},{2,18},{3,19},{4,20},{5,21},{6,22},{7,23},{8,24},{9,... | collective-permute-start | bytes 663560 | tf_op jit(solution)/shard_map/ppermute | solution.py:295
  55.7 11.9 %collective-permute-start.6 = (bf16[128,896]{1,0:T(8,128)(2,1)S(1)}, bf16[128,896]{1,0:T(8,128)(2,1)S(1)}, u32[]{:S(2)}, u32[]{:S(2)}) collective-permute-start(bf16[128,896]{1,0:T(8,128)(2,1)S(1)} %get-tuple-element.56), channel_id=1, source_target_pairs={{16,0},{17,1},{18,2},{19,3},{20,4},{21,5},{22,6},{23,7},{24,8},{25... | collective-permute-start | bytes 688136 | tf_op jit(solution)/shard_map/ppermute | solution.py:306
  62.0 10.3 %collective-permute-start.7 = (bf16[128,896]{1,0:T(8,128)(2,1)S(1)}, bf16[128,896]{1,0:T(8,128)(2,1)S(1)}, u32[]{:S(2)}, u32[]{:S(2)}) collective-permute-start(bf16[128,896]{1,0:T(8,128)(2,1)S(1)} %get-tuple-element.57), channel_id=1, source_target_pairs={{0,16},{1,17},{2,18},{3,19},{4,20},{5,21},{6,22},{7,23},{8,24},{9,... | collective-permute-start | bytes 688136 | tf_op jit(solution)/shard_map/ppermute | solution.py:307
  95.5 4.9 %collective-permute-start.8 = (bf16[512,512]{1,0:T(8,128)(2,1)}, bf16[512,512]{1,0:T(8,128)(2,1)S(1)}, u32[]{:S(2)}, u32[]{:S(2)}) collective-permute-start(bf16[512,512]{1,0:T(8,128)(2,1)} %shard_map.71), channel_id=1, source_target_pairs={{0,1},{1,0},{2,3},{3,2},{4,5},{5,4},{6,7},{7,6},{8,9},{9,8},{10,11... | collective-permute-start | bytes 1572872 | tf_op jit(solution)/shard_map/ppermute | solution.py:312
  100.3 15.6 %copy-start = (bf16[512,384]{1,0:T(8,128)(2,1)S(1)}, bf16[512,384]{1,0:T(8,128)(2,1)}, u32[]{:S(2)}) copy-start(bf16[512,384]{1,0:T(8,128)(2,1)} %constant.172.clone.order) | copy-start | bytes 1179652
Sparse Core Ops, SparseCore 0:
  33.5 43.8 all-gather.1

commit v10 on v5

--- a/solution.py
+++ b/solution.py
@@ -160,7 +160,7 @@
         out_specs=(VMEM,) * len(out_shape),
         compiler_params=pltpu.CompilerParams(vmem_limit_bytes=12 * 1024 * 1024),
         cost_estimate=pl.CostEstimate(
-            flops=160 * pairs * TILE * TILE * FEAT,
+            flops=60 * pairs * TILE * TILE * FEAT,
             bytes_accessed=len(groups) * 4 * TILE * FEAT,
             transcendentals=pairs * TILE * TILE * HEADS,
         ),
@@ -279,18 +279,18 @@
 def body(queries, keys, values, window, out_weight):
     my_tile = lax.axis_index(TOK)
     core = lax.axis_index("head")
-    kv = stacked(keys, values)
+    kv = lax.optimization_barrier(jnp.concatenate([keys, values]))
     ap = lax.ppermute(kv, ALL, first_axis(1))
     am = lax.ppermute(kv, ALL, first_axis(-1))
-    part = jnp.pad(out_weight.T, ((0, PAD - SHARE), (0, 0)))
-    line_y = lax.all_to_all(jnp.broadcast_to(part, (8, PAD, FEAT)), "y", 0, 0)
-    weight = lax.all_gather(line_y.reshape(-1, FEAT), "z", tiled=True)
+    line_y = lax.all_to_all(jnp.broadcast_to(out_weight.T, (8, SHARE, FEAT)), "y", 0, 0)
     bias = biases(window, my_tile, core)
     q0 = with_biases(queries, bias[0])
     qp = lax.ppermute(with_biases(queries, bias[2]), ALL, row_axis(1))
     qm = lax.ppermute(with_biases(queries, bias[1]), ALL, row_axis(-1))
-    ap, am, qp, qm = lax.optimization_barrier((ap, am, qp, qm))
     line = stacked(kv, ap, am)
+    line_y, _ = lax.optimization_barrier((line_y, line))
+    line_y = jnp.pad(line_y, ((0, 0), (0, PAD - SHARE), (0, 0)))
+    weight = lax.all_gather(line_y.reshape(-1, FEAT), "z", tiled=True)
     bp = lax.ppermute(line, ALL, second_axis(1))
     bm = lax.ppermute(line, ALL, second_axis(-1))
     near = [(n, 0, 3 * n) for n in range(3)]

time: 134 us -> 118 us (0.88)
  the two profiles are of different devices: /device:TPU:240 before, /device:TPU:304 now
where the time goes in v10:
time: 118 us
  blocking collectives  39 us (33%)
  starting transfers between devices  32.8 us (28%)
  Pallas kernels  14.2 us (12%)
  between operations  13.6 us (12%)
  waiting for transfers between devices  12.8 us (11%)
  local copies, waits for them, and re-layouts  3.64 us (3%)
  other arithmetic  1.63 us (1%)
    all_gather x1, blocking collectives, body(): rows = lax.all_gather(attended, 'x', tiled=True)  24.9 us
    all_to_all x1, blocking collectives, body(): pieces = lax.all_to_all(columns.reshape(4, TILE, -1), 'x', 0, 0)  14.1 us
    pallas_call x3, Pallas kernels, attention(): pl.pallas_call(functools.partial(attention_kernel, groups, count, state i...  11.3 us
    all_to_all x1, starting transfers between devices, body(): lax.all_to_all(jnp.broadcast_to(out_weight.T, (8, SHARE, FEAT)), 'y', 0, 0)  6.98 us
    ppermute x1, starting transfers between devices, body(): bm = lax.ppermute(line, ALL, second_axis(-1))  5.58 us
    ppermute x1, starting transfers between devices, body(): back_p = lax.ppermute(om, ALL, row_axis(1))  4.28 us
    ppermute x1, starting transfers between devices, body(): qp = lax.ppermute(with_biases(queries, bias[2]), ALL, row_axis(1))  4.28 us
    ppermute x1, waiting for transfers between devices, body(): qm = lax.ppermute(with_biases(queries, bias[1]), ALL, row_axis(-1))  4.21 us
  transfers between devices with their start and end apart: 11, of which 4 were waited for; matrix products, arithmetic and copies ran while one was open for 2% of the time, Pallas kernels for 11%

profile of v10, /device:TPU:304, one launch (start us, length us, event | category | flops | bytes accessed | tf_op | source)
XLA Modules:
  0.0 117.8 jit_solution(4623812019795569052)
XLA Ops:
  6.5 0.0 copy-start.5
  6.5 0.0 copy-start.4
  6.5 1.1 pad_maximum_fusion.refs_0_.refs_3_
  7.6 1.9 %collective-permute-start = (bf16[256,768]{1,0:T(8,128)(2,1)S(1)}, bf16[256,768]{1,0:T(8,128)(2,1)S(1)}, u32[]{:S(2)}, u32[]{:S(2)}) collective-permute-start(bf16[256,768]{1,0:T(8,128)(2,1)S(1)} %pad_maximum_fusion.refs_0_.refs_3_), channel_id=1, source_target_pairs={{64,0},{3,1},{66,2},{5,3},{68,4},{7,5},{70,6},{9,7},{72,8},{11,9},... | collective-permute-start | bytes 1179656 | tf_op jit(solution)/shard_map/ppermute | solution.py:283
  9.5 3.9 %collective-permute-start.1 = (bf16[256,768]{1,0:T(8,128)(2,1)S(1)}, bf16[256,768]{1,0:T(8,128)(2,1)S(1)}, u32[]{:S(2)}, u32[]{:S(2)}) collective-permute-start(bf16[256,768]{1,0:T(8,128)(2,1)S(1)} %pad_maximum_fusion.refs_0_.refs_3_), channel_id=1, source_target_pairs={{1,3},{3,5},{5,7},{7,9},{9,11},{11,13},{13,15},{17,19},{19,21},{21... | collective-permute-start | bytes 1179656 | tf_op jit(solution)/shard_map/ppermute | solution.py:284
  13.5 1.4 %broadcast_in_dim.46 = bf16[8,12,768]{2,1,0:T(8,128)(2,1)} broadcast(bf16[12,768]{1,0:T(8,128)(2,1)} %bitcast.8), dimensions={1,2} | broadcast | bytes 165888 | tf_op jit(solution)/shard_map/broadcast_in_dim | solution.py:285
  14.9 7.0 %all-to-all-start = ((bf16[8,12,768]{2,1,0:T(8,128)(2,1)}), bf16[8,12,768]{2,1,0:T(8,128)(2,1)S(1)}, u32[]{:S(2)}, u32[]{:S(2)}) async-start(bf16[8,12,768]{2,1,0:T(8,128)(2,1)} %broadcast_in_dim.46), calls=%async_computation | async-start | bytes 393216 | tf_op jit(solution)/shard_map/all_to_all | solution.py:285
  21.9 0.0 all-gather.2.cloned.1.call-start
  21.9 0.0 copy-done.4
  21.9 0.2 compare_reduce_fusion
  22.2 0.0 copy-done.5
  22.2 0.1 fusion.4
  22.3 0.0 copy-start.3
  22.3 0.0 collective-permute-done.refs_1_.refs_4_
  22.3 0.0 collective-permute-done.1.refs_2_.refs_5_
  22.3 0.1 shard_map.64
  22.4 1.3 %collective-permute-start.2 = (bf16[768,768]{1,0:T(8,128)(2,1)S(1)}, bf16[768,768]{1,0:T(8,128)(2,1)}, u32[]{:S(2)}, u32[]{:S(2)}) collective-permute-start(bf16[768,768]{1,0:T(8,128)(2,1)S(1)} %shard_map.64), channel_id=1, source_target_pairs={{2,0},{65,1},{4,2},{67,3},{6,4},{69,5},{8,6},{71,7},{10,8},{73,9},... | collective-permute-start | bytes 3538952 | tf_op jit(solution)/shard_map/ppermute | solution.py:294
  23.7 5.6 %collective-permute-start.3 = (bf16[768,768]{1,0:T(8,128)(2,1)S(1)}, bf16[768,768]{1,0:T(8,128)(2,1)}, u32[]{:S(2)}, u32[]{:S(2)}) collective-permute-start(bf16[768,768]{1,0:T(8,128)(2,1)S(1)} %shard_map.64), channel_id=1, source_target_pairs={{0,2},{2,4},{4,6},{6,8},{8,10},{10,12},{12,14},{16,18},{18,20},{20... | collective-permute-start | bytes 3538952 | tf_op jit(solution)/shard_map/ppermute | solution.py:295
  29.3 0.0 all-to-all-done
  29.3 0.7 pad.13
  30.0 0.0 all-gather.2.cloned.1.call-update
  30.0 0.0 copy-done.3
  30.0 0.1 pad_maximum_fusion.1
  30.2 4.3 %collective-permute-start.4 = (bf16[144,768]{1,0:T(8,128)(2,1)S(1)}, bf16[144,768]{1,0:T(8,128)(2,1)S(1)}, u32[]{:S(2)}, u32[]{:S(2)}) collective-permute-start(bf16[144,768]{1,0:T(8,128)(2,1)S(1)} %get-tuple-element.56), channel_id=1, source_target_pairs={{16,0},{17,1},{18,2},{19,3},{20,4},{21,5},{22,6},{23,7},{24,8},{25... | collective-permute-start | bytes 663560 | tf_op jit(solution)/shard_map/ppermute | solution.py:288
  34.4 1.3 %collective-permute-start.5 = (bf16[144,768]{1,0:T(8,128)(2,1)S(1)}, bf16[144,768]{1,0:T(8,128)(2,1)S(1)}, u32[]{:S(2)}, u32[]{:S(2)}) collective-permute-start(bf16[144,768]{1,0:T(8,128)(2,1)S(1)} %get-tuple-element.55), channel_id=1, source_target_pairs={{0,16},{1,17},{2,18},{3,19},{4,20},{5,21},{6,22},{7,23},{8,24},{9,... | collective-permute-start | bytes 663560 | tf_op jit(solution)/shard_map/ppermute | solution.py:289
  35.7 4.1 %collective-permute-done.4.refs_0_ = bf16[144,768]{1,0:T(8,128)(2,1)S(1)} collective-permute-done((bf16[144,768]{1,0:T(8,128)(2,1)S(1)}, bf16[144,768]{1,0:T(8,128)(2,1)S(1)}, u32[]{:S(2)}, u32[]{:S(2)}) %collective-permute-start.4) | collective-permute-done | bytes 221216 | tf_op jit(solution)/shard_map/ppermute | solution.py:288
  39.8 4.2 %collective-permute-done.5.refs_1_ = bf16[144,768]{1,0:T(8,128)(2,1)S(1)} collective-permute-done((bf16[144,768]{1,0:T(8,128)(2,1)S(1)}, bf16[144,768]{1,0:T(8,128)(2,1)S(1)}, u32[]{:S(2)}, u32[]{:S(2)}) %collective-permute-start.5) | collective-permute-done | bytes 221216 | tf_op jit(solution)/shard_map/ppermute | solution.py:289
  44.1 2.1 %shard_map.65 = (f32[384,768]{1,0:T(8,128)S(1)}, f32[384,128]{1,0:T(8,128)S(1)}) custom-call(bf16[144,768]{1,0:T(8,128)(2,1)S(1)} %collective-permute-done.4.refs_0_, bf16[144,768]{1,0:T(8,128)(2,1)S(1)} %collective-permute-done.5.refs_1_, bf16[144,768]{1,0:T(8,128)(2,1)S(1)} %get-tuple-element.57.refs_2_.refs_0_, ...), custom_call_target="tpu_custom_call" | custom-call | flops 6794772480 | bytes 1179648 | tf_op jit(solution)/shard_map/pallas_call | solution.py:155
  46.2 0.0 collective-permute-done.2.refs_1_.refs_2_
  46.2 0.0 collective-permute-done.3.refs_2_.refs_3_
  46.2 4.8 %shard_map.67 = (bf16[128,896]{1,0:T(8,128)(2,1)S(1)}, bf16[128,896]{1,0:T(8,128)(2,1)S(1)}) custom-call(bf16[144,768]{1,0:T(8,128)(2,1)S(1)} %collective-permute-done.4.refs_0_, bf16[144,768]{1,0:T(8,128)(2,1)S(1)} %collective-permute-done.5.refs_1_, bf16[768,768]{1,0:T(8,128)(2,1)} %collective-permute-done.2.refs_1_.refs_2_, ...), custom_call_target="tpu_custom_call" | custom-call | flops 9059696640 | bytes 2359296 | tf_op jit(solution)/shard_map/pallas_call | solution.py:155
  51.0 4.3 %collective-permute-start.6 = (bf16[128,896]{1,0:T(8,128)(2,1)S(1)}, bf16[128,896]{1,0:T(8,128)(2,1)S(1)}, u32[]{:S(2)}, u32[]{:S(2)}) collective-permute-start(bf16[128,896]{1,0:T(8,128)(2,1)S(1)} %get-tuple-element.52), channel_id=1, source_target_pairs={{16,0},{17,1},{18,2},{19,3},{20,4},{21,5},{22,6},{23,7},{24,8},{25... | collective-permute-start | bytes 688136 | tf_op jit(solution)/shard_map/ppermute | solution.py:300
  55.3 1.3 %collective-permute-start.7 = (bf16[128,896]{1,0:T(8,128)(2,1)S(1)}, bf16[128,896]{1,0:T(8,128)(2,1)S(1)}, u32[]{:S(2)}, u32[]{:S(2)}) collective-permute-start(bf16[128,896]{1,0:T(8,128)(2,1)S(1)} %get-tuple-element.53), channel_id=1, source_target_pairs={{0,16},{1,17},{2,18},{3,19},{4,20},{5,21},{6,22},{7,23},{8,24},{9,... | collective-permute-start | bytes 688136 | tf_op jit(solution)/shard_map/ppermute | solution.py:301
  56.6 4.4 %shard_map.66 = (f32[128,768]{1,0:T(8,128)S(1)}, f32[128,128]{1,0:T(8,128)S(1)}) custom-call(bf16[144,768]{1,0:T(8,128)(2,1)S(1)} %get-tuple-element.57.refs_2_.refs_0_, bf16[768,768]{1,0:T(8,128)(2,1)} %collective-permute-done.2.refs_1_.refs_2_, bf16[768,768]{1,0:T(8,128)(2,1)} %collective-permute-done.3.refs_2_.refs_3_, ...), custom_call_target="tpu_custom_call" | custom-call | flops 4529848320 | bytes 2359296 | tf_op jit(solution)/shard_map/pallas_call | solution.py:155
  60.9 0.0 collective-permute-done.6.op
  60.9 3.2 %collective-permute-done.7.om = bf16[128,896]{1,0:T(8,128)(2,1)S(1)} collective-permute-done((bf16[128,896]{1,0:T(8,128)(2,1)S(1)}, bf16[128,896]{1,0:T(8,128)(2,1)S(1)}, u32[]{:S(2)}, u32[]{:S(2)}) %collective-permute-start.7) | collective-permute-done | bytes 229408 | tf_op jit(solution)/shard_map/ppermute | solution.py:301
  64.2 0.5 shard_map.68
  64.7 24.9 %all_gather.6.rows = bf16[512,768]{1,0:T(8,128)(2,1)S(1)} all-gather(bf16[128,768]{1,0:T(8,128)(2,1)S(1)} %shard_map.68), channel_id=1, replica_groups=mesh['z'=8,'y'=8,'x'=4,'head'=2] {'x'}, dimensions={0}, use_global_device_ids=true | all-gather | bytes 983040 | tf_op jit(solution)/shard_map/all_gather | solution.py:304
  89.6 0.0 all-gather.2.cloned.1.call-done.weight
  89.6 0.0 copy-start
  89.6 1.4 %copy-done = bf16[1024,768]{1,0:T(8,128)(2,1)S(1)} copy-done((bf16[1024,768]{1,0:T(8,128)(2,1)S(1)}, bf16[1024,768]{1,0:T(8,128)(2,1)}, u32[]{:S(2)}) %copy-start) | copy-done | bytes 1572888
  91.0 0.0 copy-start.1
  91.0 0.6 shard_map.70
  91.6 1.9 %collective-permute-start.8 = (bf16[512,512]{1,0:T(8,128)(2,1)S(1)}, bf16[512,512]{1,0:T(8,128)(2,1)S(1)}, u32[]{:S(2)}, u32[]{:S(2)}) collective-permute-start(bf16[512,512]{1,0:T(8,128)(2,1)S(1)} %shard_map.70), channel_id=1, source_target_pairs={{0,1},{1,0},{2,3},{3,2},{4,5},{5,4},{6,7},{7,6},{8,9},{9,8},{10,11... | collective-permute-start | bytes 1572872 | tf_op jit(solution)/shard_map/ppermute | solution.py:306
  93.6 0.0 copy-done.1
  93.6 0.6 shard_map.69
  94.2 0.0 copy-start.2
  94.2 1.2 %collective-permute-done.8 = bf16[512,512]{1,0:T(8,128)(2,1)S(1)} collective-permute-done((bf16[512,512]{1,0:T(8,128)(2,1)S(1)}, bf16[512,512]{1,0:T(8,128)(2,1)S(1)}, u32[]{:S(2)}, u32[]{:S(2)}) %collective-permute-start.8) | collective-permute-done | bytes 524320 | tf_op jit(solution)/shard_map/ppermute | solution.py:306
  95.4 0.2 add_convert_fusion
  95.6 14.1 %all_to_all.10.pieces = bf16[4,128,512]{2,1,0:T(8,128)(2,1)S(1)} all-to-all(bf16[4,128,512]{2,1,0:T(8,128)(2,1)S(1)} %bitcast.6), channel_id=1, replica_groups=mesh['z'=8,'y'=8,'x'=4,'head'=2] {'x'}, dimensions={0} | all-to-all | bytes 1048576 | tf_op jit(solution)/shard_map/all_to_all | solution.py:309
  109.8 0.0 copy-done.2
  109.8 1.2 shard_map.71
  (5 shorter events, 0.1 us)
Async XLA Ops:
  6.5 15.6 %copy-start.5 = (pred[16]{0:T(512)(128)(4,1)S(1)}, pred[16]{0:T(512)(128)(4,1)}, u32[]{:S(2)}) copy-start(pred[16]{0:T(512)(128)(4,1)} %constant.152.clone.1) | copy-start | bytes 52
  6.5 15.4 %copy-start.4 = (s32[1,27]{1,0:T(1,128)S(1)}, s32[1,27]{1,0:T(1,128)}, u32[]{:S(2)}) copy-start(s32[1,27]{1,0:T(1,128)} %param.15) | copy-start | bytes 328
  7.6 14.7 %collective-permute-start = (bf16[256,768]{1,0:T(8,128)(2,1)S(1)}, bf16[256,768]{1,0:T(8,128)(2,1)S(1)}, u32[]{:S(2)}, u32[]{:S(2)}) collective-permute-start(bf16[256,768]{1,0:T(8,128)(2,1)S(1)} %pad_maximum_fusion.refs_0_.refs_3_), channel_id=1, source_target_pairs={{64,0},{3,1},{66,2},{5,3},{68,4},{7,5},{70,6},{9,7},{72,8},{11,9},... | collective-permute-start | bytes 1179656 | tf_op jit(solution)/shard_map/ppermute | solution.py:283
  9.5 12.7 %collective-permute-start.1 = (bf16[256,768]{1,0:T(8,128)(2,1)S(1)}, bf16[256,768]{1,0:T(8,128)(2,1)S(1)}, u32[]{:S(2)}, u32[]{:S(2)}) collective-permute-start(bf16[256,768]{1,0:T(8,128)(2,1)S(1)} %pad_maximum_fusion.refs_0_.refs_3_), channel_id=1, source_target_pairs={{1,3},{3,5},{5,7},{7,9},{9,11},{11,13},{13,15},{17,19},{19,21},{21... | collective-permute-start | bytes 1179656 | tf_op jit(solution)/shard_map/ppermute | solution.py:284
  14.9 14.4 %all-to-all-start = ((bf16[8,12,768]{2,1,0:T(8,128)(2,1)}), bf16[8,12,768]{2,1,0:T(8,128)(2,1)S(1)}, u32[]{:S(2)}, u32[]{:S(2)}) async-start(bf16[8,12,768]{2,1,0:T(8,128)(2,1)} %broadcast_in_dim.46), calls=%async_computation | async-start | bytes 393216 | tf_op jit(solution)/shard_map/all_to_all | solution.py:285
  21.9 67.7 %all-gather.2.cloned.1.call-start = ((), (), s32[]{:S(2)}) async-start(), calls=%async_computation.2 | async-start | bytes 1769472 | tf_op jit(solution)/shard_map/all_gather | solution.py:293
  22.3 7.7 %copy-start.3 = (bf16[128,768]{1,0:T(8,128)(2,1)S(1)}, bf16[128,768]{1,0:T(8,128)(2,1)}, u32[]{:S(2)}) copy-start(bf16[128,768]{1,0:T(8,128)(2,1)} %param.12) | copy-start | bytes 589828
  22.4 23.8 %collective-permute-start.2 = (bf16[768,768]{1,0:T(8,128)(2,1)S(1)}, bf16[768,768]{1,0:T(8,128)(2,1)}, u32[]{:S(2)}, u32[]{:S(2)}) collective-permute-start(bf16[768,768]{1,0:T(8,128)(2,1)S(1)} %shard_map.64), channel_id=1, source_target_pairs={{2,0},{65,1},{4,2},{67,3},{6,4},{69,5},{8,6},{71,7},{10,8},{73,9},... | collective-permute-start | bytes 3538952 | tf_op jit(solution)/shard_map/ppermute | solution.py:294
  23.7 22.5 %collective-permute-start.3 = (bf16[768,768]{1,0:T(8,128)(2,1)S(1)}, bf16[768,768]{1,0:T(8,128)(2,1)}, u32[]{:S(2)}, u32[]{:S(2)}) collective-permute-start(bf16[768,768]{1,0:T(8,128)(2,1)S(1)} %shard_map.64), channel_id=1, source_target_pairs={{0,2},{2,4},{4,6},{6,8},{8,10},{10,12},{12,14},{16,18},{18,20},{20... | collective-permute-start | bytes 3538952 | tf_op jit(solution)/shard_map/ppermute | solution.py:295
  30.2 9.7 %collective-permute-start.4 = (bf16[144,768]{1,0:T(8,128)(2,1)S(1)}, bf16[144,768]{1,0:T(8,128)(2,1)S(1)}, u32[]{:S(2)}, u32[]{:S(2)}) collective-permute-start(bf16[144,768]{1,0:T(8,128)(2,1)S(1)} %get-tuple-element.56), channel_id=1, source_target_pairs={{16,0},{17,1},{18,2},{19,3},{20,4},{21,5},{22,6},{23,7},{24,8},{25... | collective-permute-start | bytes 663560 | tf_op jit(solution)/shard_map/ppermute | solution.py:288
  34.4 9.6 %collective-permute-start.5 = (bf16[144,768]{1,0:T(8,128)(2,1)S(1)}, bf16[144,768]{1,0:T(8,128)(2,1)S(1)}, u32[]{:S(2)}, u32[]{:S(2)}) collective-permute-start(bf16[144,768]{1,0:T(8,128)(2,1)S(1)} %get-tuple-element.55), channel_id=1, source_target_pairs={{0,16},{1,17},{2,18},{3,19},{4,20},{5,21},{6,22},{7,23},{8,24},{9,... | collective-permute-start | bytes 663560 | tf_op jit(solution)/shard_map/ppermute | solution.py:289
  51.0 10.0 %collective-permute-start.6 = (bf16[128,896]{1,0:T(8,128)(2,1)S(1)}, bf16[128,896]{1,0:T(8,128)(2,1)S(1)}, u32[]{:S(2)}, u32[]{:S(2)}) collective-permute-start(bf16[128,896]{1,0:T(8,128)(2,1)S(1)} %get-tuple-element.52), channel_id=1, source_target_pairs={{16,0},{17,1},{18,2},{19,3},{20,4},{21,5},{22,6},{23,7},{24,8},{25... | collective-permute-start | bytes 688136 | tf_op jit(solution)/shard_map/ppermute | solution.py:300
  55.3 8.9 %collective-permute-start.7 = (bf16[128,896]{1,0:T(8,128)(2,1)S(1)}, bf16[128,896]{1,0:T(8,128)(2,1)S(1)}, u32[]{:S(2)}, u32[]{:S(2)}) collective-permute-start(bf16[128,896]{1,0:T(8,128)(2,1)S(1)} %get-tuple-element.53), channel_id=1, source_target_pairs={{0,16},{1,17},{2,18},{3,19},{4,20},{5,21},{6,22},{7,23},{8,24},{9,... | collective-permute-start | bytes 688136 | tf_op jit(solution)/shard_map/ppermute | solution.py:301
  89.6 1.4 %copy-start = (bf16[1024,768]{1,0:T(8,128)(2,1)S(1)}, bf16[1024,768]{1,0:T(8,128)(2,1)}, u32[]{:S(2)}) copy-start(bf16[1024,768]{1,0:T(8,128)(2,1)} %all-gather.2.cloned.1.call-done.weight) | copy-start | bytes 4718596
  91.0 2.5 %copy-start.1 = (bf16[1024,768]{1,0:T(8,128)(2,1)S(1)}, bf16[1024,768]{1,0:T(8,128)(2,1)}, u32[]{:S(2)}) copy-start(bf16[1024,768]{1,0:T(8,128)(2,1)} %all-gather.2.cloned.1.call-done.weight) | copy-start | bytes 4718596
  91.6 3.8 %collective-permute-start.8 = (bf16[512,512]{1,0:T(8,128)(2,1)S(1)}, bf16[512,512]{1,0:T(8,128)(2,1)S(1)}, u32[]{:S(2)}, u32[]{:S(2)}) collective-permute-start(bf16[512,512]{1,0:T(8,128)(2,1)S(1)} %shard_map.70), channel_id=1, source_target_pairs={{0,1},{1,0},{2,3},{3,2},{4,5},{5,4},{6,7},{7,6},{8,9},{9,8},{10,11... | collective-permute-start | bytes 1572872 | tf_op jit(solution)/shard_map/ppermute | solution.py:306
  94.2 15.6 %copy-start.2 = (bf16[512,384]{1,0:T(8,128)(2,1)S(1)}, bf16[512,384]{1,0:T(8,128)(2,1)}, u32[]{:S(2)}) copy-start(bf16[512,384]{1,0:T(8,128)(2,1)} %constant.172.clone.order) | copy-start | bytes 1179652
Sparse Core Ops, SparseCore 0:
  30.1 42.5 all-gather.1

commit v11 on v10

--- a/solution.py
+++ b/solution.py
@@ -216,7 +216,7 @@
     )(*operands)
 
 
-def project_kernel(_, rows, weight, out):
+def project_kernel(rows, weight, out):
     product = lax.dot_general(
         rows[...], weight[...], (((1,), (1,)), ((), ())), preferred_element_type=jnp.float32
     )
@@ -225,23 +225,17 @@
 
 def project(rows, weight, which, dtype):
     half = weight.shape[0] // 2
+    part = lax.dynamic_slice_in_dim(weight, which * half, half, 0)
     return pl.pallas_call(
         project_kernel,
-        grid_spec=pltpu.PrefetchScalarGridSpec(
-            num_scalar_prefetch=1,
-            grid=(1,),
-            in_specs=[
-                pl.BlockSpec(rows.shape, lambda i, c: (0, 0)),
-                pl.BlockSpec((half, FEAT), lambda i, c: (c[0], 0)),
-            ],
-            out_specs=pl.BlockSpec((rows.shape[0], half), lambda i, c: (0, 0)),
-        ),
         out_shape=jax.ShapeDtypeStruct((rows.shape[0], half), dtype),
+        in_specs=[VMEM, VMEM],
+        out_specs=VMEM,
         compiler_params=pltpu.CompilerParams(vmem_limit_bytes=12 * 1024 * 1024),
         cost_estimate=pl.CostEstimate(
             flops=2 * rows.shape[0] * half * FEAT, bytes_accessed=3 * 2**20, transcendentals=0
         ),
-    )(which[None], rows, weight)
+    )(rows, part)
 
 
 PAD = 16
@@ -304,6 +298,7 @@
     rows = lax.all_gather(attended, "x", tiled=True)
     other = project(rows, weight, 1 - core, jnp.bfloat16)
     received = lax.ppermute(other, "head", [(0, 1), (1, 0)])
+    weight, _ = lax.optimization_barrier((weight, other))
     mine = project(rows, weight, core, jnp.float32)
     columns = (mine + received.astype(jnp.float32)).astype(jnp.bfloat16)
     pieces = lax.all_to_all(columns.reshape(4, TILE, -1), "x", 0, 0)

time: 118 us -> 119 us (level)
    unnamed x12 -> x10, local copies, waits for them, and re-layouts: 1.43 us -> 0.02 us
    dynamic_slice x0 -> x2, local copies, waits for them, and re-layouts: none -> 1.24 us  [project(): part = lax.dynamic_slice_in_dim(weight, which * half, half, 0)]
where the time goes in v11:
time: 119 us
  blocking collectives  39 us (33%)
  starting transfers between devices  32.8 us (28%)
  Pallas kernels  14.2 us (12%)
  between operations  13.7 us (12%)
  waiting for transfers between devices  12.9 us (11%)
  local copies, waits for them, and re-layouts  3.48 us (3%)
  other arithmetic  2.67 us (2%)
    all_gather x1, blocking collectives, body(): rows = lax.all_gather(attended, 'x', tiled=True)  24.8 us
    all_to_all x1, blocking collectives, body(): pieces = lax.all_to_all(columns.reshape(4, TILE, -1), 'x', 0, 0)  14.2 us
    pallas_call x3, Pallas kernels, attention(): pl.pallas_call(functools.partial(attention_kernel, groups, count, state i...  11.3 us
    all_to_all x1, starting transfers between devices, body(): lax.all_to_all(jnp.broadcast_to(out_weight.T, (8, SHARE, FEAT)), 'y', 0, 0)  6.98 us
    ppermute x1, starting transfers between devices, body(): bm = lax.ppermute(line, ALL, second_axis(-1))  5.59 us
    ppermute x1, starting transfers between devices, body(): back_p = lax.ppermute(om, ALL, row_axis(1))  4.28 us
    ppermute x1, starting transfers between devices, body(): qp = lax.ppermute(with_biases(queries, bias[2]), ALL, row_axis(1))  4.28 us
    ppermute x1, waiting for transfers between devices, body(): qm = lax.ppermute(with_biases(queries, bias[1]), ALL, row_axis(-1))  4.21 us
  transfers between devices with their start and end apart: 11, of which 4 were waited for; matrix products, arithmetic and copies ran while one was open for 2% of the time, Pallas kernels for 11%

profile of v11, /device:TPU:304, one launch (start us, length us, event | category | flops | bytes accessed | tf_op | source)
XLA Modules:
  0.0 118.7 jit_solution(11973083123868754675)
XLA Ops:
  6.5 0.0 copy-start.4
  6.5 0.0 copy-start.3
  6.5 1.1 pad_maximum_fusion.refs_0_.refs_3_
  7.6 1.9 %collective-permute-start = (bf16[256,768]{1,0:T(8,128)(2,1)S(1)}, bf16[256,768]{1,0:T(8,128)(2,1)S(1)}, u32[]{:S(2)}, u32[]{:S(2)}) collective-permute-start(bf16[256,768]{1,0:T(8,128)(2,1)S(1)} %pad_maximum_fusion.refs_0_.refs_3_), channel_id=1, source_target_pairs={{64,0},{3,1},{66,2},{5,3},{68,4},{7,5},{70,6},{9,7},{72,8},{11,9},... | collective-permute-start | bytes 1179656 | tf_op jit(solution)/shard_map/ppermute | solution.py:277
  9.5 3.9 %collective-permute-start.1 = (bf16[256,768]{1,0:T(8,128)(2,1)S(1)}, bf16[256,768]{1,0:T(8,128)(2,1)S(1)}, u32[]{:S(2)}, u32[]{:S(2)}) collective-permute-start(bf16[256,768]{1,0:T(8,128)(2,1)S(1)} %pad_maximum_fusion.refs_0_.refs_3_), channel_id=1, source_target_pairs={{1,3},{3,5},{5,7},{7,9},{9,11},{11,13},{13,15},{17,19},{19,21},{21... | collective-permute-start | bytes 1179656 | tf_op jit(solution)/shard_map/ppermute | solution.py:278
  13.5 1.4 %broadcast_in_dim.39 = bf16[8,12,768]{2,1,0:T(8,128)(2,1)} broadcast(bf16[12,768]{1,0:T(8,128)(2,1)} %bitcast.6), dimensions={1,2} | broadcast | bytes 165888 | tf_op jit(solution)/shard_map/broadcast_in_dim | solution.py:279
  14.9 7.0 %all-to-all-start = ((bf16[8,12,768]{2,1,0:T(8,128)(2,1)}), bf16[8,12,768]{2,1,0:T(8,128)(2,1)S(1)}, u32[]{:S(2)}, u32[]{:S(2)}) async-start(bf16[8,12,768]{2,1,0:T(8,128)(2,1)} %broadcast_in_dim.39), calls=%async_computation | async-start | bytes 393216 | tf_op jit(solution)/shard_map/all_to_all | solution.py:279
  21.9 0.0 all-gather.2.cloned.1.call-start
  21.9 0.0 copy-done.3
  21.9 0.2 compare_reduce_fusion
  22.2 0.0 copy-done.4
  22.2 0.1 fusion.4
  22.3 0.0 copy-start.2
  22.3 0.0 collective-permute-done.refs_1_.refs_4_
  22.3 0.0 collective-permute-done.1.refs_2_.refs_5_
  22.3 0.1 shard_map.64
  22.4 1.3 %collective-permute-start.2 = (bf16[768,768]{1,0:T(8,128)(2,1)S(1)}, bf16[768,768]{1,0:T(8,128)(2,1)}, u32[]{:S(2)}, u32[]{:S(2)}) collective-permute-start(bf16[768,768]{1,0:T(8,128)(2,1)S(1)} %shard_map.64), channel_id=1, source_target_pairs={{2,0},{65,1},{4,2},{67,3},{6,4},{69,5},{8,6},{71,7},{10,8},{73,9},... | collective-permute-start | bytes 3538952 | tf_op jit(solution)/shard_map/ppermute | solution.py:288
  23.7 5.6 %collective-permute-start.3 = (bf16[768,768]{1,0:T(8,128)(2,1)S(1)}, bf16[768,768]{1,0:T(8,128)(2,1)}, u32[]{:S(2)}, u32[]{:S(2)}) collective-permute-start(bf16[768,768]{1,0:T(8,128)(2,1)S(1)} %shard_map.64), channel_id=1, source_target_pairs={{0,2},{2,4},{4,6},{6,8},{8,10},{10,12},{12,14},{16,18},{18,20},{20... | collective-permute-start | bytes 3538952 | tf_op jit(solution)/shard_map/ppermute | solution.py:289
  29.3 0.0 all-to-all-done
  29.3 0.7 pad.13
  30.0 0.0 all-gather.2.cloned.1.call-update
  30.0 0.0 copy-done.2
  30.0 0.1 pad_maximum_fusion.1
  30.2 4.3 %collective-permute-start.4 = (bf16[144,768]{1,0:T(8,128)(2,1)S(1)}, bf16[144,768]{1,0:T(8,128)(2,1)S(1)}, u32[]{:S(2)}, u32[]{:S(2)}) collective-permute-start(bf16[144,768]{1,0:T(8,128)(2,1)S(1)} %get-tuple-element.58), channel_id=1, source_target_pairs={{16,0},{17,1},{18,2},{19,3},{20,4},{21,5},{22,6},{23,7},{24,8},{25... | collective-permute-start | bytes 663560 | tf_op jit(solution)/shard_map/ppermute | solution.py:282
  34.4 1.3 %collective-permute-start.5 = (bf16[144,768]{1,0:T(8,128)(2,1)S(1)}, bf16[144,768]{1,0:T(8,128)(2,1)S(1)}, u32[]{:S(2)}, u32[]{:S(2)}) collective-permute-start(bf16[144,768]{1,0:T(8,128)(2,1)S(1)} %get-tuple-element.57), channel_id=1, source_target_pairs={{0,16},{1,17},{2,18},{3,19},{4,20},{5,21},{6,22},{7,23},{8,24},{9,... | collective-permute-start | bytes 663560 | tf_op jit(solution)/shard_map/ppermute | solution.py:283
  35.7 4.1 %collective-permute-done.4.refs_0_ = bf16[144,768]{1,0:T(8,128)(2,1)S(1)} collective-permute-done((bf16[144,768]{1,0:T(8,128)(2,1)S(1)}, bf16[144,768]{1,0:T(8,128)(2,1)S(1)}, u32[]{:S(2)}, u32[]{:S(2)}) %collective-permute-start.4) | collective-permute-done | bytes 221216 | tf_op jit(solution)/shard_map/ppermute | solution.py:282
  39.8 4.2 %collective-permute-done.5.refs_1_ = bf16[144,768]{1,0:T(8,128)(2,1)S(1)} collective-permute-done((bf16[144,768]{1,0:T(8,128)(2,1)S(1)}, bf16[144,768]{1,0:T(8,128)(2,1)S(1)}, u32[]{:S(2)}, u32[]{:S(2)}) %collective-permute-start.5) | collective-permute-done | bytes 221216 | tf_op jit(solution)/shard_map/ppermute | solution.py:283
  44.1 2.1 %shard_map.65 = (f32[384,768]{1,0:T(8,128)S(1)}, f32[384,128]{1,0:T(8,128)S(1)}) custom-call(bf16[144,768]{1,0:T(8,128)(2,1)S(1)} %collective-permute-done.4.refs_0_, bf16[144,768]{1,0:T(8,128)(2,1)S(1)} %collective-permute-done.5.refs_1_, bf16[144,768]{1,0:T(8,128)(2,1)S(1)} %get-tuple-element.59.refs_2_.refs_0_, ...), custom_call_target="tpu_custom_call" | custom-call | flops 6794772480 | bytes 1179648 | tf_op jit(solution)/shard_map/pallas_call | solution.py:155
  46.2 0.0 collective-permute-done.2.refs_1_.refs_2_
  46.2 0.0 collective-permute-done.3.refs_2_.refs_3_
  46.2 4.8 %shard_map.67 = (bf16[128,896]{1,0:T(8,128)(2,1)S(1)}, bf16[128,896]{1,0:T(8,128)(2,1)S(1)}) custom-call(bf16[144,768]{1,0:T(8,128)(2,1)S(1)} %collective-permute-done.4.refs_0_, bf16[144,768]{1,0:T(8,128)(2,1)S(1)} %collective-permute-done.5.refs_1_, bf16[768,768]{1,0:T(8,128)(2,1)} %collective-permute-done.2.refs_1_.refs_2_, ...), custom_call_target="tpu_custom_call" | custom-call | flops 9059696640 | bytes 2359296 | tf_op jit(solution)/shard_map/pallas_call | solution.py:155
  51.0 4.3 %collective-permute-start.6 = (bf16[128,896]{1,0:T(8,128)(2,1)S(1)}, bf16[128,896]{1,0:T(8,128)(2,1)S(1)}, u32[]{:S(2)}, u32[]{:S(2)}) collective-permute-start(bf16[128,896]{1,0:T(8,128)(2,1)S(1)} %get-tuple-element.53), channel_id=1, source_target_pairs={{16,0},{17,1},{18,2},{19,3},{20,4},{21,5},{22,6},{23,7},{24,8},{25... | collective-permute-start | bytes 688136 | tf_op jit(solution)/shard_map/ppermute | solution.py:294
  55.3 1.3 %collective-permute-start.7 = (bf16[128,896]{1,0:T(8,128)(2,1)S(1)}, bf16[128,896]{1,0:T(8,128)(2,1)S(1)}, u32[]{:S(2)}, u32[]{:S(2)}) collective-permute-start(bf16[128,896]{1,0:T(8,128)(2,1)S(1)} %get-tuple-element.54), channel_id=1, source_target_pairs={{0,16},{1,17},{2,18},{3,19},{4,20},{5,21},{6,22},{7,23},{8,24},{9,... | collective-permute-start | bytes 688136 | tf_op jit(solution)/shard_map/ppermute | solution.py:295
  56.6 4.4 %shard_map.66 = (f32[128,768]{1,0:T(8,128)S(1)}, f32[128,128]{1,0:T(8,128)S(1)}) custom-call(bf16[144,768]{1,0:T(8,128)(2,1)S(1)} %get-tuple-element.59.refs_2_.refs_0_, bf16[768,768]{1,0:T(8,128)(2,1)} %collective-permute-done.2.refs_1_.refs_2_, bf16[768,768]{1,0:T(8,128)(2,1)} %collective-permute-done.3.refs_2_.refs_3_, ...), custom_call_target="tpu_custom_call" | custom-call | flops 4529848320 | bytes 2359296 | tf_op jit(solution)/shard_map/pallas_call | solution.py:155
  61.0 0.0 collective-permute-done.6.op
  61.0 3.2 %collective-permute-done.7.om = bf16[128,896]{1,0:T(8,128)(2,1)S(1)} collective-permute-done((bf16[128,896]{1,0:T(8,128)(2,1)S(1)}, bf16[128,896]{1,0:T(8,128)(2,1)S(1)}, u32[]{:S(2)}, u32[]{:S(2)}) %collective-permute-start.7) | collective-permute-done | bytes 229408 | tf_op jit(solution)/shard_map/ppermute | solution.py:295
  64.2 0.5 shard_map.68
  64.7 24.8 %all_gather.6.rows = bf16[512,768]{1,0:T(8,128)(2,1)S(1)} all-gather(bf16[128,768]{1,0:T(8,128)(2,1)S(1)} %shard_map.68), channel_id=1, replica_groups=mesh['z'=8,'y'=8,'x'=4,'head'=2] {'x'}, dimensions={0}, use_global_device_ids=true | all-gather | bytes 983040 | tf_op jit(solution)/shard_map/all_gather | solution.py:298
  89.6 0.0 all-gather.2.cloned.1.call-done
  89.6 1.2 constant_dynamic-slice_fusion.1.weight
  90.8 0.0 copy-start.1
  90.8 0.6 shard_map.69
  91.4 1.9 %collective-permute-start.8 = (bf16[512,512]{1,0:T(8,128)(2,1)S(1)}, bf16[512,512]{1,0:T(8,128)(2,1)}, u32[]{:S(2)}, u32[]{:S(2)}) collective-permute-start(bf16[512,512]{1,0:T(8,128)(2,1)S(1)} %shard_map.69), channel_id=1, source_target_pairs={{0,1},{1,0},{2,3},{3,2},{4,5},{5,4},{6,7},{7,6},{8,9},{9,8},{10,11... | collective-permute-start | bytes 1572872 | tf_op jit(solution)/shard_map/ppermute | solution.py:300
  93.3 0.0 copy-done.1
  93.3 0.1 constant_dynamic-slice_fusion.weight
  93.4 0.6 shard_map.70
  94.0 0.0 copy-start
  94.0 1.3 %collective-permute-done.8 = bf16[512,512]{1,0:T(8,128)(2,1)} collective-permute-done((bf16[512,512]{1,0:T(8,128)(2,1)S(1)}, bf16[512,512]{1,0:T(8,128)(2,1)}, u32[]{:S(2)}, u32[]{:S(2)}) %collective-permute-start.8) | collective-permute-done | bytes 524320 | tf_op jit(solution)/shard_map/ppermute | solution.py:300
  95.3 1.2 %add_convert_fusion = bf16[512,512]{1,0:T(8,128)(2,1)S(1)} fusion(f32[512,512]{1,0:T(8,128)S(1)} %shard_map.70, bf16[512,512]{1,0:T(8,128)(2,1)} %collective-permute-done.8), kind=kLoop, calls=%fused_computation | loop fusion | flops 786432 | bytes 2097152 | tf_op jit(solution)/shard_map/convert_element_type | solution.py:303
  96.5 14.2 %all_to_all.10.pieces = bf16[4,128,512]{2,1,0:T(8,128)(2,1)S(1)} all-to-all(bf16[4,128,512]{2,1,0:T(8,128)(2,1)S(1)} %bitcast.4), channel_id=1, replica_groups=mesh['z'=8,'y'=8,'x'=4,'head'=2] {'x'}, dimensions={0} | all-to-all | bytes 1048576 | tf_op jit(solution)/shard_map/all_to_all | solution.py:304
  110.7 0.0 copy-done
  110.7 1.2 shard_map.71
  (5 shorter events, 0.1 us)
Async XLA Ops:
  6.5 15.6 %copy-start.4 = (pred[16]{0:T(512)(128)(4,1)S(1)}, pred[16]{0:T(512)(128)(4,1)}, u32[]{:S(2)}) copy-start(pred[16]{0:T(512)(128)(4,1)} %constant.153.clone.1) | copy-start | bytes 52
  6.5 15.4 %copy-start.3 = (s32[1,27]{1,0:T(1,128)S(1)}, s32[1,27]{1,0:T(1,128)}, u32[]{:S(2)}) copy-start(s32[1,27]{1,0:T(1,128)} %param.15) | copy-start | bytes 328
  7.6 14.7 %collective-permute-start = (bf16[256,768]{1,0:T(8,128)(2,1)S(1)}, bf16[256,768]{1,0:T(8,128)(2,1)S(1)}, u32[]{:S(2)}, u32[]{:S(2)}) collective-permute-start(bf16[256,768]{1,0:T(8,128)(2,1)S(1)} %pad_maximum_fusion.refs_0_.refs_3_), channel_id=1, source_target_pairs={{64,0},{3,1},{66,2},{5,3},{68,4},{7,5},{70,6},{9,7},{72,8},{11,9},... | collective-permute-start | bytes 1179656 | tf_op jit(solution)/shard_map/ppermute | solution.py:277
  9.5 12.7 %collective-permute-start.1 = (bf16[256,768]{1,0:T(8,128)(2,1)S(1)}, bf16[256,768]{1,0:T(8,128)(2,1)S(1)}, u32[]{:S(2)}, u32[]{:S(2)}) collective-permute-start(bf16[256,768]{1,0:T(8,128)(2,1)S(1)} %pad_maximum_fusion.refs_0_.refs_3_), channel_id=1, source_target_pairs={{1,3},{3,5},{5,7},{7,9},{9,11},{11,13},{13,15},{17,19},{19,21},{21... | collective-permute-start | bytes 1179656 | tf_op jit(solution)/shard_map/ppermute | solution.py:278
  14.9 14.4 %all-to-all-start = ((bf16[8,12,768]{2,1,0:T(8,128)(2,1)}), bf16[8,12,768]{2,1,0:T(8,128)(2,1)S(1)}, u32[]{:S(2)}, u32[]{:S(2)}) async-start(bf16[8,12,768]{2,1,0:T(8,128)(2,1)} %broadcast_in_dim.39), calls=%async_computation | async-start | bytes 393216 | tf_op jit(solution)/shard_map/all_to_all | solution.py:279
  21.9 67.7 %all-gather.2.cloned.1.call-start = ((), (), s32[]{:S(2)}) async-start(), calls=%async_computation.2 | async-start | bytes 1769472 | tf_op jit(solution)/shard_map/all_gather | solution.py:287
  22.3 7.7 %copy-start.2 = (bf16[128,768]{1,0:T(8,128)(2,1)S(1)}, bf16[128,768]{1,0:T(8,128)(2,1)}, u32[]{:S(2)}) copy-start(bf16[128,768]{1,0:T(8,128)(2,1)} %param.12) | copy-start | bytes 589828
  22.4 23.8 %collective-permute-start.2 = (bf16[768,768]{1,0:T(8,128)(2,1)S(1)}, bf16[768,768]{1,0:T(8,128)(2,1)}, u32[]{:S(2)}, u32[]{:S(2)}) collective-permute-start(bf16[768,768]{1,0:T(8,128)(2,1)S(1)} %shard_map.64), channel_id=1, source_target_pairs={{2,0},{65,1},{4,2},{67,3},{6,4},{69,5},{8,6},{71,7},{10,8},{73,9},... | collective-permute-start | bytes 3538952 | tf_op jit(solution)/shard_map/ppermute | solution.py:288
  23.7 22.5 %collective-permute-start.3 = (bf16[768,768]{1,0:T(8,128)(2,1)S(1)}, bf16[768,768]{1,0:T(8,128)(2,1)}, u32[]{:S(2)}, u32[]{:S(2)}) collective-permute-start(bf16[768,768]{1,0:T(8,128)(2,1)S(1)} %shard_map.64), channel_id=1, source_target_pairs={{0,2},{2,4},{4,6},{6,8},{8,10},{10,12},{12,14},{16,18},{18,20},{20... | collective-permute-start | bytes 3538952 | tf_op jit(solution)/shard_map/ppermute | solution.py:289
  30.2 9.7 %collective-permute-start.4 = (bf16[144,768]{1,0:T(8,128)(2,1)S(1)}, bf16[144,768]{1,0:T(8,128)(2,1)S(1)}, u32[]{:S(2)}, u32[]{:S(2)}) collective-permute-start(bf16[144,768]{1,0:T(8,128)(2,1)S(1)} %get-tuple-element.58), channel_id=1, source_target_pairs={{16,0},{17,1},{18,2},{19,3},{20,4},{21,5},{22,6},{23,7},{24,8},{25... | collective-permute-start | bytes 663560 | tf_op jit(solution)/shard_map/ppermute | solution.py:282
  34.4 9.6 %collective-permute-start.5 = (bf16[144,768]{1,0:T(8,128)(2,1)S(1)}, bf16[144,768]{1,0:T(8,128)(2,1)S(1)}, u32[]{:S(2)}, u32[]{:S(2)}) collective-permute-start(bf16[144,768]{1,0:T(8,128)(2,1)S(1)} %get-tuple-element.57), channel_id=1, source_target_pairs={{0,16},{1,17},{2,18},{3,19},{4,20},{5,21},{6,22},{7,23},{8,24},{9,... | collective-permute-start | bytes 663560 | tf_op jit(solution)/shard_map/ppermute | solution.py:283
  51.0 10.0 %collective-permute-start.6 = (bf16[128,896]{1,0:T(8,128)(2,1)S(1)}, bf16[128,896]{1,0:T(8,128)(2,1)S(1)}, u32[]{:S(2)}, u32[]{:S(2)}) collective-permute-start(bf16[128,896]{1,0:T(8,128)(2,1)S(1)} %get-tuple-element.53), channel_id=1, source_target_pairs={{16,0},{17,1},{18,2},{19,3},{20,4},{21,5},{22,6},{23,7},{24,8},{25... | collective-permute-start | bytes 688136 | tf_op jit(solution)/shard_map/ppermute | solution.py:294
  55.3 8.9 %collective-permute-start.7 = (bf16[128,896]{1,0:T(8,128)(2,1)S(1)}, bf16[128,896]{1,0:T(8,128)(2,1)S(1)}, u32[]{:S(2)}, u32[]{:S(2)}) collective-permute-start(bf16[128,896]{1,0:T(8,128)(2,1)S(1)} %get-tuple-element.54), channel_id=1, source_target_pairs={{0,16},{1,17},{2,18},{3,19},{4,20},{5,21},{6,22},{7,23},{8,24},{9,... | collective-permute-start | bytes 688136 | tf_op jit(solution)/shard_map/ppermute | solution.py:295
  90.8 2.6 %copy-start.1 = (bf16[1024,768]{1,0:T(8,128)(2,1)S(1)}, bf16[1024,768]{1,0:T(8,128)(2,1)}, u32[]{:S(2)}) copy-start(bf16[1024,768]{1,0:T(8,128)(2,1)} %all-gather.2.cloned.1.call-done) | copy-start | bytes 4718596
  91.4 3.9 %collective-permute-start.8 = (bf16[512,512]{1,0:T(8,128)(2,1)S(1)}, bf16[512,512]{1,0:T(8,128)(2,1)}, u32[]{:S(2)}, u32[]{:S(2)}) collective-permute-start(bf16[512,512]{1,0:T(8,128)(2,1)S(1)} %shard_map.69), channel_id=1, source_target_pairs={{0,1},{1,0},{2,3},{3,2},{4,5},{5,4},{6,7},{7,6},{8,9},{9,8},{10,11... | collective-permute-start | bytes 1572872 | tf_op jit(solution)/shard_map/ppermute | solution.py:300
  94.0 16.7 %copy-start = (bf16[512,384]{1,0:T(8,128)(2,1)S(1)}, bf16[512,384]{1,0:T(8,128)(2,1)}, u32[]{:S(2)}) copy-start(bf16[512,384]{1,0:T(8,128)(2,1)} %constant.176.clone.order) | copy-start | bytes 1179652
Sparse Core Ops, SparseCore 0:
  30.1 42.5 all-gather.1
